TPU v7x, 32 devices: a whole 2x2x4 slice. The times are simulated.
32 devices in a mesh: lat: 8 (over z, x), lev: 4 (over y, core).
Axes of the slice: x: 2, y: 2, z: 4, core: 2. Of those that a mesh axis runs over, the one named last changes fastest.
Arguments:
- tokens: bfloat16 [2, 4, 16, 64, 1024], P(None, 'lev', 'lat'), may hold values from -40 to 40
- key_mask: int32 [2, 16], replicated, may hold values from 0 to 1, as said below
- w_qkv: bfloat16 [1024, 3072], replicated, may hold values from -0.1875 to 0.1875
- w_mix: bfloat16 [4, 1024, 1024], P('lev'), may hold values from -0.09375 to 0.09375
- level_scale: float32 [4, 1024], P('lev'), may hold values from 0.1 to 1.9
- cotangent: bfloat16 [2, 4, 16, 64, 1024], P(None, 'lev', 'lat'), may hold values from -6 to 6
Outputs:
- output: bfloat16 [2, 4, 16, 64, 1024], P(None, 'lev', 'lat')
- d_tokens: bfloat16 [2, 4, 16, 64, 1024], P(None, 'lev', 'lat')
- mix_grad: float32 [4, 1024, 1024], P('lev', 'lat')
Inputs may be any that keep to these rules, and one draw needn't show every extreme that they name: `key_mask`: each sample has 1 to 4 padded rows, all at the end of the latitude rows, and the rest real; some sample has exactly 4 padded rows.
All inputs are finite; a program needn't handle non-finite values.
Results may differ from a plain program's by a relative error of at most 0.015.
Values may be sent and summed in bfloat16 or wider, within the bound.
No kernel may reach another device: no remote copies, remote signals or barrier semaphores. Data moves between devices by JAX's collectives and lax.ppermute only.
A program may use at most 128 MiB of HBM per device.

v0:
```python
import functools
import math

import jax
import jax.numpy as jnp
from jax import lax
from jax.experimental import pallas as pl
from jax.experimental.pallas import tpu as pltpu
from jax.sharding import PartitionSpec as P

HEADS = 16
GROUP = 256

epsilon = 1e-06
score_scale = 0.25

F32 = jnp.float32
BF16 = jnp.bfloat16


def nn(a, b):
    return lax.dot_general(a, b, (((1,), (0,)), ((), ())), preferred_element_type=F32)


def nt(a, b):
    return lax.dot_general(a, b, (((1,), (1,)), ((), ())), preferred_element_type=F32)


def tn(a, b):
    return lax.dot_general(a, b, (((0,), (0,)), ((), ())), preferred_element_type=F32)


def block_mean(head_width):
    row = lax.broadcasted_iota(jnp.int32, (GROUP, GROUP), 0) // head_width
    col = lax.broadcasted_iota(jnp.int32, (GROUP, GROUP), 1) // head_width
    return jnp.where(row == col, 1.0 / head_width, 0.0).astype(BF16)


def params():
    return pltpu.CompilerParams(vmem_limit_bytes=36 * 1024 * 1024)


def half_cols(which, width):
    half = width // 2
    core = lax.axis_index("lev") % 2
    return pl.ds(pl.multiple_of((core ^ which) * half, half), half)


def in_hbm(array):
    return pltpu.with_memory_space_constraint(array, pltpu.HBM)


def call(kernel, name, out_shape, *operands):
    return pl.pallas_call(
        kernel, out_shape=out_shape, compiler_params=params(), name=name
    )(*operands)


def pack_kernel(tok_ref, cot_ref, gain_ref, tok_out, *cot_outs):
    batch, rows, parts, chunk, width = tok_ref.shape
    for b in range(batch):
        for q in range(parts):
            for r in range(rows):
                tok_out[b * parts + q, r * chunk : (r + 1) * chunk, :] = tok_ref[b, r, q]
    for s in range(2):
        cols = half_cols(s, width)
        gain = gain_ref[:, cols]
        for b in range(batch):
            for q in range(parts):
                for r in range(rows):
                    piece = cot_ref[b, r, q, :, cols].astype(F32)
                    cot_outs[s][b * parts + q, r * chunk : (r + 1) * chunk, :] = (
                        piece * gain
                    ).astype(BF16)


def pack(tokens, cot, gain):
    batch, rows, parts, chunk, width = tokens.shape
    shape = (batch * parts, rows * chunk)
    return call(
        pack_kernel,
        "pack",
        [jax.ShapeDtypeStruct(shape + (width,), BF16)]
        + [jax.ShapeDtypeStruct(shape + (width // 2,), BF16)] * 2,
        in_hbm(tokens),
        in_hbm(cot),
        in_hbm(gain),
    )


def output_kernel(tok_ref, gain_ref, own_ref, other_ref, out_ref):
    batch, rows, parts, chunk, width = tok_ref.shape
    for s, ref in enumerate((own_ref, other_ref)):
        cols = half_cols(s, width)
        gain = gain_ref[:, cols]
        for t in range(batch * parts):
            b, q = t // parts, t % parts
            for r in range(rows):
                mixed = ref[t, r * chunk : (r + 1) * chunk, :].astype(F32)
                out_ref[b, r, q, :, cols] = (
                    tok_ref[b, r, q, :, cols].astype(F32) + gain * mixed
                ).astype(BF16)


def make_output(tokens, gain, mixed):
    return call(
        output_kernel,
        "make_output",
        jax.ShapeDtypeStruct(tokens.shape, BF16),
        tokens,
        gain,
        *mixed,
    )


def gradient_kernel(cot_ref, back_ref, out_ref):
    batch, rows, parts, chunk, width = cot_ref.shape
    for b in range(batch):
        for q in range(parts):
            for r in range(rows):
                back = back_ref[b * parts + q, r * chunk : (r + 1) * chunk, :width].astype(F32)
                out_ref[b, r, q] = (cot_ref[b, r, q].astype(F32) + back).astype(BF16)


def make_gradient(cot, back):
    return call(
        gradient_kernel, "make_gradient", jax.ShapeDtypeStruct(cot.shape, BF16), cot, back
    )


def by_head(tile, lane):
    zero = jnp.zeros_like(tile)
    return jnp.concatenate([jnp.where(lane == 0, tile, zero), jnp.where(lane == 1, tile, zero)], axis=0)


def one_head(stacked, lane):
    count = lane.shape[0]
    return jnp.where(lane == 0, stacked[:count], stacked[count:])


def side_by_side(stacked):
    count = stacked.shape[0] // 2
    return jnp.concatenate([stacked[:count], stacked[count:]], axis=1)


def forward_kernel(
    samples, lat_count, chunk, owners,
    tok_ref, mask_ref, wq_ref, wk_ref, wv_ref, wm_ref, _,
    qn_ref, kn_ref, v_ref, rq_ref, rk_ref, ri_ref, p_ref, att_ref, own_ref, other_ref,
    normed_ref, acc_ref, keep_ref,
):
    step = pl.program_id(0)
    count, width = normed_ref.shape
    head_width = width // HEADS

    @pl.when(step == 0)
    def _():
        x = tok_ref[...].astype(F32)
        rx = lax.rsqrt(jnp.mean(x * x, axis=-1, keepdims=True) + epsilon)
        normed_ref[...] = (x * rx).astype(BF16)
        acc_ref[...] = jnp.zeros_like(acc_ref)
        spread = (
            lax.broadcasted_iota(jnp.int32, (lat_count, count), 0)
            == lax.broadcasted_iota(jnp.int32, (lat_count, count), 1) // chunk
        ).astype(F32)
        per_sample = nn(mask_ref[...].astype(F32), spread)
        mine = lax.axis_index("lat") // (owners // samples)
        pick = lax.broadcasted_iota(jnp.int32, (samples, count), 0) == mine
        valid = jnp.sum(jnp.where(pick, per_sample, 0.0), axis=0, keepdims=True)
        same = (
            lax.broadcasted_iota(jnp.int32, (count, count), 0) % chunk
            == lax.broadcasted_iota(jnp.int32, (count, count), 1) % chunk
        )
        keep_ref[...] = jnp.where(same, valid, 0.0)

    normed = normed_ref[...]
    mean_mat = block_mean(head_width)
    q = nn(normed, wq_ref[...])
    k = nn(normed, wk_ref[...])
    v = nn(normed, wv_ref[...]).astype(BF16)
    rq = lax.rsqrt(nn((q * q).astype(BF16), mean_mat) + epsilon)
    rk = lax.rsqrt(nn((k * k).astype(BF16), mean_mat) + epsilon)
    qn = (q * rq).astype(BF16)
    kn = (k * rk).astype(BF16)
    qn_ref[...] = qn
    kn_ref[...] = kn
    v_ref[...] = v
    rq_ref[...] = rq.astype(BF16)
    rk_ref[...] = rk.astype(BF16)
    keep = keep_ref[...]
    keep = jnp.concatenate([keep, keep], axis=0)
    lane = lax.broadcasted_iota(jnp.int32, (count, 128), 1) // head_width
    ones = jnp.ones((count, 128), BF16)
    tiles = []
    for t in range(GROUP // 128):
        cols = slice(t * 128, (t + 1) * 128)
        v_ones = jnp.concatenate([v[:, cols], ones], axis=1)
        e = jnp.exp(nt(by_head(qn[:, cols] * score_scale, lane), kn[:, cols])) * keep
        e = e.astype(BF16)
        p_ref[t] = e
        o = nn(e, v_ones)
        inverse = 1.0 / o[:, 128:]
        tiles.append(one_head(o[:, :128] * inverse, lane))
        ri_ref[:, cols] = one_head(inverse, lane)
    att = jnp.concatenate(tiles, axis=1).astype(BF16)
    features = att_ref.shape[-1]
    for f in range(GROUP // features):
        att_ref[f] = att[:, f * features : (f + 1) * features]
    acc_ref[...] += nn(att, wm_ref[...])

    @pl.when(step == pl.num_programs(0) - 1)
    def _():
        for s, ref in enumerate((own_ref, other_ref)):
            ref[...] = acc_ref[:, half_cols(s, width)].astype(BF16)


def forward(tok_col, key_mask, w_qkv, w_mix, chunk, owners, after):
    count, width = tok_col.shape
    samples, lat_count = key_mask.shape
    steps = width // GROUP
    features = width // owners
    same = lambda shape: pl.BlockSpec(shape, lambda i: (0, 0))
    cols = pl.BlockSpec((count, GROUP), lambda i: (0, i))
    weight = lambda which: pl.BlockSpec((width, GROUP), lambda i: (0, i + which * steps))
    return pl.pallas_call(
        functools.partial(forward_kernel, samples, lat_count, chunk, owners),
        out_shape=(
            [pltpu.HBM((count, width), BF16)] * 5
            + [pltpu.HBM((count, width), F32)]
            + [pltpu.HBM((width // 128, 2 * count, count), BF16)]
            + [jax.ShapeDtypeStruct((owners, count, features), BF16)]
            + [jax.ShapeDtypeStruct((count, width // 2), BF16)] * 2
        ),
        grid=(steps,),
        in_specs=[
            same((count, width)),
            same((samples, lat_count)),
            weight(0),
            weight(1),
            weight(2),
            pl.BlockSpec((GROUP, width), lambda i: (i, 0)),
            pl.BlockSpec(memory_space=pl.ANY),
        ],
        out_specs=(
            [cols] * 6
            + [pl.BlockSpec((GROUP // 128, 2 * count, count), lambda i: (i, 0, 0))]
            + [pl.BlockSpec((GROUP // features, count, features), lambda i: (i, 0, 0))]
            + [same((count, width // 2))] * 2
        ),
        scratch_shapes=[
            pltpu.VMEM((count, width), BF16),
            pltpu.VMEM((count, width), F32),
            pltpu.VMEM((count, count), F32),
        ],
        compiler_params=params(),
        cost_estimate=pl.CostEstimate(
            flops=2 * count * width * (4 * width + 2 * count * 4),
            bytes_accessed=20 * count * width + 8 * width * width,
            transcendentals=HEADS * count * count,
        ),
        name="forward",
    )(tok_col, key_mask, *[in_hbm(w_qkv)] * 3, in_hbm(w_mix), after)


def backward_kernel(
    tok_ref, own_ref, other_ref, wm_ref, wq_ref, wk_ref, wv_ref,
    qn_ref, kn_ref, v_ref, rq_ref, rk_ref, ri_ref, p_ref, *rest,
):
    out_ref, acc_ref = rest[-2:]
    step = pl.program_id(0)
    count, width = acc_ref.shape
    head_width = width // HEADS
    d_att = nt(own_ref[...], wm_ref[:, half_cols(0, width)])
    d_att += nt(other_ref[...], wm_ref[:, half_cols(1, width)])
    inverse = ri_ref[...]
    d_att = (d_att * inverse).astype(BF16)
    qn, kn, v = qn_ref[...], kn_ref[...], v_ref[...]
    lane = lax.broadcasted_iota(jnp.int32, (count, 128), 1) // head_width
    dq_tiles, dk_tiles, dv_tiles = [], [], []
    for t in range(GROUP // 128):
        cols = slice(t * 128, (t + 1) * 128)
        d_t = d_att[:, cols]
        d_p = nt(by_head(d_t, lane), v[:, cols])
        e = p_ref[t]
        e_wide = e.astype(F32)
        first = t * 128
        second = first + head_width
        row_inverse = jnp.concatenate(
            [inverse[:, first : first + 1], inverse[:, second : second + 1]], axis=0
        )
        weighted = e_wide * d_p
        inner = jnp.sum(weighted, axis=-1, keepdims=True) * row_inverse
        d_s = (weighted - e_wide * inner).astype(BF16)
        dq_tiles.append(one_head(nn(d_s, kn[:, cols]), lane) * score_scale)
        dk_tiles.append(one_head(tn(side_by_side(d_s), qn[:, cols]), lane) * score_scale)
        dv_tiles.append(one_head(tn(side_by_side(e), d_t), lane))
    mean_mat = block_mean(head_width)
    dq = jnp.concatenate(dq_tiles, axis=1)
    dk = jnp.concatenate(dk_tiles, axis=1)
    dv = jnp.concatenate(dv_tiles, axis=1).astype(BF16)

    def through_norm(upstream, unit, factor):
        unit = unit.astype(F32)
        inner = nn((upstream * unit).astype(BF16), mean_mat)
        return (factor.astype(F32) * (upstream - unit * inner)).astype(BF16)

    gq = through_norm(dq, qn, rq_ref[...])
    gk = through_norm(dk, kn, rk_ref[...])
    total = nt(gq, wq_ref[...]) + nt(gk, wk_ref[...]) + nt(dv, wv_ref[...])

    @pl.when(step == 0)
    def _():
        acc_ref[...] = total

    @pl.when(step > 0)
    def _():
        acc_ref[...] += total

    @pl.when(step == pl.num_programs(0) - 1)
    def _():
        x = tok_ref[...].astype(F32)
        rx = lax.rsqrt(jnp.mean(x * x, axis=-1, keepdims=True) + epsilon)
        d = acc_ref[...]
        inner = jnp.mean(d * x, axis=-1, keepdims=True)
        out_ref[...] = (rx * d - x * (rx * rx * rx * inner)).astype(BF16)


def backward(tok_col, flow, w_mix, w_qkv, saved, *after):
    count, width = tok_col.shape
    steps = width // GROUP
    same = lambda shape: pl.BlockSpec(shape, lambda i: (0, 0))
    cols = pl.BlockSpec((count, GROUP), lambda i: (0, i))
    weight = lambda which: pl.BlockSpec((width, GROUP), lambda i: (0, i + which * steps))
    return pl.pallas_call(
        backward_kernel,
        out_shape=jax.ShapeDtypeStruct((count, width), BF16),
        grid=(steps,),
        in_specs=[
            same((count, width)),
            same((count, width // 2)),
            same((count, width // 2)),
            pl.BlockSpec((GROUP, width), lambda i: (i, 0)),
            weight(0),
            weight(1),
            weight(2),
            *([cols] * 6),
            pl.BlockSpec((GROUP // 128, 2 * count, count), lambda i: (i, 0, 0)),
        ]
        + [pl.BlockSpec(memory_space=pl.ANY)] * len(after),
        out_specs=same((count, width)),
        scratch_shapes=[pltpu.VMEM((count, width), F32)],
        compiler_params=params(),
        cost_estimate=pl.CostEstimate(
            flops=2 * count * width * (4 * width + 4 * count * 4),
            bytes_accessed=20 * count * width + 8 * width * width,
            transcendentals=0,
        ),
        name="backward",
    )(tok_col, *flow, in_hbm(w_mix), *[in_hbm(w_qkv)] * 3, *map(in_hbm, saved), *after)


def mix_gradient_kernel(factor, own_flow_ref, other_flow_ref, *refs):
    att_refs, out_refs = refs[: len(refs) // 2], refs[len(refs) // 2 :]
    width = out_refs[0].shape[-1]
    for att_ref, out_ref in zip(att_refs, out_refs):
        att = att_ref[...]
        for s, flow_ref in enumerate((own_flow_ref, other_flow_ref)):
            term = tn(att, flow_ref[...]) * factor
            out_ref[:, half_cols(s, width)] = term.astype(out_ref.dtype)


def mix_gradient(attended, flow, factor):
    rows, features = attended[0].shape
    width = 2 * flow[0].shape[-1]
    out = [jax.ShapeDtypeStruct((features, width), F32)]
    out += [jax.ShapeDtypeStruct((features, width), BF16)] * (len(attended) - 1)
    return pl.pallas_call(
        functools.partial(mix_gradient_kernel, factor),
        out_shape=out,
        compiler_params=params(),
        cost_estimate=pl.CostEstimate(
            flops=2 * rows * features * width * len(attended),
            bytes_accessed=2 * rows * (features * len(attended) + width),
            transcendentals=0,
        ),
        name="mix_gradient",
    )(*flow, *attended)


def chip_rows(array, axis, chip):
    rows = array.shape[axis] // (lax.axis_size("lev") // 2)
    return lax.dynamic_slice_in_dim(array, (chip * rows).astype(jnp.uint32), rows, axis)


def swap(block):
    return lax.all_to_all(block, "lat", split_axis=0, concat_axis=0, tiled=True)


def from_level(block, offset):
    return lax.ppermute(block, "lev", [(i, i ^ offset) for i in range(lax.axis_size("lev"))])


def add_kernel(own_ref, received_ref, out_ref):
    out_ref[...] = (own_ref[...].astype(F32) + received_ref[...].astype(F32)).astype(BF16)


def add(own, received):
    return call(add_kernel, "add", jax.ShapeDtypeStruct(own.shape, BF16), own, received)


def pair_total(own, other):
    return add(own, from_level(other, 1))


def before_last(total):
    offset = 2
    while 2 * offset < lax.axis_size("lev"):
        total = add(total, from_level(total, offset))
        offset *= 2
    return total, from_level(total, offset)


def row_half(which, rows):
    top = lax.axis_index("lev") // (lax.axis_size("lev") // 2)
    return pl.ds(pl.multiple_of((top ^ which) * rows, rows), rows)


def split_kernel(own_ref, received_ref, first_ref, second_ref):
    rows = first_ref.shape[1]
    for which, ref in enumerate((first_ref, second_ref)):
        at = row_half(which, rows)
        total = own_ref[:, at, :].astype(F32) + received_ref[:, at, :].astype(F32)
        ref[...] = total.astype(BF16)


def split_rows(own, received):
    owners, cells, half = own.shape
    rows = cells // 2
    if rows % 16 == 0:
        part = jax.ShapeDtypeStruct((owners, rows, half), BF16)
        return call(split_kernel, "split_rows", [part, part], own, received)
    total = (own.astype(F32) + received.astype(F32)).astype(BF16)
    top = lax.axis_index("lev") // (lax.axis_size("lev") // 2)
    return [lax.dynamic_slice_in_dim(total, (top ^ k) * rows, rows, 1) for k in range(2)]


def add_flow_kernel(first_ref, second_ref, received_ref, _, __, out_ref):
    rows = first_ref.shape[1]
    out_ref[:, row_half(0, rows), :] = first_ref[...]
    second = second_ref[...].astype(F32) + received_ref[...].astype(F32)
    out_ref[:, row_half(1, rows), :] = second.astype(BF16)


def add_flow(first, second, received, *after):
    owners, rows, half = first.shape
    if rows % 16:
        second = (second.astype(F32) + received.astype(F32)).astype(BF16)
        top = lax.axis_index("lev") // (lax.axis_size("lev") // 2)
        pair = jnp.where(top == 0, jnp.stack([first, second]), jnp.stack([second, first]))
        return jnp.concatenate([pair[0], pair[1]], axis=1)
    whole = pl.BlockSpec(memory_space=pltpu.VMEM)
    return pl.pallas_call(
        add_flow_kernel,
        out_shape=jax.ShapeDtypeStruct((owners, 2 * rows, half), BF16),
        in_specs=[whole] * 3 + [pl.BlockSpec(memory_space=pl.ANY)] * 2,
        out_specs=whole,
        compiler_params=params(),
        name="add_flow",
    )(first, second, received, *after)


def join_kernel(first_ref, second_ref, out_ref):
    count = first_ref.shape[0]
    out_ref[:count] = first_ref[...]
    out_ref[count:] = second_ref[...]


def join(first, second):
    shape = jax.ShapeDtypeStruct((2 * first.shape[0],) + first.shape[1:], BF16)
    return call(join_kernel, "join", shape, first, second)


def from_owner(block, offset):
    return lax.ppermute(block, "lat", [(i, i ^ offset) for i in range(lax.axis_size("lat"))])


def gather_offsets(owners):
    offsets = [owners // 4, owners // 2]
    while len(offsets) < owners.bit_length() - 1:
        offsets.append(owners >> (len(offsets) + 1))
    return offsets


def arrange_kernel(first_ref, second_ref, _, out_ref):
    owners = out_ref.shape[1]
    half = owners // 2
    offsets = gather_offsets(owners)
    for u in range(owners):
        band = lax.axis_index("lat") ^ sum(o for k, o in enumerate(offsets) if u >> k & 1)
        ref = first_ref if u < half else second_ref
        out_ref[:, band] = ref[u % half]


def arrange(first, second, after):
    _, owners, rows, half = first.shape
    whole = pl.BlockSpec(memory_space=pltpu.VMEM)
    return pl.pallas_call(
        arrange_kernel,
        out_shape=jax.ShapeDtypeStruct((owners, owners, rows, half), BF16),
        in_specs=[whole, whole, pl.BlockSpec(memory_space=pl.ANY)],
        out_specs=whole,
        compiler_params=params(),
        name="arrange",
    )(first, second, after)


def add_mixed_kernel(own_ref, received_ref, back_ref, out_ref):
    width = back_ref.shape[-1]
    out_ref[:, :width] = back_ref[...]
    out_ref[:, width:] = (own_ref[...].astype(F32) + received_ref[...].astype(F32)).astype(BF16)


def add_mixed(own, received, back):
    count, width = back.shape
    shape = jax.ShapeDtypeStruct((count, width + own.shape[-1]), BF16)
    return call(add_mixed_kernel, "add_mixed", shape, own, received, back)


def cut_kernel(in_ref, _, out_ref):
    out_ref[...] = in_ref[:, :, in_ref.shape[-1] - out_ref.shape[-1] :]


def cut_mixed(received, after):
    owners, cells, wide = received.shape
    whole = pl.BlockSpec(memory_space=pltpu.VMEM)
    return pl.pallas_call(
        cut_kernel,
        out_shape=jax.ShapeDtypeStruct((owners, cells, wide // 3), BF16),
        in_specs=[whole, pl.BlockSpec(memory_space=pl.ANY)],
        out_specs=whole,
        compiler_params=params(),
        name="cut_mixed",
    )(received, after)


def on_device(tokens, key_mask, w_qkv, w_mix, level_scale, cotangent):
    batch, _, rows, lon, width = tokens.shape
    owners = lax.axis_size("lat")
    parts = owners // batch
    chunk = lon // parts
    cells = rows * chunk
    count = batch * rows * lon
    half = width // 2
    tok_band = tokens.reshape(batch, rows, parts, chunk, width)
    cot_band = cotangent.reshape(batch, rows, parts, chunk, width)
    w_mix = w_mix.reshape(width, width)

    tok_send, cot_own, cot_other = pack(tok_band, cot_band, level_scale)
    tok_col = swap(tok_send).reshape(count, width)
    last = lax.axis_size("lev") // 2
    received = from_level(cot_other, 1)
    offset = 2
    while offset < last:
        cot_own = add(cot_own, received)
        received = from_level(cot_own, offset)
        offset *= 2
    first, second = split_rows(cot_own, received)
    first, received = add(first, from_level(second, last)), from_level(first, last)
    rows = cells // last
    offsets = gather_offsets(owners)
    flow_rows = first
    if last > 2:
        part = lax.axis_index("lev") // 2 % (last // 2)
        flow_rows = lax.dynamic_slice_in_dim(first, part * rows, rows, 1)
    flow_rows = flow_rows[None]
    flow_rows = join(flow_rows, from_owner(flow_rows, offsets[0]))
    flow_band = add_flow(first, second, received, tok_col, flow_rows)
    flow_own = swap(flow_band).reshape(count, half)
    flow = (flow_own, from_level(flow_own, 1))
    chip = lax.shift_right_logical(lax.axis_index("lev"), 1)
    chips = lax.axis_size("lev") // 2

    *saved, attended, mix_own, mix_other = forward(
        tok_col, key_mask, w_qkv, w_mix, chunk, owners, flow_band
    )
    attended = swap(attended)
    mix_terms = before_last(pair_total(mix_own, mix_other))
    for offset in offsets[1:-1]:
        flow_rows = join(flow_rows, from_owner(flow_rows, offset))
    received = from_owner(flow_rows, offsets[-1])
    back_col = backward(tok_col, flow, w_mix, w_qkv, saved, mix_terms[0], flow_rows)
    sent = add_mixed(*mix_terms, back_col)
    back = swap(sent.reshape(owners, cells, width + half))
    d_tokens = make_gradient(cot_band, back)

    factor = 1.0 / math.sqrt(count * owners)
    features = width // owners
    attended = attended.reshape(owners, owners, cells, features)
    attended = [chip_rows(attended, 2, chip ^ k).reshape(-1, features) for k in range(chips)]
    attended[1:] = [from_level(attended[k], 2 * k) for k in range(1, chips)]
    flow_rows = arrange(flow_rows, received, sent).reshape(-1, half)
    grads = mix_gradient(attended, (flow_rows, from_level(flow_rows, 1)), factor)
    mix_grad = grads[0]
    for k in range(1, chips):
        mix_grad += from_level(grads[k], 2 * k).astype(F32)

    mix_band = cut_mixed(back, mix_grad)
    output = make_output(tok_band, level_scale, (mix_band, from_level(mix_band, 1)))
    return (
        output.reshape(tokens.shape),
        d_tokens.reshape(tokens.shape),
        mix_grad.reshape(1, width // owners, width),
    )


def solution(mesh):
    return jax.shard_map(
        on_device,
        mesh=mesh,
        in_specs=(
            P(None, "lev", "lat", None, None),
            P(),
            P(),
            P("lev", None, None),
            P("lev", None),
            P(None, "lev", "lat", None, None),
        ),
        out_specs=(
            P(None, "lev", "lat", None, None),
            P(None, "lev", "lat", None, None),
            P("lev", "lat", None),
        ),
        check_vma=False,
    )
```

profile of v0, /device:TPU:0, one launch (start us, length us, event | category | flops | bytes accessed | tf_op | source)
XLA Modules:
  0.0 98.2 jit_solution(17983876468868503248)
XLA Ops:
  0.6 2.1 %pack.1 = (bf16[8,32,1024]{2,1,0:T(8,128)(2,1)}, bf16[8,32,512]{2,1,0:T(8,128)(2,1)S(1)}, bf16[8,32,512]{2,1,0:T(8,128)(2,1)S(1)}) custom-call(bf16[2,2,4,16,1024]{4,3,2,1,0:T(8,128)(2,1)} %bitcast.25, bf16[2,2,4,16,1024]{4,3,2,1,0:T(8,128)(2,1)} %bitcast.23, f32[1,1024]{1,0:T(1,128)} %gain_ref.3), custom_call_target="tpu_custom_call" | custom-call | tf_op jit(solution)/shard_map/pack/pallas_call | solution.py:54
  2.7 7.4 %all-to-all-start = ((bf16[8,32,1024]{2,1,0:T(8,128)(2,1)}), bf16[8,32,1024]{2,1,0:T(8,128)(2,1)S(1)}, u32[]{:S(2)}, u32[]{:S(2)}) async-start(bf16[8,32,1024]{2,1,0:T(8,128)(2,1)} %get-tuple-element.20), calls=%async_computation | async-start | bytes 1048576 | tf_op jit(solution)/shard_map/all_to_all | solution.py:396
  10.1 0.0 collective-permute-start
  10.1 1.5 %collective-permute-done.received_ref = bf16[8,32,512]{2,1,0:T(8,128)(2,1)S(1)} collective-permute-done((bf16[8,32,512]{2,1,0:T(8,128)(2,1)S(1)}, bf16[8,32,512]{2,1,0:T(8,128)(2,1)S(1)}, u32[]{:S(2)}, u32[]{:S(2)}) %collective-permute-start) | collective-permute-done | bytes 262176 | tf_op jit(solution)/shard_map/ppermute | solution.py:400
  11.6 0.1 split_rows.1
  11.7 1.6 %collective-permute-start.1 = (bf16[8,16,512]{2,1,0:T(8,128)(2,1)S(1)}, bf16[8,16,512]{2,1,0:T(8,128)(2,1)S(1)}, u32[]{:S(2)}, u32[]{:S(2)}) collective-permute-start(bf16[8,16,512]{2,1,0:T(8,128)(2,1)S(1)} %get-tuple-element.24.second_ref), channel_id=1, source_target_pairs={{0,2},{1,3},{2,0},{3,1},{4,6},{5,7},{6,4},{7,5},{8,10},{9,11},{10,... | collective-permute-start | bytes 393224 | tf_op jit(solution)/shard_map/ppermute | solution.py:400
  13.3 4.0 %collective-permute-done.1.received_ref = bf16[8,16,512]{2,1,0:T(8,128)(2,1)S(1)} collective-permute-done((bf16[8,16,512]{2,1,0:T(8,128)(2,1)S(1)}, bf16[8,16,512]{2,1,0:T(8,128)(2,1)S(1)}, u32[]{:S(2)}, u32[]{:S(2)}) %collective-permute-start.1) | collective-permute-done | bytes 131104 | tf_op jit(solution)/shard_map/ppermute | solution.py:400
  17.3 2.1 %collective-permute-start.3 = (bf16[1,8,16,512]{3,2,1,0:T(8,128)(2,1)S(1)}, bf16[1,8,16,512]{3,2,1,0:T(8,128)(2,1)S(1)}, u32[]{:S(2)}, u32[]{:S(2)}) collective-permute-start(bf16[1,8,16,512]{3,2,1,0:T(8,128)(2,1)S(1)} %bitcast.28), channel_id=1, source_target_pairs={{0,8},{4,12},{8,0},{12,4},{16,24},{20,28},{24,16},{28,20},{1,9},{5... | collective-permute-start | bytes 393224 | tf_op jit(solution)/shard_map/ppermute | solution.py:484
  19.4 1.5 %collective-permute-start.2 = (bf16[8,16,512]{2,1,0:T(8,128)(2,1)S(1)}, bf16[8,16,512]{2,1,0:T(8,128)(2,1)S(1)}, u32[]{:S(2)}, u32[]{:S(2)}) collective-permute-start(bf16[8,16,512]{2,1,0:T(8,128)(2,1)S(1)} %get-tuple-element.23.own_ref), channel_id=1, source_target_pairs={{0,2},{1,3},{2,0},{3,1},{4,6},{5,7},{6,4},{7,5},{8,10},{9,11},{10,... | collective-permute-start | bytes 393224 | tf_op jit(solution)/shard_map/ppermute | solution.py:400
  20.9 3.9 %collective-permute-done.3.second_ref = bf16[1,8,16,512]{3,2,1,0:T(8,128)(2,1)S(1)} collective-permute-done((bf16[1,8,16,512]{3,2,1,0:T(8,128)(2,1)S(1)}, bf16[1,8,16,512]{3,2,1,0:T(8,128)(2,1)S(1)}, u32[]{:S(2)}, u32[]{:S(2)}) %collective-permute-start.3) | collective-permute-done | bytes 131104 | tf_op jit(solution)/shard_map/ppermute | solution.py:484
  24.8 0.0 collective-permute-done.2.received_ref
  24.8 0.0 all-to-all-done
  24.8 0.8 add_flow.1._
  25.6 4.8 %all-to-all-start.1 = ((bf16[8,32,512]{2,1,0:T(8,128)(2,1)}), bf16[8,32,512]{2,1,0:T(8,128)(2,1)S(1)}, u32[]{:S(2)}, u32[]{:S(2)}) async-start(bf16[8,32,512]{2,1,0:T(8,128)(2,1)} %add_flow.1._), calls=%async_computation.1 | async-start | bytes 524288 | tf_op jit(solution)/shard_map/all_to_all | solution.py:396
  30.4 2.9 %collective-permute-start.7 = (bf16[2,8,16,512]{3,2,1,0:T(8,128)(2,1)S(1)}, bf16[2,8,16,512]{3,2,1,0:T(8,128)(2,1)S(1)}, u32[]{:S(2)}, u32[]{:S(2)}) collective-permute-start(bf16[2,8,16,512]{3,2,1,0:T(8,128)(2,1)S(1)} %join.2.__.first_ref), channel_id=1, source_target_pairs={{0,16},{4,20},{8,24},{12,28},{16,0},{20,4},{24,8},{28,12},{1,17},{... | collective-permute-start | bytes 786440 | tf_op jit(solution)/shard_map/ppermute | solution.py:484
  33.3 9.7 %forward.1 = (bf16[256,1024]{1,0:T(8,128)(2,1)}, bf16[256,1024]{1,0:T(8,128)(2,1)}, bf16[256,1024]{1,0:T(8,128)(2,1)}, bf16[256,1024]{1,0:T(8,128)(2,1)}, bf16[2...) custom-call(bf16[256,1024]{1,0:T(8,128)(2,1)S(1)} %bitcast.19, ...), custom_call_target="tpu_custom_call" | custom-call | flops 3221225472 | bytes 13631488 | tf_op jit(solution)/shard_map/forward/pallas_call | solution.py:225
  43.0 3.1 %all-to-all-done.1 = bf16[8,32,512]{2,1,0:T(8,128)(2,1)S(1)} async-done(((bf16[8,32,512]{2,1,0:T(8,128)(2,1)}), bf16[8,32,512]{2,1,0:T(8,128)(2,1)S(1)}, u32[]{:S(2)}, u32[]{:S(2)}) %all-to-all-start.1) | async-done | bytes 262176 | tf_op jit(solution)/shard_map/all_to_all | solution.py:396
  46.1 3.5 %all-to-all-start.3 = ((bf16[8,256,128]{2,1,0:T(8,128)(2,1)}), bf16[8,256,128]{2,1,0:T(8,128)(2,1)S(1)}, u32[]{:S(2)}, u32[]{:S(2)}) async-start(bf16[8,256,128]{2,1,0:T(8,128)(2,1)} %get-tuple-element.34), calls=%async_computation.3 | async-start | bytes 1048576 | tf_op jit(solution)/shard_map/all_to_all | solution.py:396
  49.6 0.1 collective-permute-start.4
  49.6 0.5 collective-permute-start.6
  50.1 0.1 collective-permute-done.7.second_ref
  50.3 1.8 %collective-permute-start.8 = (bf16[4,8,16,512]{3,2,1,0:T(8,128)(2,1)S(1)}, bf16[4,8,16,512]{3,2,1,0:T(8,128)(2,1)S(1)}, u32[]{:S(2)}, u32[]{:S(2)}) collective-permute-start(bf16[4,8,16,512]{3,2,1,0:T(8,128)(2,1)S(1)} %join.3.rest_1_.first_ref), channel_id=1, source_target_pairs={{0,4},{4,0},{8,12},{12,8},{16,20},{20,16},{24,28},{28,24},{1,5},{5... | collective-permute-start | bytes 1572872 | tf_op jit(solution)/shard_map/ppermute | solution.py:484
  52.1 0.0 collective-permute-done.4.received_ref
  52.1 0.1 add.8.rest_0_.own_ref
  52.2 1.6 %collective-permute-start.5 = (bf16[256,512]{1,0:T(8,128)(2,1)S(1)}, bf16[256,512]{1,0:T(8,128)(2,1)S(1)}, u32[]{:S(2)}, u32[]{:S(2)}) collective-permute-start(bf16[256,512]{1,0:T(8,128)(2,1)S(1)} %add.8.rest_0_.own_ref), channel_id=1, source_target_pairs={{0,2},{1,3},{2,0},{3,1},{4,6},{5,7},{6,4},{7,5},{8,10},{9,11},{10,... | collective-permute-start | bytes 786440 | tf_op jit(solution)/shard_map/ppermute | solution.py:400
  53.8 0.0 collective-permute-done.6.other_ref
  53.8 15.0 %backward.1.back_ref = bf16[256,1024]{1,0:T(8,128)(2,1)S(1)} custom-call(bf16[256,1024]{1,0:T(8,128)(2,1)S(1)} %bitcast.20, bf16[256,512]{1,0:T(8,128)(2,1)S(1)} %bitcast.31, bf16[256,512]{1,0:T(8,128)(2,1)S(1)} %collective-permute-done.6.other_ref, bf16[1024,1024]{1,0:T(8,128)(2,1)} %bitcast.34, bf16[1024,3072]{1,0:T(8,128)(2,1)} %wv_ref.3, ...), custom_call_target="tpu_custom_call" | custom-call | flops 4294967296 | bytes 13631488 | tf_op jit(solution)/shard_map/backward/pallas_call | solution.py:334
  68.7 0.0 collective-permute-done.5.received_ref
  68.7 1.0 %add_mixed.1._ = bf16[256,1536]{1,0:T(8,128)(2,1)} custom-call(bf16[256,512]{1,0:T(8,128)(2,1)S(1)} %add.8.rest_0_.own_ref, bf16[256,512]{1,0:T(8,128)(2,1)S(1)} %collective-permute-done.5.received_ref, bf16[256,1024]{1,0:T(8,128)(2,1)S(1)} %backward.1.back_ref), custom_call_target="tpu_custom_call" | custom-call | tf_op jit(solution)/shard_map/add_mixed/pallas_call | solution.py:54
  69.7 0.0 collective-permute-done.8.second_ref
  69.7 0.1 arrange.1
  69.8 0.1 collective-permute-start.9
  69.9 0.0 all-to-all-done.3
  69.9 4.9 %all-to-all-start.2 = ((bf16[8,32,1536]{2,1,0:T(8,128)(2,1)}), bf16[8,32,1536]{2,1,0:T(8,128)(2,1)S(1)}, u32[]{:S(2)}, u32[]{:S(2)}) async-start(bf16[8,32,1536]{2,1,0:T(8,128)(2,1)} %bitcast.6), calls=%async_computation.2 | async-start | bytes 1572864 | tf_op jit(solution)/shard_map/all_to_all | solution.py:396
  74.9 0.2 constant_dynamic-slice_fusion
  75.1 0.6 collective-permute-start.10
  75.7 7.9 %collective-permute-done.10.refs_1_ = bf16[1024,128]{1,0:T(8,128)(2,1)S(1)} collective-permute-done((bf16[1024,128]{1,0:T(8,128)(2,1)S(1)}, bf16[1024,128]{1,0:T(8,128)(2,1)S(1)}, u32[]{:S(2)}, u32[]{:S(2)}) %collective-permute-start.10) | collective-permute-done | bytes 262176 | tf_op jit(solution)/shard_map/ppermute | solution.py:400
  83.6 0.7 mix_gradient.1
  84.3 0.0 copy-start
  84.3 0.6 collective-permute-start.11
  84.9 7.1 %collective-permute-done.11 = bf16[128,1024]{1,0:T(8,128)(2,1)S(1)} collective-permute-done((bf16[128,1024]{1,0:T(8,128)(2,1)S(1)}, bf16[128,1024]{1,0:T(8,128)(2,1)S(1)}, u32[]{:S(2)}, u32[]{:S(2)}) %collective-permute-start.11) | collective-permute-done | bytes 262176 | tf_op jit(solution)/shard_map/ppermute | solution.py:400
  92.0 0.1 convert_add_fusion._
  92.0 0.0 copy-start.2
  92.0 3.6 %all-to-all-done.2.in_ref.back_ref = bf16[8,32,1536]{2,1,0:T(8,128)(2,1)S(1)} async-done(((bf16[8,32,1536]{2,1,0:T(8,128)(2,1)}), bf16[8,32,1536]{2,1,0:T(8,128)(2,1)S(1)}, u32[]{:S(2)}, u32[]{:S(2)}) %all-to-all-start.2) | async-done | bytes 786464 | tf_op jit(solution)/shard_map/all_to_all | solution.py:396
  95.7 0.1 collective-permute-start.12
  95.8 0.9 make_gradient.1
  96.7 0.6 collective-permute-done.12.other_ref
  97.3 1.0 make_output.1
  (13 shorter events, 0.1 us)
Async XLA Ops:
  2.7 30.6 %copy-start.4 = (s32[2,16]{1,0:T(2,128)S(1)}, s32[2,16]{1,0:T(2,128)}, u32[]{:S(2)}) copy-start(s32[2,16]{1,0:T(2,128)} %mask_ref.1) | copy-start | bytes 388
  2.7 22.1 %all-to-all-start = ((bf16[8,32,1024]{2,1,0:T(8,128)(2,1)}), bf16[8,32,1024]{2,1,0:T(8,128)(2,1)S(1)}, u32[]{:S(2)}, u32[]{:S(2)}) async-start(bf16[8,32,1024]{2,1,0:T(8,128)(2,1)} %get-tuple-element.20), calls=%async_computation | async-start | bytes 1048576 | tf_op jit(solution)/shard_map/all_to_all | solution.py:396
  10.1 1.5 %collective-permute-start = (bf16[8,32,512]{2,1,0:T(8,128)(2,1)S(1)}, bf16[8,32,512]{2,1,0:T(8,128)(2,1)S(1)}, u32[]{:S(2)}, u32[]{:S(2)}) collective-permute-start(bf16[8,32,512]{2,1,0:T(8,128)(2,1)S(1)} %get-tuple-element.22), channel_id=1, source_target_pairs={{0,1},{1,0},{2,3},{3,2},{4,5},{5,4},{6,7},{7,6},{8,9},{9,8},{10,11... | collective-permute-start | bytes 786440 | tf_op jit(solution)/shard_map/ppermute | solution.py:400
  11.7 5.6 %collective-permute-start.1 = (bf16[8,16,512]{2,1,0:T(8,128)(2,1)S(1)}, bf16[8,16,512]{2,1,0:T(8,128)(2,1)S(1)}, u32[]{:S(2)}, u32[]{:S(2)}) collective-permute-start(bf16[8,16,512]{2,1,0:T(8,128)(2,1)S(1)} %get-tuple-element.24.second_ref), channel_id=1, source_target_pairs={{0,2},{1,3},{2,0},{3,1},{4,6},{5,7},{6,4},{7,5},{8,10},{9,11},{10,... | collective-permute-start | bytes 393224 | tf_op jit(solution)/shard_map/ppermute | solution.py:400
  17.3 7.5 %collective-permute-start.3 = (bf16[1,8,16,512]{3,2,1,0:T(8,128)(2,1)S(1)}, bf16[1,8,16,512]{3,2,1,0:T(8,128)(2,1)S(1)}, u32[]{:S(2)}, u32[]{:S(2)}) collective-permute-start(bf16[1,8,16,512]{3,2,1,0:T(8,128)(2,1)S(1)} %bitcast.28), channel_id=1, source_target_pairs={{0,8},{4,12},{8,0},{12,4},{16,24},{20,28},{24,16},{28,20},{1,9},{5... | collective-permute-start | bytes 393224 | tf_op jit(solution)/shard_map/ppermute | solution.py:484
  19.4 5.4 %collective-permute-start.2 = (bf16[8,16,512]{2,1,0:T(8,128)(2,1)S(1)}, bf16[8,16,512]{2,1,0:T(8,128)(2,1)S(1)}, u32[]{:S(2)}, u32[]{:S(2)}) collective-permute-start(bf16[8,16,512]{2,1,0:T(8,128)(2,1)S(1)} %get-tuple-element.23.own_ref), channel_id=1, source_target_pairs={{0,2},{1,3},{2,0},{3,1},{4,6},{5,7},{6,4},{7,5},{8,10},{9,11},{10,... | collective-permute-start | bytes 393224 | tf_op jit(solution)/shard_map/ppermute | solution.py:400
  25.6 20.5 %all-to-all-start.1 = ((bf16[8,32,512]{2,1,0:T(8,128)(2,1)}), bf16[8,32,512]{2,1,0:T(8,128)(2,1)S(1)}, u32[]{:S(2)}, u32[]{:S(2)}) async-start(bf16[8,32,512]{2,1,0:T(8,128)(2,1)} %add_flow.1._), calls=%async_computation.1 | async-start | bytes 524288 | tf_op jit(solution)/shard_map/all_to_all | solution.py:396
  30.4 19.9 %collective-permute-start.7 = (bf16[2,8,16,512]{3,2,1,0:T(8,128)(2,1)S(1)}, bf16[2,8,16,512]{3,2,1,0:T(8,128)(2,1)S(1)}, u32[]{:S(2)}, u32[]{:S(2)}) collective-permute-start(bf16[2,8,16,512]{3,2,1,0:T(8,128)(2,1)S(1)} %join.2.__.first_ref), channel_id=1, source_target_pairs={{0,16},{4,20},{8,24},{12,28},{16,0},{20,4},{24,8},{28,12},{1,17},{... | collective-permute-start | bytes 786440 | tf_op jit(solution)/shard_map/ppermute | solution.py:484
  46.1 23.8 %all-to-all-start.3 = ((bf16[8,256,128]{2,1,0:T(8,128)(2,1)}), bf16[8,256,128]{2,1,0:T(8,128)(2,1)S(1)}, u32[]{:S(2)}, u32[]{:S(2)}) async-start(bf16[8,256,128]{2,1,0:T(8,128)(2,1)} %get-tuple-element.34), calls=%async_computation.3 | async-start | bytes 1048576 | tf_op jit(solution)/shard_map/all_to_all | solution.py:396
  49.6 2.5 %collective-permute-start.4 = (bf16[256,512]{1,0:T(8,128)(2,1)S(1)}, bf16[256,512]{1,0:T(8,128)(2,1)S(1)}, u32[]{:S(2)}, u32[]{:S(2)}) collective-permute-start(bf16[256,512]{1,0:T(8,128)(2,1)S(1)} %get-tuple-element.26), channel_id=1, source_target_pairs={{0,1},{1,0},{2,3},{3,2},{4,5},{5,4},{6,7},{7,6},{8,9},{9,8},{10,11... | collective-permute-start | bytes 786440 | tf_op jit(solution)/shard_map/ppermute | solution.py:400
  49.6 4.1 %collective-permute-start.6 = (bf16[256,512]{1,0:T(8,128)(2,1)S(1)}, bf16[256,512]{1,0:T(8,128)(2,1)S(1)}, u32[]{:S(2)}, u32[]{:S(2)}) collective-permute-start(bf16[256,512]{1,0:T(8,128)(2,1)S(1)} %bitcast.30), channel_id=1, source_target_pairs={{0,1},{1,0},{2,3},{3,2},{4,5},{5,4},{6,7},{7,6},{8,9},{9,8},{10,11... | collective-permute-start | bytes 786440 | tf_op jit(solution)/shard_map/ppermute | solution.py:400
  50.3 19.4 %collective-permute-start.8 = (bf16[4,8,16,512]{3,2,1,0:T(8,128)(2,1)S(1)}, bf16[4,8,16,512]{3,2,1,0:T(8,128)(2,1)S(1)}, u32[]{:S(2)}, u32[]{:S(2)}) collective-permute-start(bf16[4,8,16,512]{3,2,1,0:T(8,128)(2,1)S(1)} %join.3.rest_1_.first_ref), channel_id=1, source_target_pairs={{0,4},{4,0},{8,12},{12,8},{16,20},{20,16},{24,28},{28,24},{1,5},{5... | collective-permute-start | bytes 1572872 | tf_op jit(solution)/shard_map/ppermute | solution.py:484
  52.2 16.6 %collective-permute-start.5 = (bf16[256,512]{1,0:T(8,128)(2,1)S(1)}, bf16[256,512]{1,0:T(8,128)(2,1)S(1)}, u32[]{:S(2)}, u32[]{:S(2)}) collective-permute-start(bf16[256,512]{1,0:T(8,128)(2,1)S(1)} %add.8.rest_0_.own_ref), channel_id=1, source_target_pairs={{0,2},{1,3},{2,0},{3,1},{4,6},{5,7},{6,4},{7,5},{8,10},{9,11},{10,... | collective-permute-start | bytes 786440 | tf_op jit(solution)/shard_map/ppermute | solution.py:400
  69.8 13.7 %collective-permute-start.9 = (bf16[1024,512]{1,0:T(8,128)(2,1)S(1)}, bf16[1024,512]{1,0:T(8,128)(2,1)S(1)}, u32[]{:S(2)}, u32[]{:S(2)}) collective-permute-start(bf16[1024,512]{1,0:T(8,128)(2,1)S(1)} %bitcast.21), channel_id=1, source_target_pairs={{0,1},{1,0},{2,3},{3,2},{4,5},{5,4},{6,7},{7,6},{8,9},{9,8},{10,11... | collective-permute-start | bytes 3145736 | tf_op jit(solution)/shard_map/ppermute | solution.py:400
  69.9 25.7 %all-to-all-start.2 = ((bf16[8,32,1536]{2,1,0:T(8,128)(2,1)}), bf16[8,32,1536]{2,1,0:T(8,128)(2,1)S(1)}, u32[]{:S(2)}, u32[]{:S(2)}) async-start(bf16[8,32,1536]{2,1,0:T(8,128)(2,1)} %bitcast.6), calls=%async_computation.2 | async-start | bytes 1572864 | tf_op jit(solution)/shard_map/all_to_all | solution.py:396
  75.1 8.5 %collective-permute-start.10 = (bf16[1024,128]{1,0:T(8,128)(2,1)S(1)}, bf16[1024,128]{1,0:T(8,128)(2,1)S(1)}, u32[]{:S(2)}, u32[]{:S(2)}) collective-permute-start(bf16[1024,128]{1,0:T(8,128)(2,1)S(1)} %bitcast.38), channel_id=1, source_target_pairs={{0,2},{1,3},{2,0},{3,1},{4,6},{5,7},{6,4},{7,5},{8,10},{9,11},{10,... | collective-permute-start | bytes 786440 | tf_op jit(solution)/shard_map/ppermute | solution.py:400
  84.3 11.4 %copy-start = (bf16[2,1,2,64,1024]{4,3,2,1,0:T(8,128)(2,1)S(1)}, bf16[2,1,2,64,1024]{4,3,2,1,0:T(8,128)(2,1)}, u32[]{:S(2)}) copy-start(bf16[2,1,2,64,1024]{4,3,2,1,0:T(8,128)(2,1)} %param.11) | copy-start | bytes 1572868
  84.3 7.7 %collective-permute-start.11 = (bf16[128,1024]{1,0:T(8,128)(2,1)S(1)}, bf16[128,1024]{1,0:T(8,128)(2,1)S(1)}, u32[]{:S(2)}, u32[]{:S(2)}) collective-permute-start(bf16[128,1024]{1,0:T(8,128)(2,1)S(1)} %get-tuple-element.36), channel_id=1, source_target_pairs={{0,2},{1,3},{2,0},{3,1},{4,6},{5,7},{6,4},{7,5},{8,10},{9,11},{10,... | collective-permute-start | bytes 786440 | tf_op jit(solution)/shard_map/ppermute | solution.py:400
  92.0 5.3 %copy-start.1 = (bf16[2,1,2,64,1024]{4,3,2,1,0:T(8,128)(2,1)S(1)}, bf16[2,1,2,64,1024]{4,3,2,1,0:T(8,128)(2,1)}, u32[]{:S(2)}) copy-start(bf16[2,1,2,64,1024]{4,3,2,1,0:T(8,128)(2,1)} %param.6) | copy-start | bytes 1572868
  92.0 5.3 %copy-start.3 = (f32[1,1024]{1,0:T(1,128)S(1)}, f32[1,1024]{1,0:T(1,128)}, u32[]{:S(2)}) copy-start(f32[1,1024]{1,0:T(1,128)} %gain_ref.3) | copy-start | bytes 12292
  92.0 6.2 %copy-start.2 = (f32[128,1024]{1,0:T(8,128)}, f32[128,1024]{1,0:T(8,128)S(1)}, u32[]{:S(2)}) copy-start(f32[128,1024]{1,0:T(8,128)S(1)} %convert_add_fusion._) | copy-start | bytes 1572868
  95.7 1.6 %collective-permute-start.12 = (bf16[8,32,512]{2,1,0:T(8,128)(2,1)S(1)}, bf16[8,32,512]{2,1,0:T(8,128)(2,1)S(1)}, u32[]{:S(2)}, u32[]{:S(2)}) collective-permute-start(bf16[8,32,512]{2,1,0:T(8,128)(2,1)S(1)} %cut_mixed.1.own_ref), channel_id=1, source_target_pairs={{0,1},{1,0},{2,3},{3,2},{4,5},{5,4},{6,7},{7,6},{8,9},{9,8},{10,11... | collective-permute-start | bytes 786440 | tf_op jit(solution)/shard_map/ppermute | solution.py:400
where the time goes:
time: 98.8 us; the launch traced here: 98.2 us
  starting transfers between devices  34 us (34%)
  waiting for transfers between devices  31.8 us (32%)
  Pallas kernels  31.4 us (32%)
    ppermute x10, waiting for transfers between devices, from_level(): lax.ppermute(block, 'lev', [(i, i ^ offset) for i in range(lax.axis_size(...  21.1 us
    all_to_all x4, starting transfers between devices, swap(): return lax.all_to_all(block, 'lat', split_axis=0, concat_axis=0, tiled=True)  20.6 us
    pallas_call x1, Pallas kernels, backward(): pl.pallas_call(backward_kernel, out_shape=jax.ShapeDtypeStruct((count, wi...  15 us
    pallas_call x1, Pallas kernels, forward(): pl.pallas_call(functools.partial(forward_kernel, samples, lat_count, chun...  9.67 us
    ppermute x3, starting transfers between devices, from_owner(): lax.ppermute(block, 'lat', [(i, i ^ offset) for i in range(lax.axis_size(...  6.81 us
    all_to_all x4, waiting for transfers between devices, swap(): return lax.all_to_all(block, 'lat', split_axis=0, concat_axis=0, tiled=True)  6.68 us
    ppermute x10, starting transfers between devices, from_level(): lax.ppermute(block, 'lev', [(i, i ^ offset) for i in range(lax.axis_size(...  6.58 us
    pallas_call x9, Pallas kernels, call(): pl.pallas_call(kernel, out_shape=out_shape, compiler_params=params(), nam...  5.15 us
  transfers between devices with their start and end apart: 17, of which 9 were waited for; matrix products, arithmetic and copies ran while one was open for 0% of the time, Pallas kernels for 28%

commit v1 on v0

--- a/solution.py
+++ b/solution.py
@@ -266,12 +266,17 @@
     tok_ref, own_ref, other_ref, wm_ref, wq_ref, wk_ref, wv_ref,
     qn_ref, kn_ref, v_ref, rq_ref, rk_ref, ri_ref, p_ref, *rest,
 ):
-    out_ref, acc_ref = rest[-2:]
+    out_ref, acc_ref, flow_t_ref = rest[-3:]
     step = pl.program_id(0)
-    count, width = acc_ref.shape
+    width, count = acc_ref.shape
     head_width = width // HEADS
-    d_att = nt(own_ref[...], wm_ref[:, half_cols(0, width)])
-    d_att += nt(other_ref[...], wm_ref[:, half_cols(1, width)])
+
+    @pl.when(step == 0)
+    def _():
+        for s, ref in enumerate((own_ref, other_ref)):
+            flow_t_ref[half_cols(s, width), :] = ref[...].T
+
+    d_att = nn(wm_ref[...], flow_t_ref[...]).T
     inverse = ri_ref[...]
     d_att = (d_att * inverse).astype(BF16)
     qn, kn, v = qn_ref[...], kn_ref[...], v_ref[...]
@@ -306,7 +311,7 @@
 
     gq = through_norm(dq, qn, rq_ref[...])
     gk = through_norm(dk, kn, rk_ref[...])
-    total = nt(gq, wq_ref[...]) + nt(gk, wk_ref[...]) + nt(dv, wv_ref[...])
+    total = nt(wq_ref[...], gq) + nt(wk_ref[...], gk) + nt(wv_ref[...], dv)
 
     @pl.when(step == 0)
     def _():
@@ -320,7 +325,7 @@
     def _():
         x = tok_ref[...].astype(F32)
         rx = lax.rsqrt(jnp.mean(x * x, axis=-1, keepdims=True) + epsilon)
-        d = acc_ref[...]
+        d = acc_ref[...].T
         inner = jnp.mean(d * x, axis=-1, keepdims=True)
         out_ref[...] = (rx * d - x * (rx * rx * rx * inner)).astype(BF16)
 
@@ -348,7 +353,7 @@
         ]
         + [pl.BlockSpec(memory_space=pl.ANY)] * len(after),
         out_specs=same((count, width)),
-        scratch_shapes=[pltpu.VMEM((count, width), F32)],
+        scratch_shapes=[pltpu.VMEM((width, count), F32), pltpu.VMEM((width, count), BF16)],
         compiler_params=params(),
         cost_estimate=pl.CostEstimate(
             flops=2 * count * width * (4 * width + 4 * count * 4),

time: 98.8 us -> 99.9 us (1.011)
  Pallas kernels: 31.4 us -> 32.5 us
    pallas_call x1, Pallas kernels: 15 us -> 16.1 us  [backward(): pl.pallas_call(backward_kernel, out_shape=jax.ShapeDtypeStruct((count, wi...]
  transfers between devices with their start and end apart: 17 -> 17, of which waited for: 9 -> 9; matrix products, arithmetic and copies ran while one was open for 0% -> 0% of each run, Pallas kernels for 28% -> 29%
where the time goes in v1:
time: 99.9 us; the launch traced here: 99.4 us
  starting transfers between devices  34 us (34%)
  Pallas kernels  32.5 us (33%)
  waiting for transfers between devices  31.8 us (32%)
    ppermute x10, waiting for transfers between devices, from_level(): lax.ppermute(block, 'lev', [(i, i ^ offset) for i in range(lax.axis_size(...  21.1 us
    all_to_all x4, starting transfers between devices, swap(): return lax.all_to_all(block, 'lat', split_axis=0, concat_axis=0, tiled=True)  20.6 us
    pallas_call x1, Pallas kernels, backward(): pl.pallas_call(backward_kernel, out_shape=jax.ShapeDtypeStruct((count, wi...  16.1 us
    pallas_call x1, Pallas kernels, forward(): pl.pallas_call(functools.partial(forward_kernel, samples, lat_count, chun...  9.67 us
    ppermute x3, starting transfers between devices, from_owner(): lax.ppermute(block, 'lat', [(i, i ^ offset) for i in range(lax.axis_size(...  6.81 us
    all_to_all x4, waiting for transfers between devices, swap(): return lax.all_to_all(block, 'lat', split_axis=0, concat_axis=0, tiled=True)  6.68 us
    ppermute x10, starting transfers between devices, from_level(): lax.ppermute(block, 'lev', [(i, i ^ offset) for i in range(lax.axis_size(...  6.55 us
    pallas_call x9, Pallas kernels, call(): pl.pallas_call(kernel, out_shape=out_shape, compiler_params=params(), nam...  5.15 us
  transfers between devices with their start and end apart: 17, of which 9 were waited for; matrix products, arithmetic and copies ran while one was open for 0% of the time, Pallas kernels for 29%

profile of v1, /device:TPU:0, one launch (start us, length us, event | category | flops | bytes accessed | tf_op | source)
XLA Modules:
  0.0 99.4 jit_solution(13995376362692702355)
XLA Ops:
  0.6 2.1 %pack.1 = (bf16[8,32,1024]{2,1,0:T(8,128)(2,1)}, bf16[8,32,512]{2,1,0:T(8,128)(2,1)S(1)}, bf16[8,32,512]{2,1,0:T(8,128)(2,1)S(1)}) custom-call(bf16[2,2,4,16,1024]{4,3,2,1,0:T(8,128)(2,1)} %bitcast.25, bf16[2,2,4,16,1024]{4,3,2,1,0:T(8,128)(2,1)} %bitcast.23, f32[1,1024]{1,0:T(1,128)} %gain_ref.3), custom_call_target="tpu_custom_call" | custom-call | tf_op jit(solution)/shard_map/pack/pallas_call | solution.py:54
  2.7 7.4 %all-to-all-start = ((bf16[8,32,1024]{2,1,0:T(8,128)(2,1)}), bf16[8,32,1024]{2,1,0:T(8,128)(2,1)S(1)}, u32[]{:S(2)}, u32[]{:S(2)}) async-start(bf16[8,32,1024]{2,1,0:T(8,128)(2,1)} %get-tuple-element.20), calls=%async_computation | async-start | bytes 1048576 | tf_op jit(solution)/shard_map/all_to_all | solution.py:401
  10.1 0.0 collective-permute-start
  10.1 1.5 %collective-permute-done.received_ref = bf16[8,32,512]{2,1,0:T(8,128)(2,1)S(1)} collective-permute-done((bf16[8,32,512]{2,1,0:T(8,128)(2,1)S(1)}, bf16[8,32,512]{2,1,0:T(8,128)(2,1)S(1)}, u32[]{:S(2)}, u32[]{:S(2)}) %collective-permute-start) | collective-permute-done | bytes 262176 | tf_op jit(solution)/shard_map/ppermute | solution.py:405
  11.6 0.1 split_rows.1
  11.7 1.6 %collective-permute-start.1 = (bf16[8,16,512]{2,1,0:T(8,128)(2,1)S(1)}, bf16[8,16,512]{2,1,0:T(8,128)(2,1)S(1)}, u32[]{:S(2)}, u32[]{:S(2)}) collective-permute-start(bf16[8,16,512]{2,1,0:T(8,128)(2,1)S(1)} %get-tuple-element.24.second_ref), channel_id=1, source_target_pairs={{0,2},{1,3},{2,0},{3,1},{4,6},{5,7},{6,4},{7,5},{8,10},{9,11},{10,... | collective-permute-start | bytes 393224 | tf_op jit(solution)/shard_map/ppermute | solution.py:405
  13.3 4.0 %collective-permute-done.1.received_ref = bf16[8,16,512]{2,1,0:T(8,128)(2,1)S(1)} collective-permute-done((bf16[8,16,512]{2,1,0:T(8,128)(2,1)S(1)}, bf16[8,16,512]{2,1,0:T(8,128)(2,1)S(1)}, u32[]{:S(2)}, u32[]{:S(2)}) %collective-permute-start.1) | collective-permute-done | bytes 131104 | tf_op jit(solution)/shard_map/ppermute | solution.py:405
  17.3 2.1 %collective-permute-start.3 = (bf16[1,8,16,512]{3,2,1,0:T(8,128)(2,1)S(1)}, bf16[1,8,16,512]{3,2,1,0:T(8,128)(2,1)S(1)}, u32[]{:S(2)}, u32[]{:S(2)}) collective-permute-start(bf16[1,8,16,512]{3,2,1,0:T(8,128)(2,1)S(1)} %bitcast.28), channel_id=1, source_target_pairs={{0,8},{4,12},{8,0},{12,4},{16,24},{20,28},{24,16},{28,20},{1,9},{5... | collective-permute-start | bytes 393224 | tf_op jit(solution)/shard_map/ppermute | solution.py:489
  19.4 1.5 %collective-permute-start.2 = (bf16[8,16,512]{2,1,0:T(8,128)(2,1)S(1)}, bf16[8,16,512]{2,1,0:T(8,128)(2,1)S(1)}, u32[]{:S(2)}, u32[]{:S(2)}) collective-permute-start(bf16[8,16,512]{2,1,0:T(8,128)(2,1)S(1)} %get-tuple-element.23.own_ref), channel_id=1, source_target_pairs={{0,2},{1,3},{2,0},{3,1},{4,6},{5,7},{6,4},{7,5},{8,10},{9,11},{10,... | collective-permute-start | bytes 393224 | tf_op jit(solution)/shard_map/ppermute | solution.py:405
  20.9 3.9 %collective-permute-done.3.second_ref = bf16[1,8,16,512]{3,2,1,0:T(8,128)(2,1)S(1)} collective-permute-done((bf16[1,8,16,512]{3,2,1,0:T(8,128)(2,1)S(1)}, bf16[1,8,16,512]{3,2,1,0:T(8,128)(2,1)S(1)}, u32[]{:S(2)}, u32[]{:S(2)}) %collective-permute-start.3) | collective-permute-done | bytes 131104 | tf_op jit(solution)/shard_map/ppermute | solution.py:489
  24.8 0.0 collective-permute-done.2.received_ref
  24.8 0.0 all-to-all-done
  24.8 0.8 add_flow.1._
  25.6 4.8 %all-to-all-start.1 = ((bf16[8,32,512]{2,1,0:T(8,128)(2,1)}), bf16[8,32,512]{2,1,0:T(8,128)(2,1)S(1)}, u32[]{:S(2)}, u32[]{:S(2)}) async-start(bf16[8,32,512]{2,1,0:T(8,128)(2,1)} %add_flow.1._), calls=%async_computation.1 | async-start | bytes 524288 | tf_op jit(solution)/shard_map/all_to_all | solution.py:401
  30.4 2.9 %collective-permute-start.7 = (bf16[2,8,16,512]{3,2,1,0:T(8,128)(2,1)S(1)}, bf16[2,8,16,512]{3,2,1,0:T(8,128)(2,1)S(1)}, u32[]{:S(2)}, u32[]{:S(2)}) collective-permute-start(bf16[2,8,16,512]{3,2,1,0:T(8,128)(2,1)S(1)} %join.2.__.first_ref), channel_id=1, source_target_pairs={{0,16},{4,20},{8,24},{12,28},{16,0},{20,4},{24,8},{28,12},{1,17},{... | collective-permute-start | bytes 786440 | tf_op jit(solution)/shard_map/ppermute | solution.py:489
  33.3 9.7 %forward.1 = (bf16[256,1024]{1,0:T(8,128)(2,1)}, bf16[256,1024]{1,0:T(8,128)(2,1)}, bf16[256,1024]{1,0:T(8,128)(2,1)}, bf16[256,1024]{1,0:T(8,128)(2,1)}, bf16[2...) custom-call(bf16[256,1024]{1,0:T(8,128)(2,1)S(1)} %bitcast.19, ...), custom_call_target="tpu_custom_call" | custom-call | flops 3221225472 | bytes 13631488 | tf_op jit(solution)/shard_map/forward/pallas_call | solution.py:225
  43.0 3.1 %all-to-all-done.1 = bf16[8,32,512]{2,1,0:T(8,128)(2,1)S(1)} async-done(((bf16[8,32,512]{2,1,0:T(8,128)(2,1)}), bf16[8,32,512]{2,1,0:T(8,128)(2,1)S(1)}, u32[]{:S(2)}, u32[]{:S(2)}) %all-to-all-start.1) | async-done | bytes 262176 | tf_op jit(solution)/shard_map/all_to_all | solution.py:401
  46.1 3.5 %all-to-all-start.3 = ((bf16[8,256,128]{2,1,0:T(8,128)(2,1)}), bf16[8,256,128]{2,1,0:T(8,128)(2,1)S(1)}, u32[]{:S(2)}, u32[]{:S(2)}) async-start(bf16[8,256,128]{2,1,0:T(8,128)(2,1)} %get-tuple-element.34), calls=%async_computation.3 | async-start | bytes 1048576 | tf_op jit(solution)/shard_map/all_to_all | solution.py:401
  49.6 0.1 collective-permute-start.4
  49.6 0.5 collective-permute-start.6
  50.1 0.1 collective-permute-done.7.second_ref
  50.3 1.8 %collective-permute-start.8 = (bf16[4,8,16,512]{3,2,1,0:T(8,128)(2,1)S(1)}, bf16[4,8,16,512]{3,2,1,0:T(8,128)(2,1)S(1)}, u32[]{:S(2)}, u32[]{:S(2)}) collective-permute-start(bf16[4,8,16,512]{3,2,1,0:T(8,128)(2,1)S(1)} %join.3.rest_1_.first_ref), channel_id=1, source_target_pairs={{0,4},{4,0},{8,12},{12,8},{16,20},{20,16},{24,28},{28,24},{1,5},{5... | collective-permute-start | bytes 1572872 | tf_op jit(solution)/shard_map/ppermute | solution.py:489
  52.1 0.0 collective-permute-done.4.received_ref
  52.1 0.1 add.8.rest_0_.own_ref
  52.2 1.6 %collective-permute-start.5 = (bf16[256,512]{1,0:T(8,128)(2,1)S(1)}, bf16[256,512]{1,0:T(8,128)(2,1)S(1)}, u32[]{:S(2)}, u32[]{:S(2)}) collective-permute-start(bf16[256,512]{1,0:T(8,128)(2,1)S(1)} %add.8.rest_0_.own_ref), channel_id=1, source_target_pairs={{0,2},{1,3},{2,0},{3,1},{4,6},{5,7},{6,4},{7,5},{8,10},{9,11},{10,... | collective-permute-start | bytes 786440 | tf_op jit(solution)/shard_map/ppermute | solution.py:405
  53.8 0.0 collective-permute-done.6.other_ref
  53.8 16.1 %backward.1.back_ref = bf16[256,1024]{1,0:T(8,128)(2,1)S(1)} custom-call(bf16[256,1024]{1,0:T(8,128)(2,1)S(1)} %bitcast.20, bf16[256,512]{1,0:T(8,128)(2,1)S(1)} %bitcast.31, bf16[256,512]{1,0:T(8,128)(2,1)S(1)} %collective-permute-done.6.other_ref, bf16[1024,1024]{1,0:T(8,128)(2,1)} %bitcast.34, bf16[1024,3072]{1,0:T(8,128)(2,1)} %wv_ref.3, ...), custom_call_target="tpu_custom_call" | custom-call | flops 4294967296 | bytes 13631488 | tf_op jit(solution)/shard_map/backward/pallas_call | solution.py:339
  69.9 0.0 collective-permute-done.5.received_ref
  69.9 1.0 %add_mixed.1._ = bf16[256,1536]{1,0:T(8,128)(2,1)} custom-call(bf16[256,512]{1,0:T(8,128)(2,1)S(1)} %add.8.rest_0_.own_ref, bf16[256,512]{1,0:T(8,128)(2,1)S(1)} %collective-permute-done.5.received_ref, bf16[256,1024]{1,0:T(8,128)(2,1)S(1)} %backward.1.back_ref), custom_call_target="tpu_custom_call" | custom-call | tf_op jit(solution)/shard_map/add_mixed/pallas_call | solution.py:54
  70.9 0.0 collective-permute-done.8.second_ref
  70.9 0.1 arrange.1
  70.9 0.1 collective-permute-start.9
  71.0 0.0 all-to-all-done.3
  71.0 4.9 %all-to-all-start.2 = ((bf16[8,32,1536]{2,1,0:T(8,128)(2,1)}), bf16[8,32,1536]{2,1,0:T(8,128)(2,1)S(1)}, u32[]{:S(2)}, u32[]{:S(2)}) async-start(bf16[8,32,1536]{2,1,0:T(8,128)(2,1)} %bitcast.6), calls=%async_computation.2 | async-start | bytes 1572864 | tf_op jit(solution)/shard_map/all_to_all | solution.py:401
  76.0 0.2 constant_dynamic-slice_fusion
  76.2 0.6 collective-permute-start.10
  76.8 7.9 %collective-permute-done.10.refs_1_ = bf16[1024,128]{1,0:T(8,128)(2,1)S(1)} collective-permute-done((bf16[1024,128]{1,0:T(8,128)(2,1)S(1)}, bf16[1024,128]{1,0:T(8,128)(2,1)S(1)}, u32[]{:S(2)}, u32[]{:S(2)}) %collective-permute-start.10) | collective-permute-done | bytes 262176 | tf_op jit(solution)/shard_map/ppermute | solution.py:405
  84.7 0.7 mix_gradient.1
  85.4 0.0 copy-start
  85.4 0.6 collective-permute-start.11
  86.0 7.1 %collective-permute-done.11 = bf16[128,1024]{1,0:T(8,128)(2,1)S(1)} collective-permute-done((bf16[128,1024]{1,0:T(8,128)(2,1)S(1)}, bf16[128,1024]{1,0:T(8,128)(2,1)S(1)}, u32[]{:S(2)}, u32[]{:S(2)}) %collective-permute-start.11) | collective-permute-done | bytes 262176 | tf_op jit(solution)/shard_map/ppermute | solution.py:405
  93.1 0.1 convert_add_fusion._
  93.2 0.0 copy-start.2
  93.2 3.6 %all-to-all-done.2.in_ref.back_ref = bf16[8,32,1536]{2,1,0:T(8,128)(2,1)S(1)} async-done(((bf16[8,32,1536]{2,1,0:T(8,128)(2,1)}), bf16[8,32,1536]{2,1,0:T(8,128)(2,1)S(1)}, u32[]{:S(2)}, u32[]{:S(2)}) %all-to-all-start.2) | async-done | bytes 786464 | tf_op jit(solution)/shard_map/all_to_all | solution.py:401
  96.8 0.1 collective-permute-start.12
  96.9 0.9 make_gradient.1
  97.8 0.6 collective-permute-done.12.other_ref
  98.4 1.0 make_output.1
  (13 shorter events, 0.1 us)
Async XLA Ops:
  2.7 30.6 %copy-start.4 = (s32[2,16]{1,0:T(2,128)S(1)}, s32[2,16]{1,0:T(2,128)}, u32[]{:S(2)}) copy-start(s32[2,16]{1,0:T(2,128)} %mask_ref.1) | copy-start | bytes 388
  2.7 22.1 %all-to-all-start = ((bf16[8,32,1024]{2,1,0:T(8,128)(2,1)}), bf16[8,32,1024]{2,1,0:T(8,128)(2,1)S(1)}, u32[]{:S(2)}, u32[]{:S(2)}) async-start(bf16[8,32,1024]{2,1,0:T(8,128)(2,1)} %get-tuple-element.20), calls=%async_computation | async-start | bytes 1048576 | tf_op jit(solution)/shard_map/all_to_all | solution.py:401
  10.1 1.5 %collective-permute-start = (bf16[8,32,512]{2,1,0:T(8,128)(2,1)S(1)}, bf16[8,32,512]{2,1,0:T(8,128)(2,1)S(1)}, u32[]{:S(2)}, u32[]{:S(2)}) collective-permute-start(bf16[8,32,512]{2,1,0:T(8,128)(2,1)S(1)} %get-tuple-element.22), channel_id=1, source_target_pairs={{0,1},{1,0},{2,3},{3,2},{4,5},{5,4},{6,7},{7,6},{8,9},{9,8},{10,11... | collective-permute-start | bytes 786440 | tf_op jit(solution)/shard_map/ppermute | solution.py:405
  11.7 5.6 %collective-permute-start.1 = (bf16[8,16,512]{2,1,0:T(8,128)(2,1)S(1)}, bf16[8,16,512]{2,1,0:T(8,128)(2,1)S(1)}, u32[]{:S(2)}, u32[]{:S(2)}) collective-permute-start(bf16[8,16,512]{2,1,0:T(8,128)(2,1)S(1)} %get-tuple-element.24.second_ref), channel_id=1, source_target_pairs={{0,2},{1,3},{2,0},{3,1},{4,6},{5,7},{6,4},{7,5},{8,10},{9,11},{10,... | collective-permute-start | bytes 393224 | tf_op jit(solution)/shard_map/ppermute | solution.py:405
  17.3 7.5 %collective-permute-start.3 = (bf16[1,8,16,512]{3,2,1,0:T(8,128)(2,1)S(1)}, bf16[1,8,16,512]{3,2,1,0:T(8,128)(2,1)S(1)}, u32[]{:S(2)}, u32[]{:S(2)}) collective-permute-start(bf16[1,8,16,512]{3,2,1,0:T(8,128)(2,1)S(1)} %bitcast.28), channel_id=1, source_target_pairs={{0,8},{4,12},{8,0},{12,4},{16,24},{20,28},{24,16},{28,20},{1,9},{5... | collective-permute-start | bytes 393224 | tf_op jit(solution)/shard_map/ppermute | solution.py:489
  19.4 5.4 %collective-permute-start.2 = (bf16[8,16,512]{2,1,0:T(8,128)(2,1)S(1)}, bf16[8,16,512]{2,1,0:T(8,128)(2,1)S(1)}, u32[]{:S(2)}, u32[]{:S(2)}) collective-permute-start(bf16[8,16,512]{2,1,0:T(8,128)(2,1)S(1)} %get-tuple-element.23.own_ref), channel_id=1, source_target_pairs={{0,2},{1,3},{2,0},{3,1},{4,6},{5,7},{6,4},{7,5},{8,10},{9,11},{10,... | collective-permute-start | bytes 393224 | tf_op jit(solution)/shard_map/ppermute | solution.py:405
  25.6 20.5 %all-to-all-start.1 = ((bf16[8,32,512]{2,1,0:T(8,128)(2,1)}), bf16[8,32,512]{2,1,0:T(8,128)(2,1)S(1)}, u32[]{:S(2)}, u32[]{:S(2)}) async-start(bf16[8,32,512]{2,1,0:T(8,128)(2,1)} %add_flow.1._), calls=%async_computation.1 | async-start | bytes 524288 | tf_op jit(solution)/shard_map/all_to_all | solution.py:401
  30.4 19.9 %collective-permute-start.7 = (bf16[2,8,16,512]{3,2,1,0:T(8,128)(2,1)S(1)}, bf16[2,8,16,512]{3,2,1,0:T(8,128)(2,1)S(1)}, u32[]{:S(2)}, u32[]{:S(2)}) collective-permute-start(bf16[2,8,16,512]{3,2,1,0:T(8,128)(2,1)S(1)} %join.2.__.first_ref), channel_id=1, source_target_pairs={{0,16},{4,20},{8,24},{12,28},{16,0},{20,4},{24,8},{28,12},{1,17},{... | collective-permute-start | bytes 786440 | tf_op jit(solution)/shard_map/ppermute | solution.py:489
  46.1 25.0 %all-to-all-start.3 = ((bf16[8,256,128]{2,1,0:T(8,128)(2,1)}), bf16[8,256,128]{2,1,0:T(8,128)(2,1)S(1)}, u32[]{:S(2)}, u32[]{:S(2)}) async-start(bf16[8,256,128]{2,1,0:T(8,128)(2,1)} %get-tuple-element.34), calls=%async_computation.3 | async-start | bytes 1048576 | tf_op jit(solution)/shard_map/all_to_all | solution.py:401
  49.6 2.5 %collective-permute-start.4 = (bf16[256,512]{1,0:T(8,128)(2,1)S(1)}, bf16[256,512]{1,0:T(8,128)(2,1)S(1)}, u32[]{:S(2)}, u32[]{:S(2)}) collective-permute-start(bf16[256,512]{1,0:T(8,128)(2,1)S(1)} %get-tuple-element.26), channel_id=1, source_target_pairs={{0,1},{1,0},{2,3},{3,2},{4,5},{5,4},{6,7},{7,6},{8,9},{9,8},{10,11... | collective-permute-start | bytes 786440 | tf_op jit(solution)/shard_map/ppermute | solution.py:405
  49.6 4.1 %collective-permute-start.6 = (bf16[256,512]{1,0:T(8,128)(2,1)S(1)}, bf16[256,512]{1,0:T(8,128)(2,1)S(1)}, u32[]{:S(2)}, u32[]{:S(2)}) collective-permute-start(bf16[256,512]{1,0:T(8,128)(2,1)S(1)} %bitcast.30), channel_id=1, source_target_pairs={{0,1},{1,0},{2,3},{3,2},{4,5},{5,4},{6,7},{7,6},{8,9},{9,8},{10,11... | collective-permute-start | bytes 786440 | tf_op jit(solution)/shard_map/ppermute | solution.py:405
  50.3 20.6 %collective-permute-start.8 = (bf16[4,8,16,512]{3,2,1,0:T(8,128)(2,1)S(1)}, bf16[4,8,16,512]{3,2,1,0:T(8,128)(2,1)S(1)}, u32[]{:S(2)}, u32[]{:S(2)}) collective-permute-start(bf16[4,8,16,512]{3,2,1,0:T(8,128)(2,1)S(1)} %join.3.rest_1_.first_ref), channel_id=1, source_target_pairs={{0,4},{4,0},{8,12},{12,8},{16,20},{20,16},{24,28},{28,24},{1,5},{5... | collective-permute-start | bytes 1572872 | tf_op jit(solution)/shard_map/ppermute | solution.py:489
  52.2 17.7 %collective-permute-start.5 = (bf16[256,512]{1,0:T(8,128)(2,1)S(1)}, bf16[256,512]{1,0:T(8,128)(2,1)S(1)}, u32[]{:S(2)}, u32[]{:S(2)}) collective-permute-start(bf16[256,512]{1,0:T(8,128)(2,1)S(1)} %add.8.rest_0_.own_ref), channel_id=1, source_target_pairs={{0,2},{1,3},{2,0},{3,1},{4,6},{5,7},{6,4},{7,5},{8,10},{9,11},{10,... | collective-permute-start | bytes 786440 | tf_op jit(solution)/shard_map/ppermute | solution.py:405
  70.9 13.7 %collective-permute-start.9 = (bf16[1024,512]{1,0:T(8,128)(2,1)S(1)}, bf16[1024,512]{1,0:T(8,128)(2,1)S(1)}, u32[]{:S(2)}, u32[]{:S(2)}) collective-permute-start(bf16[1024,512]{1,0:T(8,128)(2,1)S(1)} %bitcast.21), channel_id=1, source_target_pairs={{0,1},{1,0},{2,3},{3,2},{4,5},{5,4},{6,7},{7,6},{8,9},{9,8},{10,11... | collective-permute-start | bytes 3145736 | tf_op jit(solution)/shard_map/ppermute | solution.py:405
  71.0 25.7 %all-to-all-start.2 = ((bf16[8,32,1536]{2,1,0:T(8,128)(2,1)}), bf16[8,32,1536]{2,1,0:T(8,128)(2,1)S(1)}, u32[]{:S(2)}, u32[]{:S(2)}) async-start(bf16[8,32,1536]{2,1,0:T(8,128)(2,1)} %bitcast.6), calls=%async_computation.2 | async-start | bytes 1572864 | tf_op jit(solution)/shard_map/all_to_all | solution.py:401
  76.2 8.5 %collective-permute-start.10 = (bf16[1024,128]{1,0:T(8,128)(2,1)S(1)}, bf16[1024,128]{1,0:T(8,128)(2,1)S(1)}, u32[]{:S(2)}, u32[]{:S(2)}) collective-permute-start(bf16[1024,128]{1,0:T(8,128)(2,1)S(1)} %bitcast.38), channel_id=1, source_target_pairs={{0,2},{1,3},{2,0},{3,1},{4,6},{5,7},{6,4},{7,5},{8,10},{9,11},{10,... | collective-permute-start | bytes 786440 | tf_op jit(solution)/shard_map/ppermute | solution.py:405
  85.4 11.4 %copy-start = (bf16[2,1,2,64,1024]{4,3,2,1,0:T(8,128)(2,1)S(1)}, bf16[2,1,2,64,1024]{4,3,2,1,0:T(8,128)(2,1)}, u32[]{:S(2)}) copy-start(bf16[2,1,2,64,1024]{4,3,2,1,0:T(8,128)(2,1)} %param.11) | copy-start | bytes 1572868
  85.4 7.7 %collective-permute-start.11 = (bf16[128,1024]{1,0:T(8,128)(2,1)S(1)}, bf16[128,1024]{1,0:T(8,128)(2,1)S(1)}, u32[]{:S(2)}, u32[]{:S(2)}) collective-permute-start(bf16[128,1024]{1,0:T(8,128)(2,1)S(1)} %get-tuple-element.36), channel_id=1, source_target_pairs={{0,2},{1,3},{2,0},{3,1},{4,6},{5,7},{6,4},{7,5},{8,10},{9,11},{10,... | collective-permute-start | bytes 786440 | tf_op jit(solution)/shard_map/ppermute | solution.py:405
  93.1 5.3 %copy-start.1 = (bf16[2,1,2,64,1024]{4,3,2,1,0:T(8,128)(2,1)S(1)}, bf16[2,1,2,64,1024]{4,3,2,1,0:T(8,128)(2,1)}, u32[]{:S(2)}) copy-start(bf16[2,1,2,64,1024]{4,3,2,1,0:T(8,128)(2,1)} %param.6) | copy-start | bytes 1572868
  93.1 5.3 %copy-start.3 = (f32[1,1024]{1,0:T(1,128)S(1)}, f32[1,1024]{1,0:T(1,128)}, u32[]{:S(2)}) copy-start(f32[1,1024]{1,0:T(1,128)} %gain_ref.3) | copy-start | bytes 12292
  93.2 6.2 %copy-start.2 = (f32[128,1024]{1,0:T(8,128)}, f32[128,1024]{1,0:T(8,128)S(1)}, u32[]{:S(2)}) copy-start(f32[128,1024]{1,0:T(8,128)S(1)} %convert_add_fusion._) | copy-start | bytes 1572868
  96.8 1.6 %collective-permute-start.12 = (bf16[8,32,512]{2,1,0:T(8,128)(2,1)S(1)}, bf16[8,32,512]{2,1,0:T(8,128)(2,1)S(1)}, u32[]{:S(2)}, u32[]{:S(2)}) collective-permute-start(bf16[8,32,512]{2,1,0:T(8,128)(2,1)S(1)} %cut_mixed.1.own_ref), channel_id=1, source_target_pairs={{0,1},{1,0},{2,3},{3,2},{4,5},{5,4},{6,7},{7,6},{8,9},{9,8},{10,11... | collective-permute-start | bytes 786440 | tf_op jit(solution)/shard_map/ppermute | solution.py:405

commit v2 on v0

--- a/solution.py
+++ b/solution.py
@@ -133,9 +133,9 @@
     return jnp.concatenate([jnp.where(lane == 0, tile, zero), jnp.where(lane == 1, tile, zero)], axis=0)
 
 
-def one_head(stacked, lane):
-    count = lane.shape[0]
-    return jnp.where(lane == 0, stacked[:count], stacked[count:])
+def own_rows(turned, head_width):
+    count = turned.shape[1] // 2
+    return [turned[:head_width, :count], turned[head_width:, count:]]
 
 
 def side_by_side(stacked):
@@ -190,18 +190,18 @@
     keep = keep_ref[...]
     keep = jnp.concatenate([keep, keep], axis=0)
     lane = lax.broadcasted_iota(jnp.int32, (count, 128), 1) // head_width
-    ones = jnp.ones((count, 128), BF16)
+    ones = by_head(jnp.ones((count, 128), BF16), lane)
     tiles = []
     for t in range(GROUP // 128):
         cols = slice(t * 128, (t + 1) * 128)
-        v_ones = jnp.concatenate([v[:, cols], ones], axis=1)
+        v_ones = jnp.concatenate([by_head(v[:, cols], lane), ones], axis=1)
         e = jnp.exp(nt(by_head(qn[:, cols] * score_scale, lane), kn[:, cols])) * keep
         e = e.astype(BF16)
         p_ref[t] = e
-        o = nn(e, v_ones)
+        o = nn(side_by_side(e), v_ones)
         inverse = 1.0 / o[:, 128:]
-        tiles.append(one_head(o[:, :128] * inverse, lane))
-        ri_ref[:, cols] = one_head(inverse, lane)
+        tiles.append(o[:, :128] * inverse)
+        ri_ref[:, cols] = inverse
     att = jnp.concatenate(tiles, axis=1).astype(BF16)
     features = att_ref.shape[-1]
     for f in range(GROUP // features):
@@ -291,13 +291,14 @@
         weighted = e_wide * d_p
         inner = jnp.sum(weighted, axis=-1, keepdims=True) * row_inverse
         d_s = (weighted - e_wide * inner).astype(BF16)
-        dq_tiles.append(one_head(nn(d_s, kn[:, cols]), lane) * score_scale)
-        dk_tiles.append(one_head(tn(side_by_side(d_s), qn[:, cols]), lane) * score_scale)
-        dv_tiles.append(one_head(tn(side_by_side(e), d_t), lane))
+        d_s = side_by_side(d_s)
+        dq_tiles.append(nn(d_s, by_head(kn[:, cols], lane)))
+        dk_tiles += own_rows(tn(qn[:, cols], d_s), head_width)
+        dv_tiles += own_rows(tn(d_t, side_by_side(e)), head_width)
     mean_mat = block_mean(head_width)
-    dq = jnp.concatenate(dq_tiles, axis=1)
-    dk = jnp.concatenate(dk_tiles, axis=1)
-    dv = jnp.concatenate(dv_tiles, axis=1).astype(BF16)
+    dq = jnp.concatenate(dq_tiles, axis=1) * score_scale
+    dk = jnp.concatenate(dk_tiles, axis=0).T * score_scale
+    dv = jnp.concatenate(dv_tiles, axis=0).T.astype(BF16)
 
     def through_norm(upstream, unit, factor):
         unit = unit.astype(F32)

time: 98.8 us -> 97.6 us (0.988)
  Pallas kernels: 31.4 us -> 30.2 us
    pallas_call x1, Pallas kernels: 15 us -> 13.8 us  [backward(): pl.pallas_call(backward_kernel, out_shape=jax.ShapeDtypeStruct((count, wi...]
  transfers between devices with their start and end apart: 17 -> 17, of which waited for: 9 -> 9; matrix products, arithmetic and copies ran while one was open for 0% -> 0% of each run, Pallas kernels for 28% -> 27%
where the time goes in v2:
time: 97.6 us; the launch traced here: 97.1 us
  starting transfers between devices  34 us (35%)
  waiting for transfers between devices  31.8 us (33%)
  Pallas kernels  30.2 us (31%)
    ppermute x10, waiting for transfers between devices, from_level(): lax.ppermute(block, 'lev', [(i, i ^ offset) for i in range(lax.axis_size(...  21.1 us
    all_to_all x4, starting transfers between devices, swap(): return lax.all_to_all(block, 'lat', split_axis=0, concat_axis=0, tiled=True)  20.6 us
    pallas_call x1, Pallas kernels, backward(): pl.pallas_call(backward_kernel, out_shape=jax.ShapeDtypeStruct((count, wi...  13.8 us
    pallas_call x1, Pallas kernels, forward(): pl.pallas_call(functools.partial(forward_kernel, samples, lat_count, chun...  9.67 us
    ppermute x3, starting transfers between devices, from_owner(): lax.ppermute(block, 'lat', [(i, i ^ offset) for i in range(lax.axis_size(...  6.81 us
    all_to_all x4, waiting for transfers between devices, swap(): return lax.all_to_all(block, 'lat', split_axis=0, concat_axis=0, tiled=True)  6.68 us
    ppermute x10, starting transfers between devices, from_level(): lax.ppermute(block, 'lev', [(i, i ^ offset) for i in range(lax.axis_size(...  6.55 us
    pallas_call x9, Pallas kernels, call(): pl.pallas_call(kernel, out_shape=out_shape, compiler_params=params(), nam...  5.15 us
  transfers between devices with their start and end apart: 17, of which 9 were waited for; matrix products, arithmetic and copies ran while one was open for 0% of the time, Pallas kernels for 27%

profile of v2, /device:TPU:0, one launch (start us, length us, event | category | flops | bytes accessed | tf_op | source)
XLA Modules:
  0.0 97.1 jit_solution(5080091051954717914)
XLA Ops:
  0.6 2.1 %pack.1 = (bf16[8,32,1024]{2,1,0:T(8,128)(2,1)}, bf16[8,32,512]{2,1,0:T(8,128)(2,1)S(1)}, bf16[8,32,512]{2,1,0:T(8,128)(2,1)S(1)}) custom-call(bf16[2,2,4,16,1024]{4,3,2,1,0:T(8,128)(2,1)} %bitcast.25, bf16[2,2,4,16,1024]{4,3,2,1,0:T(8,128)(2,1)} %bitcast.23, f32[1,1024]{1,0:T(1,128)} %gain_ref.3), custom_call_target="tpu_custom_call" | custom-call | tf_op jit(solution)/shard_map/pack/pallas_call | solution.py:54
  2.7 7.4 %all-to-all-start = ((bf16[8,32,1024]{2,1,0:T(8,128)(2,1)}), bf16[8,32,1024]{2,1,0:T(8,128)(2,1)S(1)}, u32[]{:S(2)}, u32[]{:S(2)}) async-start(bf16[8,32,1024]{2,1,0:T(8,128)(2,1)} %get-tuple-element.20), calls=%async_computation | async-start | bytes 1048576 | tf_op jit(solution)/shard_map/all_to_all | solution.py:397
  10.1 0.0 collective-permute-start
  10.1 1.5 %collective-permute-done.received_ref = bf16[8,32,512]{2,1,0:T(8,128)(2,1)S(1)} collective-permute-done((bf16[8,32,512]{2,1,0:T(8,128)(2,1)S(1)}, bf16[8,32,512]{2,1,0:T(8,128)(2,1)S(1)}, u32[]{:S(2)}, u32[]{:S(2)}) %collective-permute-start) | collective-permute-done | bytes 262176 | tf_op jit(solution)/shard_map/ppermute | solution.py:401
  11.6 0.1 split_rows.1
  11.7 1.6 %collective-permute-start.1 = (bf16[8,16,512]{2,1,0:T(8,128)(2,1)S(1)}, bf16[8,16,512]{2,1,0:T(8,128)(2,1)S(1)}, u32[]{:S(2)}, u32[]{:S(2)}) collective-permute-start(bf16[8,16,512]{2,1,0:T(8,128)(2,1)S(1)} %get-tuple-element.24.second_ref), channel_id=1, source_target_pairs={{0,2},{1,3},{2,0},{3,1},{4,6},{5,7},{6,4},{7,5},{8,10},{9,11},{10,... | collective-permute-start | bytes 393224 | tf_op jit(solution)/shard_map/ppermute | solution.py:401
  13.3 4.0 %collective-permute-done.1.received_ref = bf16[8,16,512]{2,1,0:T(8,128)(2,1)S(1)} collective-permute-done((bf16[8,16,512]{2,1,0:T(8,128)(2,1)S(1)}, bf16[8,16,512]{2,1,0:T(8,128)(2,1)S(1)}, u32[]{:S(2)}, u32[]{:S(2)}) %collective-permute-start.1) | collective-permute-done | bytes 131104 | tf_op jit(solution)/shard_map/ppermute | solution.py:401
  17.3 2.1 %collective-permute-start.3 = (bf16[1,8,16,512]{3,2,1,0:T(8,128)(2,1)S(1)}, bf16[1,8,16,512]{3,2,1,0:T(8,128)(2,1)S(1)}, u32[]{:S(2)}, u32[]{:S(2)}) collective-permute-start(bf16[1,8,16,512]{3,2,1,0:T(8,128)(2,1)S(1)} %bitcast.28), channel_id=1, source_target_pairs={{0,8},{4,12},{8,0},{12,4},{16,24},{20,28},{24,16},{28,20},{1,9},{5... | collective-permute-start | bytes 393224 | tf_op jit(solution)/shard_map/ppermute | solution.py:485
  19.4 1.5 %collective-permute-start.2 = (bf16[8,16,512]{2,1,0:T(8,128)(2,1)S(1)}, bf16[8,16,512]{2,1,0:T(8,128)(2,1)S(1)}, u32[]{:S(2)}, u32[]{:S(2)}) collective-permute-start(bf16[8,16,512]{2,1,0:T(8,128)(2,1)S(1)} %get-tuple-element.23.own_ref), channel_id=1, source_target_pairs={{0,2},{1,3},{2,0},{3,1},{4,6},{5,7},{6,4},{7,5},{8,10},{9,11},{10,... | collective-permute-start | bytes 393224 | tf_op jit(solution)/shard_map/ppermute | solution.py:401
  20.9 3.9 %collective-permute-done.3.second_ref = bf16[1,8,16,512]{3,2,1,0:T(8,128)(2,1)S(1)} collective-permute-done((bf16[1,8,16,512]{3,2,1,0:T(8,128)(2,1)S(1)}, bf16[1,8,16,512]{3,2,1,0:T(8,128)(2,1)S(1)}, u32[]{:S(2)}, u32[]{:S(2)}) %collective-permute-start.3) | collective-permute-done | bytes 131104 | tf_op jit(solution)/shard_map/ppermute | solution.py:485
  24.8 0.0 collective-permute-done.2.received_ref
  24.8 0.0 all-to-all-done
  24.8 0.8 add_flow.1._
  25.6 4.8 %all-to-all-start.1 = ((bf16[8,32,512]{2,1,0:T(8,128)(2,1)}), bf16[8,32,512]{2,1,0:T(8,128)(2,1)S(1)}, u32[]{:S(2)}, u32[]{:S(2)}) async-start(bf16[8,32,512]{2,1,0:T(8,128)(2,1)} %add_flow.1._), calls=%async_computation.1 | async-start | bytes 524288 | tf_op jit(solution)/shard_map/all_to_all | solution.py:397
  30.4 2.9 %collective-permute-start.7 = (bf16[2,8,16,512]{3,2,1,0:T(8,128)(2,1)S(1)}, bf16[2,8,16,512]{3,2,1,0:T(8,128)(2,1)S(1)}, u32[]{:S(2)}, u32[]{:S(2)}) collective-permute-start(bf16[2,8,16,512]{3,2,1,0:T(8,128)(2,1)S(1)} %join.2.__.first_ref), channel_id=1, source_target_pairs={{0,16},{4,20},{8,24},{12,28},{16,0},{20,4},{24,8},{28,12},{1,17},{... | collective-permute-start | bytes 786440 | tf_op jit(solution)/shard_map/ppermute | solution.py:485
  33.3 9.7 %forward.1 = (bf16[256,1024]{1,0:T(8,128)(2,1)}, bf16[256,1024]{1,0:T(8,128)(2,1)}, bf16[256,1024]{1,0:T(8,128)(2,1)}, bf16[256,1024]{1,0:T(8,128)(2,1)}, bf16[2...) custom-call(bf16[256,1024]{1,0:T(8,128)(2,1)S(1)} %bitcast.19, ...), custom_call_target="tpu_custom_call" | custom-call | flops 3221225472 | bytes 13631488 | tf_op jit(solution)/shard_map/forward/pallas_call | solution.py:225
  43.0 3.1 %all-to-all-done.1 = bf16[8,32,512]{2,1,0:T(8,128)(2,1)S(1)} async-done(((bf16[8,32,512]{2,1,0:T(8,128)(2,1)}), bf16[8,32,512]{2,1,0:T(8,128)(2,1)S(1)}, u32[]{:S(2)}, u32[]{:S(2)}) %all-to-all-start.1) | async-done | bytes 262176 | tf_op jit(solution)/shard_map/all_to_all | solution.py:397
  46.1 3.5 %all-to-all-start.3 = ((bf16[8,256,128]{2,1,0:T(8,128)(2,1)}), bf16[8,256,128]{2,1,0:T(8,128)(2,1)S(1)}, u32[]{:S(2)}, u32[]{:S(2)}) async-start(bf16[8,256,128]{2,1,0:T(8,128)(2,1)} %get-tuple-element.34), calls=%async_computation.3 | async-start | bytes 1048576 | tf_op jit(solution)/shard_map/all_to_all | solution.py:397
  49.6 0.1 collective-permute-start.4
  49.6 0.5 collective-permute-start.6
  50.1 0.1 collective-permute-done.7.second_ref
  50.3 1.8 %collective-permute-start.8 = (bf16[4,8,16,512]{3,2,1,0:T(8,128)(2,1)S(1)}, bf16[4,8,16,512]{3,2,1,0:T(8,128)(2,1)S(1)}, u32[]{:S(2)}, u32[]{:S(2)}) collective-permute-start(bf16[4,8,16,512]{3,2,1,0:T(8,128)(2,1)S(1)} %join.3.rest_1_.first_ref), channel_id=1, source_target_pairs={{0,4},{4,0},{8,12},{12,8},{16,20},{20,16},{24,28},{28,24},{1,5},{5... | collective-permute-start | bytes 1572872 | tf_op jit(solution)/shard_map/ppermute | solution.py:485
  52.1 0.0 collective-permute-done.4.received_ref
  52.1 0.1 add.8.rest_0_.own_ref
  52.2 1.6 %collective-permute-start.5 = (bf16[256,512]{1,0:T(8,128)(2,1)S(1)}, bf16[256,512]{1,0:T(8,128)(2,1)S(1)}, u32[]{:S(2)}, u32[]{:S(2)}) collective-permute-start(bf16[256,512]{1,0:T(8,128)(2,1)S(1)} %add.8.rest_0_.own_ref), channel_id=1, source_target_pairs={{0,2},{1,3},{2,0},{3,1},{4,6},{5,7},{6,4},{7,5},{8,10},{9,11},{10,... | collective-permute-start | bytes 786440 | tf_op jit(solution)/shard_map/ppermute | solution.py:401
  53.8 0.0 collective-permute-done.6.other_ref
  53.8 13.8 %backward.1.back_ref = bf16[256,1024]{1,0:T(8,128)(2,1)S(1)} custom-call(bf16[256,1024]{1,0:T(8,128)(2,1)S(1)} %bitcast.20, bf16[256,512]{1,0:T(8,128)(2,1)S(1)} %bitcast.31, bf16[256,512]{1,0:T(8,128)(2,1)S(1)} %collective-permute-done.6.other_ref, bf16[1024,1024]{1,0:T(8,128)(2,1)} %bitcast.34, bf16[1024,3072]{1,0:T(8,128)(2,1)} %wv_ref.3, ...), custom_call_target="tpu_custom_call" | custom-call | flops 4294967296 | bytes 13631488 | tf_op jit(solution)/shard_map/backward/pallas_call | solution.py:335
  67.6 0.0 collective-permute-done.5.received_ref
  67.6 1.0 %add_mixed.1._ = bf16[256,1536]{1,0:T(8,128)(2,1)} custom-call(bf16[256,512]{1,0:T(8,128)(2,1)S(1)} %add.8.rest_0_.own_ref, bf16[256,512]{1,0:T(8,128)(2,1)S(1)} %collective-permute-done.5.received_ref, bf16[256,1024]{1,0:T(8,128)(2,1)S(1)} %backward.1.back_ref), custom_call_target="tpu_custom_call" | custom-call | tf_op jit(solution)/shard_map/add_mixed/pallas_call | solution.py:54
  68.6 0.0 collective-permute-done.8.second_ref
  68.6 0.1 arrange.1
  68.7 0.1 collective-permute-start.9
  68.7 0.0 all-to-all-done.3
  68.7 4.9 %all-to-all-start.2 = ((bf16[8,32,1536]{2,1,0:T(8,128)(2,1)}), bf16[8,32,1536]{2,1,0:T(8,128)(2,1)S(1)}, u32[]{:S(2)}, u32[]{:S(2)}) async-start(bf16[8,32,1536]{2,1,0:T(8,128)(2,1)} %bitcast.6), calls=%async_computation.2 | async-start | bytes 1572864 | tf_op jit(solution)/shard_map/all_to_all | solution.py:397
  73.7 0.2 constant_dynamic-slice_fusion
  73.9 0.6 collective-permute-start.10
  74.5 7.9 %collective-permute-done.10.refs_1_ = bf16[1024,128]{1,0:T(8,128)(2,1)S(1)} collective-permute-done((bf16[1024,128]{1,0:T(8,128)(2,1)S(1)}, bf16[1024,128]{1,0:T(8,128)(2,1)S(1)}, u32[]{:S(2)}, u32[]{:S(2)}) %collective-permute-start.10) | collective-permute-done | bytes 262176 | tf_op jit(solution)/shard_map/ppermute | solution.py:401
  82.4 0.7 mix_gradient.1
  83.1 0.0 copy-start
  83.1 0.6 collective-permute-start.11
  83.7 7.1 %collective-permute-done.11 = bf16[128,1024]{1,0:T(8,128)(2,1)S(1)} collective-permute-done((bf16[128,1024]{1,0:T(8,128)(2,1)S(1)}, bf16[128,1024]{1,0:T(8,128)(2,1)S(1)}, u32[]{:S(2)}, u32[]{:S(2)}) %collective-permute-start.11) | collective-permute-done | bytes 262176 | tf_op jit(solution)/shard_map/ppermute | solution.py:401
  90.8 0.1 convert_add_fusion._
  90.9 0.0 copy-start.2
  90.9 3.6 %all-to-all-done.2.in_ref.back_ref = bf16[8,32,1536]{2,1,0:T(8,128)(2,1)S(1)} async-done(((bf16[8,32,1536]{2,1,0:T(8,128)(2,1)}), bf16[8,32,1536]{2,1,0:T(8,128)(2,1)S(1)}, u32[]{:S(2)}, u32[]{:S(2)}) %all-to-all-start.2) | async-done | bytes 786464 | tf_op jit(solution)/shard_map/all_to_all | solution.py:397
  94.5 0.1 collective-permute-start.12
  94.6 0.9 make_gradient.1
  95.5 0.6 collective-permute-done.12.other_ref
  96.1 1.0 make_output.1
  (13 shorter events, 0.1 us)
Async XLA Ops:
  2.7 30.6 %copy-start.4 = (s32[2,16]{1,0:T(2,128)S(1)}, s32[2,16]{1,0:T(2,128)}, u32[]{:S(2)}) copy-start(s32[2,16]{1,0:T(2,128)} %mask_ref.1) | copy-start | bytes 388
  2.7 22.1 %all-to-all-start = ((bf16[8,32,1024]{2,1,0:T(8,128)(2,1)}), bf16[8,32,1024]{2,1,0:T(8,128)(2,1)S(1)}, u32[]{:S(2)}, u32[]{:S(2)}) async-start(bf16[8,32,1024]{2,1,0:T(8,128)(2,1)} %get-tuple-element.20), calls=%async_computation | async-start | bytes 1048576 | tf_op jit(solution)/shard_map/all_to_all | solution.py:397
  10.1 1.5 %collective-permute-start = (bf16[8,32,512]{2,1,0:T(8,128)(2,1)S(1)}, bf16[8,32,512]{2,1,0:T(8,128)(2,1)S(1)}, u32[]{:S(2)}, u32[]{:S(2)}) collective-permute-start(bf16[8,32,512]{2,1,0:T(8,128)(2,1)S(1)} %get-tuple-element.22), channel_id=1, source_target_pairs={{0,1},{1,0},{2,3},{3,2},{4,5},{5,4},{6,7},{7,6},{8,9},{9,8},{10,11... | collective-permute-start | bytes 786440 | tf_op jit(solution)/shard_map/ppermute | solution.py:401
  11.7 5.6 %collective-permute-start.1 = (bf16[8,16,512]{2,1,0:T(8,128)(2,1)S(1)}, bf16[8,16,512]{2,1,0:T(8,128)(2,1)S(1)}, u32[]{:S(2)}, u32[]{:S(2)}) collective-permute-start(bf16[8,16,512]{2,1,0:T(8,128)(2,1)S(1)} %get-tuple-element.24.second_ref), channel_id=1, source_target_pairs={{0,2},{1,3},{2,0},{3,1},{4,6},{5,7},{6,4},{7,5},{8,10},{9,11},{10,... | collective-permute-start | bytes 393224 | tf_op jit(solution)/shard_map/ppermute | solution.py:401
  17.3 7.5 %collective-permute-start.3 = (bf16[1,8,16,512]{3,2,1,0:T(8,128)(2,1)S(1)}, bf16[1,8,16,512]{3,2,1,0:T(8,128)(2,1)S(1)}, u32[]{:S(2)}, u32[]{:S(2)}) collective-permute-start(bf16[1,8,16,512]{3,2,1,0:T(8,128)(2,1)S(1)} %bitcast.28), channel_id=1, source_target_pairs={{0,8},{4,12},{8,0},{12,4},{16,24},{20,28},{24,16},{28,20},{1,9},{5... | collective-permute-start | bytes 393224 | tf_op jit(solution)/shard_map/ppermute | solution.py:485
  19.4 5.4 %collective-permute-start.2 = (bf16[8,16,512]{2,1,0:T(8,128)(2,1)S(1)}, bf16[8,16,512]{2,1,0:T(8,128)(2,1)S(1)}, u32[]{:S(2)}, u32[]{:S(2)}) collective-permute-start(bf16[8,16,512]{2,1,0:T(8,128)(2,1)S(1)} %get-tuple-element.23.own_ref), channel_id=1, source_target_pairs={{0,2},{1,3},{2,0},{3,1},{4,6},{5,7},{6,4},{7,5},{8,10},{9,11},{10,... | collective-permute-start | bytes 393224 | tf_op jit(solution)/shard_map/ppermute | solution.py:401
  25.6 20.5 %all-to-all-start.1 = ((bf16[8,32,512]{2,1,0:T(8,128)(2,1)}), bf16[8,32,512]{2,1,0:T(8,128)(2,1)S(1)}, u32[]{:S(2)}, u32[]{:S(2)}) async-start(bf16[8,32,512]{2,1,0:T(8,128)(2,1)} %add_flow.1._), calls=%async_computation.1 | async-start | bytes 524288 | tf_op jit(solution)/shard_map/all_to_all | solution.py:397
  30.4 19.9 %collective-permute-start.7 = (bf16[2,8,16,512]{3,2,1,0:T(8,128)(2,1)S(1)}, bf16[2,8,16,512]{3,2,1,0:T(8,128)(2,1)S(1)}, u32[]{:S(2)}, u32[]{:S(2)}) collective-permute-start(bf16[2,8,16,512]{3,2,1,0:T(8,128)(2,1)S(1)} %join.2.__.first_ref), channel_id=1, source_target_pairs={{0,16},{4,20},{8,24},{12,28},{16,0},{20,4},{24,8},{28,12},{1,17},{... | collective-permute-start | bytes 786440 | tf_op jit(solution)/shard_map/ppermute | solution.py:485
  46.1 22.7 %all-to-all-start.3 = ((bf16[8,256,128]{2,1,0:T(8,128)(2,1)}), bf16[8,256,128]{2,1,0:T(8,128)(2,1)S(1)}, u32[]{:S(2)}, u32[]{:S(2)}) async-start(bf16[8,256,128]{2,1,0:T(8,128)(2,1)} %get-tuple-element.34), calls=%async_computation.3 | async-start | bytes 1048576 | tf_op jit(solution)/shard_map/all_to_all | solution.py:397
  49.6 2.5 %collective-permute-start.4 = (bf16[256,512]{1,0:T(8,128)(2,1)S(1)}, bf16[256,512]{1,0:T(8,128)(2,1)S(1)}, u32[]{:S(2)}, u32[]{:S(2)}) collective-permute-start(bf16[256,512]{1,0:T(8,128)(2,1)S(1)} %get-tuple-element.26), channel_id=1, source_target_pairs={{0,1},{1,0},{2,3},{3,2},{4,5},{5,4},{6,7},{7,6},{8,9},{9,8},{10,11... | collective-permute-start | bytes 786440 | tf_op jit(solution)/shard_map/ppermute | solution.py:401
  49.6 4.1 %collective-permute-start.6 = (bf16[256,512]{1,0:T(8,128)(2,1)S(1)}, bf16[256,512]{1,0:T(8,128)(2,1)S(1)}, u32[]{:S(2)}, u32[]{:S(2)}) collective-permute-start(bf16[256,512]{1,0:T(8,128)(2,1)S(1)} %bitcast.30), channel_id=1, source_target_pairs={{0,1},{1,0},{2,3},{3,2},{4,5},{5,4},{6,7},{7,6},{8,9},{9,8},{10,11... | collective-permute-start | bytes 786440 | tf_op jit(solution)/shard_map/ppermute | solution.py:401
  50.3 18.3 %collective-permute-start.8 = (bf16[4,8,16,512]{3,2,1,0:T(8,128)(2,1)S(1)}, bf16[4,8,16,512]{3,2,1,0:T(8,128)(2,1)S(1)}, u32[]{:S(2)}, u32[]{:S(2)}) collective-permute-start(bf16[4,8,16,512]{3,2,1,0:T(8,128)(2,1)S(1)} %join.3.rest_1_.first_ref), channel_id=1, source_target_pairs={{0,4},{4,0},{8,12},{12,8},{16,20},{20,16},{24,28},{28,24},{1,5},{5... | collective-permute-start | bytes 1572872 | tf_op jit(solution)/shard_map/ppermute | solution.py:485
  52.2 15.4 %collective-permute-start.5 = (bf16[256,512]{1,0:T(8,128)(2,1)S(1)}, bf16[256,512]{1,0:T(8,128)(2,1)S(1)}, u32[]{:S(2)}, u32[]{:S(2)}) collective-permute-start(bf16[256,512]{1,0:T(8,128)(2,1)S(1)} %add.8.rest_0_.own_ref), channel_id=1, source_target_pairs={{0,2},{1,3},{2,0},{3,1},{4,6},{5,7},{6,4},{7,5},{8,10},{9,11},{10,... | collective-permute-start | bytes 786440 | tf_op jit(solution)/shard_map/ppermute | solution.py:401
  68.7 13.7 %collective-permute-start.9 = (bf16[1024,512]{1,0:T(8,128)(2,1)S(1)}, bf16[1024,512]{1,0:T(8,128)(2,1)S(1)}, u32[]{:S(2)}, u32[]{:S(2)}) collective-permute-start(bf16[1024,512]{1,0:T(8,128)(2,1)S(1)} %bitcast.21), channel_id=1, source_target_pairs={{0,1},{1,0},{2,3},{3,2},{4,5},{5,4},{6,7},{7,6},{8,9},{9,8},{10,11... | collective-permute-start | bytes 3145736 | tf_op jit(solution)/shard_map/ppermute | solution.py:401
  68.7 25.7 %all-to-all-start.2 = ((bf16[8,32,1536]{2,1,0:T(8,128)(2,1)}), bf16[8,32,1536]{2,1,0:T(8,128)(2,1)S(1)}, u32[]{:S(2)}, u32[]{:S(2)}) async-start(bf16[8,32,1536]{2,1,0:T(8,128)(2,1)} %bitcast.6), calls=%async_computation.2 | async-start | bytes 1572864 | tf_op jit(solution)/shard_map/all_to_all | solution.py:397
  73.9 8.5 %collective-permute-start.10 = (bf16[1024,128]{1,0:T(8,128)(2,1)S(1)}, bf16[1024,128]{1,0:T(8,128)(2,1)S(1)}, u32[]{:S(2)}, u32[]{:S(2)}) collective-permute-start(bf16[1024,128]{1,0:T(8,128)(2,1)S(1)} %bitcast.38), channel_id=1, source_target_pairs={{0,2},{1,3},{2,0},{3,1},{4,6},{5,7},{6,4},{7,5},{8,10},{9,11},{10,... | collective-permute-start | bytes 786440 | tf_op jit(solution)/shard_map/ppermute | solution.py:401
  83.1 11.4 %copy-start = (bf16[2,1,2,64,1024]{4,3,2,1,0:T(8,128)(2,1)S(1)}, bf16[2,1,2,64,1024]{4,3,2,1,0:T(8,128)(2,1)}, u32[]{:S(2)}) copy-start(bf16[2,1,2,64,1024]{4,3,2,1,0:T(8,128)(2,1)} %param.11) | copy-start | bytes 1572868
  83.1 7.7 %collective-permute-start.11 = (bf16[128,1024]{1,0:T(8,128)(2,1)S(1)}, bf16[128,1024]{1,0:T(8,128)(2,1)S(1)}, u32[]{:S(2)}, u32[]{:S(2)}) collective-permute-start(bf16[128,1024]{1,0:T(8,128)(2,1)S(1)} %get-tuple-element.36), channel_id=1, source_target_pairs={{0,2},{1,3},{2,0},{3,1},{4,6},{5,7},{6,4},{7,5},{8,10},{9,11},{10,... | collective-permute-start | bytes 786440 | tf_op jit(solution)/shard_map/ppermute | solution.py:401
  90.8 5.3 %copy-start.1 = (bf16[2,1,2,64,1024]{4,3,2,1,0:T(8,128)(2,1)S(1)}, bf16[2,1,2,64,1024]{4,3,2,1,0:T(8,128)(2,1)}, u32[]{:S(2)}) copy-start(bf16[2,1,2,64,1024]{4,3,2,1,0:T(8,128)(2,1)} %param.6) | copy-start | bytes 1572868
  90.8 5.3 %copy-start.3 = (f32[1,1024]{1,0:T(1,128)S(1)}, f32[1,1024]{1,0:T(1,128)}, u32[]{:S(2)}) copy-start(f32[1,1024]{1,0:T(1,128)} %gain_ref.3) | copy-start | bytes 12292
  90.9 6.2 %copy-start.2 = (f32[128,1024]{1,0:T(8,128)}, f32[128,1024]{1,0:T(8,128)S(1)}, u32[]{:S(2)}) copy-start(f32[128,1024]{1,0:T(8,128)S(1)} %convert_add_fusion._) | copy-start | bytes 1572868
  94.5 1.6 %collective-permute-start.12 = (bf16[8,32,512]{2,1,0:T(8,128)(2,1)S(1)}, bf16[8,32,512]{2,1,0:T(8,128)(2,1)S(1)}, u32[]{:S(2)}, u32[]{:S(2)}) collective-permute-start(bf16[8,32,512]{2,1,0:T(8,128)(2,1)S(1)} %cut_mixed.1.own_ref), channel_id=1, source_target_pairs={{0,1},{1,0},{2,3},{3,2},{4,5},{5,4},{6,7},{7,6},{8,9},{9,8},{10,11... | collective-permute-start | bytes 786440 | tf_op jit(solution)/shard_map/ppermute | solution.py:401

commit v3 on v2

--- a/solution.py
+++ b/solution.py
@@ -146,7 +146,7 @@
 def forward_kernel(
     samples, lat_count, chunk, owners,
     tok_ref, mask_ref, wq_ref, wk_ref, wv_ref, wm_ref, _,
-    qn_ref, kn_ref, v_ref, rq_ref, rk_ref, ri_ref, p_ref, att_ref, own_ref, other_ref,
+    qn_ref, kn_ref, v_ref, rq_ref, rk_ref, at_ref, ri_ref, p_ref, att_ref, own_ref, other_ref,
     normed_ref, acc_ref, keep_ref,
 ):
     step = pl.program_id(0)
@@ -203,6 +203,7 @@
         tiles.append(o[:, :128] * inverse)
         ri_ref[:, cols] = inverse
     att = jnp.concatenate(tiles, axis=1).astype(BF16)
+    at_ref[...] = att
     features = att_ref.shape[-1]
     for f in range(GROUP // features):
         att_ref[f] = att[:, f * features : (f + 1) * features]
@@ -225,7 +226,7 @@
     return pl.pallas_call(
         functools.partial(forward_kernel, samples, lat_count, chunk, owners),
         out_shape=(
-            [pltpu.HBM((count, width), BF16)] * 5
+            [pltpu.HBM((count, width), BF16)] * 6
             + [pltpu.HBM((count, width), F32)]
             + [pltpu.HBM((width // 128, 2 * count, count), BF16)]
             + [jax.ShapeDtypeStruct((owners, count, features), BF16)]
@@ -242,7 +243,7 @@
             pl.BlockSpec(memory_space=pl.ANY),
         ],
         out_specs=(
-            [cols] * 6
+            [cols] * 7
             + [pl.BlockSpec((GROUP // 128, 2 * count, count), lambda i: (i, 0, 0))]
             + [pl.BlockSpec((GROUP // features, count, features), lambda i: (i, 0, 0))]
             + [same((count, width // 2))] * 2
@@ -264,7 +265,7 @@
 
 def backward_kernel(
     tok_ref, own_ref, other_ref, wm_ref, wq_ref, wk_ref, wv_ref,
-    qn_ref, kn_ref, v_ref, rq_ref, rk_ref, ri_ref, p_ref, *rest,
+    qn_ref, kn_ref, v_ref, rq_ref, rk_ref, at_ref, ri_ref, p_ref, *rest,
 ):
     out_ref, acc_ref = rest[-2:]
     step = pl.program_id(0)
@@ -274,6 +275,11 @@
     d_att += nt(other_ref[...], wm_ref[:, half_cols(1, width)])
     inverse = ri_ref[...]
     d_att = (d_att * inverse).astype(BF16)
+    mean_mat = block_mean(head_width)
+    product = d_att.astype(F32) * at_ref[...].astype(F32)
+    coarse = product.astype(BF16)
+    rest_of = (product - coarse.astype(F32)).astype(BF16)
+    inner_all = (nn(coarse, mean_mat) + nn(rest_of, mean_mat)) * float(head_width)
     qn, kn, v = qn_ref[...], kn_ref[...], v_ref[...]
     lane = lax.broadcasted_iota(jnp.int32, (count, 128), 1) // head_width
     dq_tiles, dk_tiles, dv_tiles = [], [], []
@@ -285,17 +291,14 @@
         e_wide = e.astype(F32)
         first = t * 128
         second = first + head_width
-        row_inverse = jnp.concatenate(
-            [inverse[:, first : first + 1], inverse[:, second : second + 1]], axis=0
+        inner = jnp.concatenate(
+            [inner_all[:, first : first + 1], inner_all[:, second : second + 1]], axis=0
         )
-        weighted = e_wide * d_p
-        inner = jnp.sum(weighted, axis=-1, keepdims=True) * row_inverse
-        d_s = (weighted - e_wide * inner).astype(BF16)
+        d_s = (e_wide * (d_p - inner)).astype(BF16)
         d_s = side_by_side(d_s)
         dq_tiles.append(nn(d_s, by_head(kn[:, cols], lane)))
         dk_tiles += own_rows(tn(qn[:, cols], d_s), head_width)
         dv_tiles += own_rows(tn(d_t, side_by_side(e)), head_width)
-    mean_mat = block_mean(head_width)
     dq = jnp.concatenate(dq_tiles, axis=1) * score_scale
     dk = jnp.concatenate(dk_tiles, axis=0).T * score_scale
     dv = jnp.concatenate(dv_tiles, axis=0).T.astype(BF16)
@@ -344,7 +347,7 @@
             weight(0),
             weight(1),
             weight(2),
-            *([cols] * 6),
+            *([cols] * 7),
             pl.BlockSpec((GROUP // 128, 2 * count, count), lambda i: (i, 0, 0)),
         ]
         + [pl.BlockSpec(memory_space=pl.ANY)] * len(after),

time: 97.6 us -> 96.5 us (0.989)
  Pallas kernels: 30.2 us -> 27.8 us
  starting transfers between devices: 34 us -> 35.4 us
    pallas_call x1, Pallas kernels: 13.8 us -> 11.3 us  [backward(): pl.pallas_call(backward_kernel, out_shape=jax.ShapeDtypeStruct((count, wi...]
    ppermute x10, waiting for transfers between devices: 21.1 us -> 19.1 us  [from_level(): lax.ppermute(block, 'lev', [(i, i ^ offset) for i in range(lax.axis_size(...]
    ppermute x10, starting transfers between devices: 6.55 us -> 8.57 us  [from_level(): lax.ppermute(block, 'lev', [(i, i ^ offset) for i in range(lax.axis_size(...]
    ppermute x3, waiting for transfers between devices: 3.98 us -> 5.94 us  [from_owner(): lax.ppermute(block, 'lat', [(i, i ^ offset) for i in range(lax.axis_size(...]
  transfers between devices with their start and end apart: 17 -> 17, of which waited for: 9 -> 10; matrix products, arithmetic and copies ran while one was open for 0% -> 0% of each run, Pallas kernels for 27% -> 25%
where the time goes in v3:
time: 96.5 us; the launch traced here: 95.9 us
  starting transfers between devices  35.4 us (37%)
  waiting for transfers between devices  31.6 us (33%)
  Pallas kernels  27.8 us (29%)
    all_to_all x4, starting transfers between devices, swap(): return lax.all_to_all(block, 'lat', split_axis=0, concat_axis=0, tiled=True)  20 us
    ppermute x10, waiting for transfers between devices, from_level(): lax.ppermute(block, 'lev', [(i, i ^ offset) for i in range(lax.axis_size(...  19.1 us
    pallas_call x1, Pallas kernels, backward(): pl.pallas_call(backward_kernel, out_shape=jax.ShapeDtypeStruct((count, wi...  11.3 us
    pallas_call x1, Pallas kernels, forward(): pl.pallas_call(functools.partial(forward_kernel, samples, lat_count, chun...  9.76 us
    ppermute x10, starting transfers between devices, from_level(): lax.ppermute(block, 'lev', [(i, i ^ offset) for i in range(lax.axis_size(...  8.57 us
    ppermute x3, starting transfers between devices, from_owner(): lax.ppermute(block, 'lat', [(i, i ^ offset) for i in range(lax.axis_size(...  6.81 us
    all_to_all x4, waiting for transfers between devices, swap(): return lax.all_to_all(block, 'lat', split_axis=0, concat_axis=0, tiled=True)  6.59 us
    ppermute x3, waiting for transfers between devices, from_owner(): lax.ppermute(block, 'lat', [(i, i ^ offset) for i in range(lax.axis_size(...  5.94 us
  transfers between devices with their start and end apart: 17, of which 10 were waited for; matrix products, arithmetic and copies ran while one was open for 0% of the time, Pallas kernels for 25%

profile of v3, /device:TPU:0, one launch (start us, length us, event | category | flops | bytes accessed | tf_op | source)
XLA Modules:
  0.0 95.9 jit_solution(1705439520844471951)
XLA Ops:
  0.6 2.1 %pack.1 = (bf16[8,32,1024]{2,1,0:T(8,128)(2,1)}, bf16[8,32,512]{2,1,0:T(8,128)(2,1)S(1)}, bf16[8,32,512]{2,1,0:T(8,128)(2,1)S(1)}) custom-call(bf16[2,2,4,16,1024]{4,3,2,1,0:T(8,128)(2,1)} %bitcast.25, bf16[2,2,4,16,1024]{4,3,2,1,0:T(8,128)(2,1)} %bitcast.23, f32[1,1024]{1,0:T(1,128)} %gain_ref.3), custom_call_target="tpu_custom_call" | custom-call | tf_op jit(solution)/shard_map/pack/pallas_call | solution.py:54
  2.7 7.4 %all-to-all-start = ((bf16[8,32,1024]{2,1,0:T(8,128)(2,1)}), bf16[8,32,1024]{2,1,0:T(8,128)(2,1)S(1)}, u32[]{:S(2)}, u32[]{:S(2)}) async-start(bf16[8,32,1024]{2,1,0:T(8,128)(2,1)} %get-tuple-element.21), calls=%async_computation | async-start | bytes 1048576 | tf_op jit(solution)/shard_map/all_to_all | solution.py:400
  10.1 0.0 collective-permute-start
  10.1 1.5 %collective-permute-done.received_ref = bf16[8,32,512]{2,1,0:T(8,128)(2,1)S(1)} collective-permute-done((bf16[8,32,512]{2,1,0:T(8,128)(2,1)S(1)}, bf16[8,32,512]{2,1,0:T(8,128)(2,1)S(1)}, u32[]{:S(2)}, u32[]{:S(2)}) %collective-permute-start) | collective-permute-done | bytes 262176 | tf_op jit(solution)/shard_map/ppermute | solution.py:404
  11.6 0.1 split_rows.1
  11.7 1.6 %collective-permute-start.1 = (bf16[8,16,512]{2,1,0:T(8,128)(2,1)S(1)}, bf16[8,16,512]{2,1,0:T(8,128)(2,1)S(1)}, u32[]{:S(2)}, u32[]{:S(2)}) collective-permute-start(bf16[8,16,512]{2,1,0:T(8,128)(2,1)S(1)} %get-tuple-element.25.second_ref), channel_id=1, source_target_pairs={{0,2},{1,3},{2,0},{3,1},{4,6},{5,7},{6,4},{7,5},{8,10},{9,11},{10,... | collective-permute-start | bytes 393224 | tf_op jit(solution)/shard_map/ppermute | solution.py:404
  13.3 4.0 %collective-permute-done.1.received_ref = bf16[8,16,512]{2,1,0:T(8,128)(2,1)S(1)} collective-permute-done((bf16[8,16,512]{2,1,0:T(8,128)(2,1)S(1)}, bf16[8,16,512]{2,1,0:T(8,128)(2,1)S(1)}, u32[]{:S(2)}, u32[]{:S(2)}) %collective-permute-start.1) | collective-permute-done | bytes 131104 | tf_op jit(solution)/shard_map/ppermute | solution.py:404
  17.3 2.1 %collective-permute-start.3 = (bf16[1,8,16,512]{3,2,1,0:T(8,128)(2,1)S(1)}, bf16[1,8,16,512]{3,2,1,0:T(8,128)(2,1)S(1)}, u32[]{:S(2)}, u32[]{:S(2)}) collective-permute-start(bf16[1,8,16,512]{3,2,1,0:T(8,128)(2,1)S(1)} %bitcast.28), channel_id=1, source_target_pairs={{0,8},{4,12},{8,0},{12,4},{16,24},{20,28},{24,16},{28,20},{1,9},{5... | collective-permute-start | bytes 393224 | tf_op jit(solution)/shard_map/ppermute | solution.py:488
  19.4 1.5 %collective-permute-start.2 = (bf16[8,16,512]{2,1,0:T(8,128)(2,1)S(1)}, bf16[8,16,512]{2,1,0:T(8,128)(2,1)S(1)}, u32[]{:S(2)}, u32[]{:S(2)}) collective-permute-start(bf16[8,16,512]{2,1,0:T(8,128)(2,1)S(1)} %get-tuple-element.24.own_ref), channel_id=1, source_target_pairs={{0,2},{1,3},{2,0},{3,1},{4,6},{5,7},{6,4},{7,5},{8,10},{9,11},{10,... | collective-permute-start | bytes 393224 | tf_op jit(solution)/shard_map/ppermute | solution.py:404
  20.9 3.9 %collective-permute-done.3.second_ref = bf16[1,8,16,512]{3,2,1,0:T(8,128)(2,1)S(1)} collective-permute-done((bf16[1,8,16,512]{3,2,1,0:T(8,128)(2,1)S(1)}, bf16[1,8,16,512]{3,2,1,0:T(8,128)(2,1)S(1)}, u32[]{:S(2)}, u32[]{:S(2)}) %collective-permute-start.3) | collective-permute-done | bytes 131104 | tf_op jit(solution)/shard_map/ppermute | solution.py:488
  24.8 0.0 collective-permute-done.2.received_ref
  24.8 0.0 all-to-all-done
  24.8 0.8 add_flow.1._
  25.6 4.8 %all-to-all-start.1 = ((bf16[8,32,512]{2,1,0:T(8,128)(2,1)}), bf16[8,32,512]{2,1,0:T(8,128)(2,1)S(1)}, u32[]{:S(2)}, u32[]{:S(2)}) async-start(bf16[8,32,512]{2,1,0:T(8,128)(2,1)} %add_flow.1._), calls=%async_computation.1 | async-start | bytes 524288 | tf_op jit(solution)/shard_map/all_to_all | solution.py:400
  30.4 2.9 %collective-permute-start.7 = (bf16[2,8,16,512]{3,2,1,0:T(8,128)(2,1)S(1)}, bf16[2,8,16,512]{3,2,1,0:T(8,128)(2,1)S(1)}, u32[]{:S(2)}, u32[]{:S(2)}) collective-permute-start(bf16[2,8,16,512]{3,2,1,0:T(8,128)(2,1)S(1)} %join.2.__.first_ref), channel_id=1, source_target_pairs={{0,16},{4,20},{8,24},{12,28},{16,0},{20,4},{24,8},{28,12},{1,17},{... | collective-permute-start | bytes 786440 | tf_op jit(solution)/shard_map/ppermute | solution.py:488
  33.3 9.8 %forward.1 = (bf16[256,1024]{1,0:T(8,128)(2,1)}, bf16[256,1024]{1,0:T(8,128)(2,1)}, bf16[256,1024]{1,0:T(8,128)(2,1)}, bf16[256,1024]{1,0:T(8,128)(2,1)}, bf16[2...) custom-call(bf16[256,1024]{1,0:T(8,128)(2,1)S(1)} %bitcast.19, ...), custom_call_target="tpu_custom_call" | custom-call | flops 3221225472 | bytes 13631488 | tf_op jit(solution)/shard_map/forward/pallas_call | solution.py:226
  43.1 3.0 %all-to-all-done.1 = bf16[8,32,512]{2,1,0:T(8,128)(2,1)S(1)} async-done(((bf16[8,32,512]{2,1,0:T(8,128)(2,1)}), bf16[8,32,512]{2,1,0:T(8,128)(2,1)S(1)}, u32[]{:S(2)}, u32[]{:S(2)}) %all-to-all-start.1) | async-done | bytes 262176 | tf_op jit(solution)/shard_map/all_to_all | solution.py:400
  46.1 3.5 %all-to-all-start.3 = ((bf16[8,256,128]{2,1,0:T(8,128)(2,1)}), bf16[8,256,128]{2,1,0:T(8,128)(2,1)S(1)}, u32[]{:S(2)}, u32[]{:S(2)}) async-start(bf16[8,256,128]{2,1,0:T(8,128)(2,1)} %get-tuple-element.36), calls=%async_computation.3 | async-start | bytes 1048576 | tf_op jit(solution)/shard_map/all_to_all | solution.py:400
  49.6 0.1 collective-permute-start.4
  49.6 0.5 collective-permute-start.6
  50.1 0.1 collective-permute-done.7.second_ref
  50.3 1.8 %collective-permute-start.8 = (bf16[4,8,16,512]{3,2,1,0:T(8,128)(2,1)S(1)}, bf16[4,8,16,512]{3,2,1,0:T(8,128)(2,1)S(1)}, u32[]{:S(2)}, u32[]{:S(2)}) collective-permute-start(bf16[4,8,16,512]{3,2,1,0:T(8,128)(2,1)S(1)} %join.3.rest_1_.first_ref), channel_id=1, source_target_pairs={{0,4},{4,0},{8,12},{12,8},{16,20},{20,16},{24,28},{28,24},{1,5},{5... | collective-permute-start | bytes 1572872 | tf_op jit(solution)/shard_map/ppermute | solution.py:488
  52.1 0.0 collective-permute-done.4.received_ref
  52.1 0.1 add.8.rest_0_.own_ref
  52.2 1.6 %collective-permute-start.5 = (bf16[256,512]{1,0:T(8,128)(2,1)S(1)}, bf16[256,512]{1,0:T(8,128)(2,1)S(1)}, u32[]{:S(2)}, u32[]{:S(2)}) collective-permute-start(bf16[256,512]{1,0:T(8,128)(2,1)S(1)} %add.8.rest_0_.own_ref), channel_id=1, source_target_pairs={{0,2},{1,3},{2,0},{3,1},{4,6},{5,7},{6,4},{7,5},{8,10},{9,11},{10,... | collective-permute-start | bytes 786440 | tf_op jit(solution)/shard_map/ppermute | solution.py:404
  53.8 0.0 collective-permute-done.6.other_ref
  53.8 11.3 %backward.1.back_ref = bf16[256,1024]{1,0:T(8,128)(2,1)S(1)} custom-call(bf16[256,1024]{1,0:T(8,128)(2,1)S(1)} %bitcast.20, bf16[256,512]{1,0:T(8,128)(2,1)S(1)} %bitcast.31, bf16[256,512]{1,0:T(8,128)(2,1)S(1)} %collective-permute-done.6.other_ref, bf16[1024,1024]{1,0:T(8,128)(2,1)} %bitcast.34, bf16[1024,3072]{1,0:T(8,128)(2,1)} %wv_ref.3, ...), custom_call_target="tpu_custom_call" | custom-call | flops 4294967296 | bytes 13631488 | tf_op jit(solution)/shard_map/backward/pallas_call | solution.py:338
  65.0 0.0 collective-permute-done.5.received_ref
  65.1 1.0 %add_mixed.1._ = bf16[256,1536]{1,0:T(8,128)(2,1)} custom-call(bf16[256,512]{1,0:T(8,128)(2,1)S(1)} %add.8.rest_0_.own_ref, bf16[256,512]{1,0:T(8,128)(2,1)S(1)} %collective-permute-done.5.received_ref, bf16[256,1024]{1,0:T(8,128)(2,1)S(1)} %backward.1.back_ref), custom_call_target="tpu_custom_call" | custom-call | tf_op jit(solution)/shard_map/add_mixed/pallas_call | solution.py:54
  66.1 2.0 %collective-permute-done.8.second_ref = bf16[4,8,16,512]{3,2,1,0:T(8,128)(2,1)S(1)} collective-permute-done((bf16[4,8,16,512]{3,2,1,0:T(8,128)(2,1)S(1)}, bf16[4,8,16,512]{3,2,1,0:T(8,128)(2,1)S(1)}, u32[]{:S(2)}, u32[]{:S(2)}) %collective-permute-start.8) | collective-permute-done | bytes 524320 | tf_op jit(solution)/shard_map/ppermute | solution.py:488
  68.0 0.1 arrange.1
  68.1 0.1 collective-permute-start.9
  68.2 0.0 all-to-all-done.3
  68.2 4.3 %all-to-all-start.2 = ((bf16[8,32,1536]{2,1,0:T(8,128)(2,1)}), bf16[8,32,1536]{2,1,0:T(8,128)(2,1)S(1)}, u32[]{:S(2)}, u32[]{:S(2)}) async-start(bf16[8,32,1536]{2,1,0:T(8,128)(2,1)} %bitcast.6), calls=%async_computation.2 | async-start | bytes 1572864 | tf_op jit(solution)/shard_map/all_to_all | solution.py:400
  72.5 0.2 constant_dynamic-slice_fusion
  72.8 1.6 %collective-permute-start.10 = (bf16[1024,128]{1,0:T(8,128)(2,1)S(1)}, bf16[1024,128]{1,0:T(8,128)(2,1)S(1)}, u32[]{:S(2)}, u32[]{:S(2)}) collective-permute-start(bf16[1024,128]{1,0:T(8,128)(2,1)S(1)} %bitcast.38), channel_id=1, source_target_pairs={{0,2},{1,3},{2,0},{3,1},{4,6},{5,7},{6,4},{7,5},{8,10},{9,11},{10,... | collective-permute-start | bytes 786440 | tf_op jit(solution)/shard_map/ppermute | solution.py:404
  74.3 6.9 %collective-permute-done.10.refs_1_ = bf16[1024,128]{1,0:T(8,128)(2,1)S(1)} collective-permute-done((bf16[1024,128]{1,0:T(8,128)(2,1)S(1)}, bf16[1024,128]{1,0:T(8,128)(2,1)S(1)}, u32[]{:S(2)}, u32[]{:S(2)}) %collective-permute-start.10) | collective-permute-done | bytes 262176 | tf_op jit(solution)/shard_map/ppermute | solution.py:404
  81.2 0.7 mix_gradient.1
  82.0 0.0 copy-start
  82.0 1.6 %collective-permute-start.11 = (bf16[128,1024]{1,0:T(8,128)(2,1)S(1)}, bf16[128,1024]{1,0:T(8,128)(2,1)S(1)}, u32[]{:S(2)}, u32[]{:S(2)}) collective-permute-start(bf16[128,1024]{1,0:T(8,128)(2,1)S(1)} %get-tuple-element.38), channel_id=1, source_target_pairs={{0,2},{1,3},{2,0},{3,1},{4,6},{5,7},{6,4},{7,5},{8,10},{9,11},{10,... | collective-permute-start | bytes 786440 | tf_op jit(solution)/shard_map/ppermute | solution.py:404
  83.6 6.1 %collective-permute-done.11 = bf16[128,1024]{1,0:T(8,128)(2,1)S(1)} collective-permute-done((bf16[128,1024]{1,0:T(8,128)(2,1)S(1)}, bf16[128,1024]{1,0:T(8,128)(2,1)S(1)}, u32[]{:S(2)}, u32[]{:S(2)}) %collective-permute-start.11) | collective-permute-done | bytes 262176 | tf_op jit(solution)/shard_map/ppermute | solution.py:404
  89.6 0.1 convert_add_fusion._
  89.7 0.0 copy-start.2
  89.7 3.6 %all-to-all-done.2.in_ref.back_ref = bf16[8,32,1536]{2,1,0:T(8,128)(2,1)S(1)} async-done(((bf16[8,32,1536]{2,1,0:T(8,128)(2,1)}), bf16[8,32,1536]{2,1,0:T(8,128)(2,1)S(1)}, u32[]{:S(2)}, u32[]{:S(2)}) %all-to-all-start.2) | async-done | bytes 786464 | tf_op jit(solution)/shard_map/all_to_all | solution.py:400
  93.3 0.1 collective-permute-start.12
  93.4 0.9 make_gradient.1
  94.3 0.6 collective-permute-done.12.other_ref
  94.9 1.0 %make_output.1 = bf16[2,2,4,16,1024]{4,3,2,1,0:T(8,128)(2,1)} custom-call(bf16[2,2,4,16,1024]{4,3,2,1,0:T(8,128)(2,1)S(1)} %bitcast.26, f32[1,1024]{1,0:T(1,128)S(1)} %copy-done.3, bf16[8,32,512]{2,1,0:T(8,128)(2,1)S(1)} %cut_mixed.1.own_ref, bf16[8,32,512]{2,1,0:T(8,128)(2,1)S(1)} %collective-permute-done.12.other_ref), custom_call_target="tpu_custom_call" | custom-call | tf_op jit(solution)/shard_map/make_output/pallas_call | solution.py:54
  (13 shorter events, 0.1 us)
Async XLA Ops:
  2.7 30.6 %copy-start.4 = (s32[2,16]{1,0:T(2,128)S(1)}, s32[2,16]{1,0:T(2,128)}, u32[]{:S(2)}) copy-start(s32[2,16]{1,0:T(2,128)} %mask_ref.1) | copy-start | bytes 388
  2.7 22.1 %all-to-all-start = ((bf16[8,32,1024]{2,1,0:T(8,128)(2,1)}), bf16[8,32,1024]{2,1,0:T(8,128)(2,1)S(1)}, u32[]{:S(2)}, u32[]{:S(2)}) async-start(bf16[8,32,1024]{2,1,0:T(8,128)(2,1)} %get-tuple-element.21), calls=%async_computation | async-start | bytes 1048576 | tf_op jit(solution)/shard_map/all_to_all | solution.py:400
  10.1 1.5 %collective-permute-start = (bf16[8,32,512]{2,1,0:T(8,128)(2,1)S(1)}, bf16[8,32,512]{2,1,0:T(8,128)(2,1)S(1)}, u32[]{:S(2)}, u32[]{:S(2)}) collective-permute-start(bf16[8,32,512]{2,1,0:T(8,128)(2,1)S(1)} %get-tuple-element.23), channel_id=1, source_target_pairs={{0,1},{1,0},{2,3},{3,2},{4,5},{5,4},{6,7},{7,6},{8,9},{9,8},{10,11... | collective-permute-start | bytes 786440 | tf_op jit(solution)/shard_map/ppermute | solution.py:404
  11.7 5.6 %collective-permute-start.1 = (bf16[8,16,512]{2,1,0:T(8,128)(2,1)S(1)}, bf16[8,16,512]{2,1,0:T(8,128)(2,1)S(1)}, u32[]{:S(2)}, u32[]{:S(2)}) collective-permute-start(bf16[8,16,512]{2,1,0:T(8,128)(2,1)S(1)} %get-tuple-element.25.second_ref), channel_id=1, source_target_pairs={{0,2},{1,3},{2,0},{3,1},{4,6},{5,7},{6,4},{7,5},{8,10},{9,11},{10,... | collective-permute-start | bytes 393224 | tf_op jit(solution)/shard_map/ppermute | solution.py:404
  17.3 7.5 %collective-permute-start.3 = (bf16[1,8,16,512]{3,2,1,0:T(8,128)(2,1)S(1)}, bf16[1,8,16,512]{3,2,1,0:T(8,128)(2,1)S(1)}, u32[]{:S(2)}, u32[]{:S(2)}) collective-permute-start(bf16[1,8,16,512]{3,2,1,0:T(8,128)(2,1)S(1)} %bitcast.28), channel_id=1, source_target_pairs={{0,8},{4,12},{8,0},{12,4},{16,24},{20,28},{24,16},{28,20},{1,9},{5... | collective-permute-start | bytes 393224 | tf_op jit(solution)/shard_map/ppermute | solution.py:488
  19.4 5.4 %collective-permute-start.2 = (bf16[8,16,512]{2,1,0:T(8,128)(2,1)S(1)}, bf16[8,16,512]{2,1,0:T(8,128)(2,1)S(1)}, u32[]{:S(2)}, u32[]{:S(2)}) collective-permute-start(bf16[8,16,512]{2,1,0:T(8,128)(2,1)S(1)} %get-tuple-element.24.own_ref), channel_id=1, source_target_pairs={{0,2},{1,3},{2,0},{3,1},{4,6},{5,7},{6,4},{7,5},{8,10},{9,11},{10,... | collective-permute-start | bytes 393224 | tf_op jit(solution)/shard_map/ppermute | solution.py:404
  25.6 20.5 %all-to-all-start.1 = ((bf16[8,32,512]{2,1,0:T(8,128)(2,1)}), bf16[8,32,512]{2,1,0:T(8,128)(2,1)S(1)}, u32[]{:S(2)}, u32[]{:S(2)}) async-start(bf16[8,32,512]{2,1,0:T(8,128)(2,1)} %add_flow.1._), calls=%async_computation.1 | async-start | bytes 524288 | tf_op jit(solution)/shard_map/all_to_all | solution.py:400
  30.4 19.9 %collective-permute-start.7 = (bf16[2,8,16,512]{3,2,1,0:T(8,128)(2,1)S(1)}, bf16[2,8,16,512]{3,2,1,0:T(8,128)(2,1)S(1)}, u32[]{:S(2)}, u32[]{:S(2)}) collective-permute-start(bf16[2,8,16,512]{3,2,1,0:T(8,128)(2,1)S(1)} %join.2.__.first_ref), channel_id=1, source_target_pairs={{0,16},{4,20},{8,24},{12,28},{16,0},{20,4},{24,8},{28,12},{1,17},{... | collective-permute-start | bytes 786440 | tf_op jit(solution)/shard_map/ppermute | solution.py:488
  46.1 22.1 %all-to-all-start.3 = ((bf16[8,256,128]{2,1,0:T(8,128)(2,1)}), bf16[8,256,128]{2,1,0:T(8,128)(2,1)S(1)}, u32[]{:S(2)}, u32[]{:S(2)}) async-start(bf16[8,256,128]{2,1,0:T(8,128)(2,1)} %get-tuple-element.36), calls=%async_computation.3 | async-start | bytes 1048576 | tf_op jit(solution)/shard_map/all_to_all | solution.py:400
  49.6 2.5 %collective-permute-start.4 = (bf16[256,512]{1,0:T(8,128)(2,1)S(1)}, bf16[256,512]{1,0:T(8,128)(2,1)S(1)}, u32[]{:S(2)}, u32[]{:S(2)}) collective-permute-start(bf16[256,512]{1,0:T(8,128)(2,1)S(1)} %get-tuple-element.27), channel_id=1, source_target_pairs={{0,1},{1,0},{2,3},{3,2},{4,5},{5,4},{6,7},{7,6},{8,9},{9,8},{10,11... | collective-permute-start | bytes 786440 | tf_op jit(solution)/shard_map/ppermute | solution.py:404
  49.6 4.1 %collective-permute-start.6 = (bf16[256,512]{1,0:T(8,128)(2,1)S(1)}, bf16[256,512]{1,0:T(8,128)(2,1)S(1)}, u32[]{:S(2)}, u32[]{:S(2)}) collective-permute-start(bf16[256,512]{1,0:T(8,128)(2,1)S(1)} %bitcast.30), channel_id=1, source_target_pairs={{0,1},{1,0},{2,3},{3,2},{4,5},{5,4},{6,7},{7,6},{8,9},{9,8},{10,11... | collective-permute-start | bytes 786440 | tf_op jit(solution)/shard_map/ppermute | solution.py:404
  50.3 17.7 %collective-permute-start.8 = (bf16[4,8,16,512]{3,2,1,0:T(8,128)(2,1)S(1)}, bf16[4,8,16,512]{3,2,1,0:T(8,128)(2,1)S(1)}, u32[]{:S(2)}, u32[]{:S(2)}) collective-permute-start(bf16[4,8,16,512]{3,2,1,0:T(8,128)(2,1)S(1)} %join.3.rest_1_.first_ref), channel_id=1, source_target_pairs={{0,4},{4,0},{8,12},{12,8},{16,20},{20,16},{24,28},{28,24},{1,5},{5... | collective-permute-start | bytes 1572872 | tf_op jit(solution)/shard_map/ppermute | solution.py:488
  52.2 12.9 %collective-permute-start.5 = (bf16[256,512]{1,0:T(8,128)(2,1)S(1)}, bf16[256,512]{1,0:T(8,128)(2,1)S(1)}, u32[]{:S(2)}, u32[]{:S(2)}) collective-permute-start(bf16[256,512]{1,0:T(8,128)(2,1)S(1)} %add.8.rest_0_.own_ref), channel_id=1, source_target_pairs={{0,2},{1,3},{2,0},{3,1},{4,6},{5,7},{6,4},{7,5},{8,10},{9,11},{10,... | collective-permute-start | bytes 786440 | tf_op jit(solution)/shard_map/ppermute | solution.py:404
  68.1 13.1 %collective-permute-start.9 = (bf16[1024,512]{1,0:T(8,128)(2,1)S(1)}, bf16[1024,512]{1,0:T(8,128)(2,1)S(1)}, u32[]{:S(2)}, u32[]{:S(2)}) collective-permute-start(bf16[1024,512]{1,0:T(8,128)(2,1)S(1)} %bitcast.21), channel_id=1, source_target_pairs={{0,1},{1,0},{2,3},{3,2},{4,5},{5,4},{6,7},{7,6},{8,9},{9,8},{10,11... | collective-permute-start | bytes 3145736 | tf_op jit(solution)/shard_map/ppermute | solution.py:404
  68.2 25.1 %all-to-all-start.2 = ((bf16[8,32,1536]{2,1,0:T(8,128)(2,1)}), bf16[8,32,1536]{2,1,0:T(8,128)(2,1)S(1)}, u32[]{:S(2)}, u32[]{:S(2)}) async-start(bf16[8,32,1536]{2,1,0:T(8,128)(2,1)} %bitcast.6), calls=%async_computation.2 | async-start | bytes 1572864 | tf_op jit(solution)/shard_map/all_to_all | solution.py:400
  72.8 8.5 %collective-permute-start.10 = (bf16[1024,128]{1,0:T(8,128)(2,1)S(1)}, bf16[1024,128]{1,0:T(8,128)(2,1)S(1)}, u32[]{:S(2)}, u32[]{:S(2)}) collective-permute-start(bf16[1024,128]{1,0:T(8,128)(2,1)S(1)} %bitcast.38), channel_id=1, source_target_pairs={{0,2},{1,3},{2,0},{3,1},{4,6},{5,7},{6,4},{7,5},{8,10},{9,11},{10,... | collective-permute-start | bytes 786440 | tf_op jit(solution)/shard_map/ppermute | solution.py:404
  82.0 11.4 %copy-start = (bf16[2,1,2,64,1024]{4,3,2,1,0:T(8,128)(2,1)S(1)}, bf16[2,1,2,64,1024]{4,3,2,1,0:T(8,128)(2,1)}, u32[]{:S(2)}) copy-start(bf16[2,1,2,64,1024]{4,3,2,1,0:T(8,128)(2,1)} %param.11) | copy-start | bytes 1572868
  82.0 7.7 %collective-permute-start.11 = (bf16[128,1024]{1,0:T(8,128)(2,1)S(1)}, bf16[128,1024]{1,0:T(8,128)(2,1)S(1)}, u32[]{:S(2)}, u32[]{:S(2)}) collective-permute-start(bf16[128,1024]{1,0:T(8,128)(2,1)S(1)} %get-tuple-element.38), channel_id=1, source_target_pairs={{0,2},{1,3},{2,0},{3,1},{4,6},{5,7},{6,4},{7,5},{8,10},{9,11},{10,... | collective-permute-start | bytes 786440 | tf_op jit(solution)/shard_map/ppermute | solution.py:404
  89.6 5.3 %copy-start.1 = (bf16[2,1,2,64,1024]{4,3,2,1,0:T(8,128)(2,1)S(1)}, bf16[2,1,2,64,1024]{4,3,2,1,0:T(8,128)(2,1)}, u32[]{:S(2)}) copy-start(bf16[2,1,2,64,1024]{4,3,2,1,0:T(8,128)(2,1)} %param.6) | copy-start | bytes 1572868
  89.6 5.3 %copy-start.3 = (f32[1,1024]{1,0:T(1,128)S(1)}, f32[1,1024]{1,0:T(1,128)}, u32[]{:S(2)}) copy-start(f32[1,1024]{1,0:T(1,128)} %gain_ref.3) | copy-start | bytes 12292
  89.7 6.2 %copy-start.2 = (f32[128,1024]{1,0:T(8,128)}, f32[128,1024]{1,0:T(8,128)S(1)}, u32[]{:S(2)}) copy-start(f32[128,1024]{1,0:T(8,128)S(1)} %convert_add_fusion._) | copy-start | bytes 1572868
  93.3 1.6 %collective-permute-start.12 = (bf16[8,32,512]{2,1,0:T(8,128)(2,1)S(1)}, bf16[8,32,512]{2,1,0:T(8,128)(2,1)S(1)}, u32[]{:S(2)}, u32[]{:S(2)}) collective-permute-start(bf16[8,32,512]{2,1,0:T(8,128)(2,1)S(1)} %cut_mixed.1.own_ref), channel_id=1, source_target_pairs={{0,1},{1,0},{2,3},{3,2},{4,5},{5,4},{6,7},{7,6},{8,9},{9,8},{10,11... | collective-permute-start | bytes 786440 | tf_op jit(solution)/shard_map/ppermute | solution.py:404

commit v4 on v3

--- a/solution.py
+++ b/solution.py
@@ -355,8 +355,8 @@
         scratch_shapes=[pltpu.VMEM((count, width), F32)],
         compiler_params=params(),
         cost_estimate=pl.CostEstimate(
-            flops=2 * count * width * (4 * width + 4 * count * 4),
-            bytes_accessed=20 * count * width + 8 * width * width,
+            flops=2 * count * width * width,
+            bytes_accessed=2 * count * width,
             transcendentals=0,
         ),
         name="backward",

time: 96.5 us -> 96.5 us (level)
  no operation moved by 1% of the time
where the time goes in v4:
time: 96.5 us; the launch traced here: 95.9 us
  starting transfers between devices  34.7 us (36%)
  waiting for transfers between devices  32.4 us (34%)
  Pallas kernels  27.8 us (29%)
    all_to_all x4, starting transfers between devices, swap(): return lax.all_to_all(block, 'lat', split_axis=0, concat_axis=0, tiled=True)  20 us
    ppermute x10, waiting for transfers between devices, from_level(): lax.ppermute(block, 'lev', [(i, i ^ offset) for i in range(lax.axis_size(...  19.1 us
    pallas_call x1, Pallas kernels, backward(): pl.pallas_call(backward_kernel, out_shape=jax.ShapeDtypeStruct((count, wi...  11.3 us
    pallas_call x1, Pallas kernels, forward(): pl.pallas_call(functools.partial(forward_kernel, samples, lat_count, chun...  9.76 us
    ppermute x10, starting transfers between devices, from_level(): lax.ppermute(block, 'lev', [(i, i ^ offset) for i in range(lax.axis_size(...  8.08 us
    ppermute x3, waiting for transfers between devices, from_owner(): lax.ppermute(block, 'lat', [(i, i ^ offset) for i in range(lax.axis_size(...  6.7 us
    all_to_all x4, waiting for transfers between devices, swap(): return lax.all_to_all(block, 'lat', split_axis=0, concat_axis=0, tiled=True)  6.59 us
    ppermute x3, starting transfers between devices, from_owner(): lax.ppermute(block, 'lat', [(i, i ^ offset) for i in range(lax.axis_size(...  6.54 us
  transfers between devices with their start and end apart: 17, of which 10 were waited for; matrix products, arithmetic and copies ran while one was open for 0% of the time, Pallas kernels for 25%

profile of v4, /device:TPU:0, one launch (start us, length us, event | category | flops | bytes accessed | tf_op | source)
XLA Modules:
  0.0 95.9 jit_solution(3037172702579037371)
XLA Ops:
  0.6 2.1 %pack.1 = (bf16[8,32,1024]{2,1,0:T(8,128)(2,1)}, bf16[8,32,512]{2,1,0:T(8,128)(2,1)S(1)}, bf16[8,32,512]{2,1,0:T(8,128)(2,1)S(1)}) custom-call(bf16[2,2,4,16,1024]{4,3,2,1,0:T(8,128)(2,1)} %bitcast.25, bf16[2,2,4,16,1024]{4,3,2,1,0:T(8,128)(2,1)} %bitcast.23, f32[1,1024]{1,0:T(1,128)} %gain_ref.3), custom_call_target="tpu_custom_call" | custom-call | tf_op jit(solution)/shard_map/pack/pallas_call | solution.py:54
  2.7 7.4 %all-to-all-start = ((bf16[8,32,1024]{2,1,0:T(8,128)(2,1)}), bf16[8,32,1024]{2,1,0:T(8,128)(2,1)S(1)}, u32[]{:S(2)}, u32[]{:S(2)}) async-start(bf16[8,32,1024]{2,1,0:T(8,128)(2,1)} %get-tuple-element.21), calls=%async_computation | async-start | bytes 1048576 | tf_op jit(solution)/shard_map/all_to_all | solution.py:400
  10.1 0.0 collective-permute-start
  10.1 1.5 %collective-permute-done.received_ref = bf16[8,32,512]{2,1,0:T(8,128)(2,1)S(1)} collective-permute-done((bf16[8,32,512]{2,1,0:T(8,128)(2,1)S(1)}, bf16[8,32,512]{2,1,0:T(8,128)(2,1)S(1)}, u32[]{:S(2)}, u32[]{:S(2)}) %collective-permute-start) | collective-permute-done | bytes 262176 | tf_op jit(solution)/shard_map/ppermute | solution.py:404
  11.6 0.1 split_rows.1
  11.7 1.6 %collective-permute-start.1 = (bf16[8,16,512]{2,1,0:T(8,128)(2,1)S(1)}, bf16[8,16,512]{2,1,0:T(8,128)(2,1)S(1)}, u32[]{:S(2)}, u32[]{:S(2)}) collective-permute-start(bf16[8,16,512]{2,1,0:T(8,128)(2,1)S(1)} %get-tuple-element.25.second_ref), channel_id=1, source_target_pairs={{0,2},{1,3},{2,0},{3,1},{4,6},{5,7},{6,4},{7,5},{8,10},{9,11},{10,... | collective-permute-start | bytes 393224 | tf_op jit(solution)/shard_map/ppermute | solution.py:404
  13.3 4.0 %collective-permute-done.1.received_ref = bf16[8,16,512]{2,1,0:T(8,128)(2,1)S(1)} collective-permute-done((bf16[8,16,512]{2,1,0:T(8,128)(2,1)S(1)}, bf16[8,16,512]{2,1,0:T(8,128)(2,1)S(1)}, u32[]{:S(2)}, u32[]{:S(2)}) %collective-permute-start.1) | collective-permute-done | bytes 131104 | tf_op jit(solution)/shard_map/ppermute | solution.py:404
  17.3 2.1 %collective-permute-start.3 = (bf16[1,8,16,512]{3,2,1,0:T(8,128)(2,1)S(1)}, bf16[1,8,16,512]{3,2,1,0:T(8,128)(2,1)S(1)}, u32[]{:S(2)}, u32[]{:S(2)}) collective-permute-start(bf16[1,8,16,512]{3,2,1,0:T(8,128)(2,1)S(1)} %bitcast.28), channel_id=1, source_target_pairs={{0,8},{4,12},{8,0},{12,4},{16,24},{20,28},{24,16},{28,20},{1,9},{5... | collective-permute-start | bytes 393224 | tf_op jit(solution)/shard_map/ppermute | solution.py:488
  19.4 1.5 %collective-permute-start.2 = (bf16[8,16,512]{2,1,0:T(8,128)(2,1)S(1)}, bf16[8,16,512]{2,1,0:T(8,128)(2,1)S(1)}, u32[]{:S(2)}, u32[]{:S(2)}) collective-permute-start(bf16[8,16,512]{2,1,0:T(8,128)(2,1)S(1)} %get-tuple-element.24.own_ref), channel_id=1, source_target_pairs={{0,2},{1,3},{2,0},{3,1},{4,6},{5,7},{6,4},{7,5},{8,10},{9,11},{10,... | collective-permute-start | bytes 393224 | tf_op jit(solution)/shard_map/ppermute | solution.py:404
  20.9 3.9 %collective-permute-done.3.second_ref = bf16[1,8,16,512]{3,2,1,0:T(8,128)(2,1)S(1)} collective-permute-done((bf16[1,8,16,512]{3,2,1,0:T(8,128)(2,1)S(1)}, bf16[1,8,16,512]{3,2,1,0:T(8,128)(2,1)S(1)}, u32[]{:S(2)}, u32[]{:S(2)}) %collective-permute-start.3) | collective-permute-done | bytes 131104 | tf_op jit(solution)/shard_map/ppermute | solution.py:488
  24.8 0.0 collective-permute-done.2.received_ref
  24.8 0.0 all-to-all-done
  24.8 0.8 add_flow.1._
  25.6 4.8 %all-to-all-start.1 = ((bf16[8,32,512]{2,1,0:T(8,128)(2,1)}), bf16[8,32,512]{2,1,0:T(8,128)(2,1)S(1)}, u32[]{:S(2)}, u32[]{:S(2)}) async-start(bf16[8,32,512]{2,1,0:T(8,128)(2,1)} %add_flow.1._), calls=%async_computation.1 | async-start | bytes 524288 | tf_op jit(solution)/shard_map/all_to_all | solution.py:400
  30.4 2.9 %collective-permute-start.7 = (bf16[2,8,16,512]{3,2,1,0:T(8,128)(2,1)S(1)}, bf16[2,8,16,512]{3,2,1,0:T(8,128)(2,1)S(1)}, u32[]{:S(2)}, u32[]{:S(2)}) collective-permute-start(bf16[2,8,16,512]{3,2,1,0:T(8,128)(2,1)S(1)} %join.2.__.first_ref), channel_id=1, source_target_pairs={{0,16},{4,20},{8,24},{12,28},{16,0},{20,4},{24,8},{28,12},{1,17},{... | collective-permute-start | bytes 786440 | tf_op jit(solution)/shard_map/ppermute | solution.py:488
  33.3 9.8 %forward.1 = (bf16[256,1024]{1,0:T(8,128)(2,1)}, bf16[256,1024]{1,0:T(8,128)(2,1)}, bf16[256,1024]{1,0:T(8,128)(2,1)}, bf16[256,1024]{1,0:T(8,128)(2,1)}, bf16[2...) custom-call(bf16[256,1024]{1,0:T(8,128)(2,1)S(1)} %bitcast.19, ...), custom_call_target="tpu_custom_call" | custom-call | flops 3221225472 | bytes 13631488 | tf_op jit(solution)/shard_map/forward/pallas_call | solution.py:226
  43.1 3.0 %all-to-all-done.1 = bf16[8,32,512]{2,1,0:T(8,128)(2,1)S(1)} async-done(((bf16[8,32,512]{2,1,0:T(8,128)(2,1)}), bf16[8,32,512]{2,1,0:T(8,128)(2,1)S(1)}, u32[]{:S(2)}, u32[]{:S(2)}) %all-to-all-start.1) | async-done | bytes 262176 | tf_op jit(solution)/shard_map/all_to_all | solution.py:400
  46.1 3.5 %all-to-all-start.3 = ((bf16[8,256,128]{2,1,0:T(8,128)(2,1)}), bf16[8,256,128]{2,1,0:T(8,128)(2,1)S(1)}, u32[]{:S(2)}, u32[]{:S(2)}) async-start(bf16[8,256,128]{2,1,0:T(8,128)(2,1)} %get-tuple-element.36), calls=%async_computation.3 | async-start | bytes 1048576 | tf_op jit(solution)/shard_map/all_to_all | solution.py:400
  49.6 0.1 collective-permute-start.4
  49.6 0.6 collective-permute-done.7.second_ref
  50.3 1.5 %collective-permute-start.8 = (bf16[4,8,16,512]{3,2,1,0:T(8,128)(2,1)S(1)}, bf16[4,8,16,512]{3,2,1,0:T(8,128)(2,1)S(1)}, u32[]{:S(2)}, u32[]{:S(2)}) collective-permute-start(bf16[4,8,16,512]{3,2,1,0:T(8,128)(2,1)S(1)} %join.3.rest_1_.first_ref), channel_id=1, source_target_pairs={{0,4},{4,0},{8,12},{12,8},{16,20},{20,16},{24,28},{28,24},{1,5},{5... | collective-permute-start | bytes 1572872 | tf_op jit(solution)/shard_map/ppermute | solution.py:488
  51.8 0.0 collective-permute-start.6
  51.8 0.0 collective-permute-done.4.received_ref
  51.8 0.1 add.8.rest_0_.own_ref
  51.9 1.6 %collective-permute-start.5 = (bf16[256,512]{1,0:T(8,128)(2,1)S(1)}, bf16[256,512]{1,0:T(8,128)(2,1)S(1)}, u32[]{:S(2)}, u32[]{:S(2)}) collective-permute-start(bf16[256,512]{1,0:T(8,128)(2,1)S(1)} %add.8.rest_0_.own_ref), channel_id=1, source_target_pairs={{0,2},{1,3},{2,0},{3,1},{4,6},{5,7},{6,4},{7,5},{8,10},{9,11},{10,... | collective-permute-start | bytes 786440 | tf_op jit(solution)/shard_map/ppermute | solution.py:404
  53.5 0.0 collective-permute-done.6.other_ref
  53.5 11.3 %backward.1.back_ref = bf16[256,1024]{1,0:T(8,128)(2,1)S(1)} custom-call(bf16[256,1024]{1,0:T(8,128)(2,1)S(1)} %bitcast.20, bf16[256,512]{1,0:T(8,128)(2,1)S(1)} %bitcast.31, bf16[256,512]{1,0:T(8,128)(2,1)S(1)} %collective-permute-done.6.other_ref, bf16[1024,1024]{1,0:T(8,128)(2,1)} %bitcast.34, bf16[1024,3072]{1,0:T(8,128)(2,1)} %wv_ref.3, ...), custom_call_target="tpu_custom_call" | custom-call | flops 536870912 | bytes 524288 | tf_op jit(solution)/shard_map/backward/pallas_call | solution.py:338
  64.8 0.0 collective-permute-done.5.received_ref
  64.8 1.0 %add_mixed.1._ = bf16[256,1536]{1,0:T(8,128)(2,1)} custom-call(bf16[256,512]{1,0:T(8,128)(2,1)S(1)} %add.8.rest_0_.own_ref, bf16[256,512]{1,0:T(8,128)(2,1)S(1)} %collective-permute-done.5.received_ref, bf16[256,1024]{1,0:T(8,128)(2,1)S(1)} %backward.1.back_ref), custom_call_target="tpu_custom_call" | custom-call | tf_op jit(solution)/shard_map/add_mixed/pallas_call | solution.py:54
  65.8 2.2 %collective-permute-done.8.second_ref = bf16[4,8,16,512]{3,2,1,0:T(8,128)(2,1)S(1)} collective-permute-done((bf16[4,8,16,512]{3,2,1,0:T(8,128)(2,1)S(1)}, bf16[4,8,16,512]{3,2,1,0:T(8,128)(2,1)S(1)}, u32[]{:S(2)}, u32[]{:S(2)}) %collective-permute-start.8) | collective-permute-done | bytes 524320 | tf_op jit(solution)/shard_map/ppermute | solution.py:488
  68.0 0.1 arrange.1
  68.1 0.1 collective-permute-start.9
  68.2 0.0 all-to-all-done.3
  68.2 4.3 %all-to-all-start.2 = ((bf16[8,32,1536]{2,1,0:T(8,128)(2,1)}), bf16[8,32,1536]{2,1,0:T(8,128)(2,1)S(1)}, u32[]{:S(2)}, u32[]{:S(2)}) async-start(bf16[8,32,1536]{2,1,0:T(8,128)(2,1)} %bitcast.6), calls=%async_computation.2 | async-start | bytes 1572864 | tf_op jit(solution)/shard_map/all_to_all | solution.py:400
  72.5 0.2 constant_dynamic-slice_fusion
  72.8 1.6 %collective-permute-start.10 = (bf16[1024,128]{1,0:T(8,128)(2,1)S(1)}, bf16[1024,128]{1,0:T(8,128)(2,1)S(1)}, u32[]{:S(2)}, u32[]{:S(2)}) collective-permute-start(bf16[1024,128]{1,0:T(8,128)(2,1)S(1)} %bitcast.38), channel_id=1, source_target_pairs={{0,2},{1,3},{2,0},{3,1},{4,6},{5,7},{6,4},{7,5},{8,10},{9,11},{10,... | collective-permute-start | bytes 786440 | tf_op jit(solution)/shard_map/ppermute | solution.py:404
  74.3 6.9 %collective-permute-done.10.refs_1_ = bf16[1024,128]{1,0:T(8,128)(2,1)S(1)} collective-permute-done((bf16[1024,128]{1,0:T(8,128)(2,1)S(1)}, bf16[1024,128]{1,0:T(8,128)(2,1)S(1)}, u32[]{:S(2)}, u32[]{:S(2)}) %collective-permute-start.10) | collective-permute-done | bytes 262176 | tf_op jit(solution)/shard_map/ppermute | solution.py:404
  81.2 0.7 mix_gradient.1
  82.0 0.0 copy-start
  82.0 1.6 %collective-permute-start.11 = (bf16[128,1024]{1,0:T(8,128)(2,1)S(1)}, bf16[128,1024]{1,0:T(8,128)(2,1)S(1)}, u32[]{:S(2)}, u32[]{:S(2)}) collective-permute-start(bf16[128,1024]{1,0:T(8,128)(2,1)S(1)} %get-tuple-element.38), channel_id=1, source_target_pairs={{0,2},{1,3},{2,0},{3,1},{4,6},{5,7},{6,4},{7,5},{8,10},{9,11},{10,... | collective-permute-start | bytes 786440 | tf_op jit(solution)/shard_map/ppermute | solution.py:404
  83.6 6.1 %collective-permute-done.11 = bf16[128,1024]{1,0:T(8,128)(2,1)S(1)} collective-permute-done((bf16[128,1024]{1,0:T(8,128)(2,1)S(1)}, bf16[128,1024]{1,0:T(8,128)(2,1)S(1)}, u32[]{:S(2)}, u32[]{:S(2)}) %collective-permute-start.11) | collective-permute-done | bytes 262176 | tf_op jit(solution)/shard_map/ppermute | solution.py:404
  89.6 0.1 convert_add_fusion._
  89.7 0.0 copy-start.2
  89.7 3.6 %all-to-all-done.2.in_ref.back_ref = bf16[8,32,1536]{2,1,0:T(8,128)(2,1)S(1)} async-done(((bf16[8,32,1536]{2,1,0:T(8,128)(2,1)}), bf16[8,32,1536]{2,1,0:T(8,128)(2,1)S(1)}, u32[]{:S(2)}, u32[]{:S(2)}) %all-to-all-start.2) | async-done | bytes 786464 | tf_op jit(solution)/shard_map/all_to_all | solution.py:400
  93.3 0.1 collective-permute-start.12
  93.4 0.9 make_gradient.1
  94.3 0.6 collective-permute-done.12.other_ref
  94.9 1.0 %make_output.1 = bf16[2,2,4,16,1024]{4,3,2,1,0:T(8,128)(2,1)} custom-call(bf16[2,2,4,16,1024]{4,3,2,1,0:T(8,128)(2,1)S(1)} %bitcast.26, f32[1,1024]{1,0:T(1,128)S(1)} %copy-done.3, bf16[8,32,512]{2,1,0:T(8,128)(2,1)S(1)} %cut_mixed.1.own_ref, bf16[8,32,512]{2,1,0:T(8,128)(2,1)S(1)} %collective-permute-done.12.other_ref), custom_call_target="tpu_custom_call" | custom-call | tf_op jit(solution)/shard_map/make_output/pallas_call | solution.py:54
  (13 shorter events, 0.1 us)
Async XLA Ops:
  2.7 30.6 %copy-start.4 = (s32[2,16]{1,0:T(2,128)S(1)}, s32[2,16]{1,0:T(2,128)}, u32[]{:S(2)}) copy-start(s32[2,16]{1,0:T(2,128)} %mask_ref.1) | copy-start | bytes 388
  2.7 22.1 %all-to-all-start = ((bf16[8,32,1024]{2,1,0:T(8,128)(2,1)}), bf16[8,32,1024]{2,1,0:T(8,128)(2,1)S(1)}, u32[]{:S(2)}, u32[]{:S(2)}) async-start(bf16[8,32,1024]{2,1,0:T(8,128)(2,1)} %get-tuple-element.21), calls=%async_computation | async-start | bytes 1048576 | tf_op jit(solution)/shard_map/all_to_all | solution.py:400
  10.1 1.5 %collective-permute-start = (bf16[8,32,512]{2,1,0:T(8,128)(2,1)S(1)}, bf16[8,32,512]{2,1,0:T(8,128)(2,1)S(1)}, u32[]{:S(2)}, u32[]{:S(2)}) collective-permute-start(bf16[8,32,512]{2,1,0:T(8,128)(2,1)S(1)} %get-tuple-element.23), channel_id=1, source_target_pairs={{0,1},{1,0},{2,3},{3,2},{4,5},{5,4},{6,7},{7,6},{8,9},{9,8},{10,11... | collective-permute-start | bytes 786440 | tf_op jit(solution)/shard_map/ppermute | solution.py:404
  11.7 5.6 %collective-permute-start.1 = (bf16[8,16,512]{2,1,0:T(8,128)(2,1)S(1)}, bf16[8,16,512]{2,1,0:T(8,128)(2,1)S(1)}, u32[]{:S(2)}, u32[]{:S(2)}) collective-permute-start(bf16[8,16,512]{2,1,0:T(8,128)(2,1)S(1)} %get-tuple-element.25.second_ref), channel_id=1, source_target_pairs={{0,2},{1,3},{2,0},{3,1},{4,6},{5,7},{6,4},{7,5},{8,10},{9,11},{10,... | collective-permute-start | bytes 393224 | tf_op jit(solution)/shard_map/ppermute | solution.py:404
  17.3 7.5 %collective-permute-start.3 = (bf16[1,8,16,512]{3,2,1,0:T(8,128)(2,1)S(1)}, bf16[1,8,16,512]{3,2,1,0:T(8,128)(2,1)S(1)}, u32[]{:S(2)}, u32[]{:S(2)}) collective-permute-start(bf16[1,8,16,512]{3,2,1,0:T(8,128)(2,1)S(1)} %bitcast.28), channel_id=1, source_target_pairs={{0,8},{4,12},{8,0},{12,4},{16,24},{20,28},{24,16},{28,20},{1,9},{5... | collective-permute-start | bytes 393224 | tf_op jit(solution)/shard_map/ppermute | solution.py:488
  19.4 5.4 %collective-permute-start.2 = (bf16[8,16,512]{2,1,0:T(8,128)(2,1)S(1)}, bf16[8,16,512]{2,1,0:T(8,128)(2,1)S(1)}, u32[]{:S(2)}, u32[]{:S(2)}) collective-permute-start(bf16[8,16,512]{2,1,0:T(8,128)(2,1)S(1)} %get-tuple-element.24.own_ref), channel_id=1, source_target_pairs={{0,2},{1,3},{2,0},{3,1},{4,6},{5,7},{6,4},{7,5},{8,10},{9,11},{10,... | collective-permute-start | bytes 393224 | tf_op jit(solution)/shard_map/ppermute | solution.py:404
  25.6 20.5 %all-to-all-start.1 = ((bf16[8,32,512]{2,1,0:T(8,128)(2,1)}), bf16[8,32,512]{2,1,0:T(8,128)(2,1)S(1)}, u32[]{:S(2)}, u32[]{:S(2)}) async-start(bf16[8,32,512]{2,1,0:T(8,128)(2,1)} %add_flow.1._), calls=%async_computation.1 | async-start | bytes 524288 | tf_op jit(solution)/shard_map/all_to_all | solution.py:400
  30.4 19.9 %collective-permute-start.7 = (bf16[2,8,16,512]{3,2,1,0:T(8,128)(2,1)S(1)}, bf16[2,8,16,512]{3,2,1,0:T(8,128)(2,1)S(1)}, u32[]{:S(2)}, u32[]{:S(2)}) collective-permute-start(bf16[2,8,16,512]{3,2,1,0:T(8,128)(2,1)S(1)} %join.2.__.first_ref), channel_id=1, source_target_pairs={{0,16},{4,20},{8,24},{12,28},{16,0},{20,4},{24,8},{28,12},{1,17},{... | collective-permute-start | bytes 786440 | tf_op jit(solution)/shard_map/ppermute | solution.py:488
  46.1 22.1 %all-to-all-start.3 = ((bf16[8,256,128]{2,1,0:T(8,128)(2,1)}), bf16[8,256,128]{2,1,0:T(8,128)(2,1)S(1)}, u32[]{:S(2)}, u32[]{:S(2)}) async-start(bf16[8,256,128]{2,1,0:T(8,128)(2,1)} %get-tuple-element.36), calls=%async_computation.3 | async-start | bytes 1048576 | tf_op jit(solution)/shard_map/all_to_all | solution.py:400
  49.6 2.3 %collective-permute-start.4 = (bf16[256,512]{1,0:T(8,128)(2,1)S(1)}, bf16[256,512]{1,0:T(8,128)(2,1)S(1)}, u32[]{:S(2)}, u32[]{:S(2)}) collective-permute-start(bf16[256,512]{1,0:T(8,128)(2,1)S(1)} %get-tuple-element.27), channel_id=1, source_target_pairs={{0,1},{1,0},{2,3},{3,2},{4,5},{5,4},{6,7},{7,6},{8,9},{9,8},{10,11... | collective-permute-start | bytes 786440 | tf_op jit(solution)/shard_map/ppermute | solution.py:404
  50.3 17.7 %collective-permute-start.8 = (bf16[4,8,16,512]{3,2,1,0:T(8,128)(2,1)S(1)}, bf16[4,8,16,512]{3,2,1,0:T(8,128)(2,1)S(1)}, u32[]{:S(2)}, u32[]{:S(2)}) collective-permute-start(bf16[4,8,16,512]{3,2,1,0:T(8,128)(2,1)S(1)} %join.3.rest_1_.first_ref), channel_id=1, source_target_pairs={{0,4},{4,0},{8,12},{12,8},{16,20},{20,16},{24,28},{28,24},{1,5},{5... | collective-permute-start | bytes 1572872 | tf_op jit(solution)/shard_map/ppermute | solution.py:488
  51.8 1.7 %collective-permute-start.6 = (bf16[256,512]{1,0:T(8,128)(2,1)S(1)}, bf16[256,512]{1,0:T(8,128)(2,1)S(1)}, u32[]{:S(2)}, u32[]{:S(2)}) collective-permute-start(bf16[256,512]{1,0:T(8,128)(2,1)S(1)} %bitcast.30), channel_id=1, source_target_pairs={{0,1},{1,0},{2,3},{3,2},{4,5},{5,4},{6,7},{7,6},{8,9},{9,8},{10,11... | collective-permute-start | bytes 786440 | tf_op jit(solution)/shard_map/ppermute | solution.py:404
  51.9 12.9 %collective-permute-start.5 = (bf16[256,512]{1,0:T(8,128)(2,1)S(1)}, bf16[256,512]{1,0:T(8,128)(2,1)S(1)}, u32[]{:S(2)}, u32[]{:S(2)}) collective-permute-start(bf16[256,512]{1,0:T(8,128)(2,1)S(1)} %add.8.rest_0_.own_ref), channel_id=1, source_target_pairs={{0,2},{1,3},{2,0},{3,1},{4,6},{5,7},{6,4},{7,5},{8,10},{9,11},{10,... | collective-permute-start | bytes 786440 | tf_op jit(solution)/shard_map/ppermute | solution.py:404
  68.1 13.1 %collective-permute-start.9 = (bf16[1024,512]{1,0:T(8,128)(2,1)S(1)}, bf16[1024,512]{1,0:T(8,128)(2,1)S(1)}, u32[]{:S(2)}, u32[]{:S(2)}) collective-permute-start(bf16[1024,512]{1,0:T(8,128)(2,1)S(1)} %bitcast.21), channel_id=1, source_target_pairs={{0,1},{1,0},{2,3},{3,2},{4,5},{5,4},{6,7},{7,6},{8,9},{9,8},{10,11... | collective-permute-start | bytes 3145736 | tf_op jit(solution)/shard_map/ppermute | solution.py:404
  68.2 25.1 %all-to-all-start.2 = ((bf16[8,32,1536]{2,1,0:T(8,128)(2,1)}), bf16[8,32,1536]{2,1,0:T(8,128)(2,1)S(1)}, u32[]{:S(2)}, u32[]{:S(2)}) async-start(bf16[8,32,1536]{2,1,0:T(8,128)(2,1)} %bitcast.6), calls=%async_computation.2 | async-start | bytes 1572864 | tf_op jit(solution)/shard_map/all_to_all | solution.py:400
  72.8 8.5 %collective-permute-start.10 = (bf16[1024,128]{1,0:T(8,128)(2,1)S(1)}, bf16[1024,128]{1,0:T(8,128)(2,1)S(1)}, u32[]{:S(2)}, u32[]{:S(2)}) collective-permute-start(bf16[1024,128]{1,0:T(8,128)(2,1)S(1)} %bitcast.38), channel_id=1, source_target_pairs={{0,2},{1,3},{2,0},{3,1},{4,6},{5,7},{6,4},{7,5},{8,10},{9,11},{10,... | collective-permute-start | bytes 786440 | tf_op jit(solution)/shard_map/ppermute | solution.py:404
  82.0 11.4 %copy-start = (bf16[2,1,2,64,1024]{4,3,2,1,0:T(8,128)(2,1)S(1)}, bf16[2,1,2,64,1024]{4,3,2,1,0:T(8,128)(2,1)}, u32[]{:S(2)}) copy-start(bf16[2,1,2,64,1024]{4,3,2,1,0:T(8,128)(2,1)} %param.11) | copy-start | bytes 1572868
  82.0 7.7 %collective-permute-start.11 = (bf16[128,1024]{1,0:T(8,128)(2,1)S(1)}, bf16[128,1024]{1,0:T(8,128)(2,1)S(1)}, u32[]{:S(2)}, u32[]{:S(2)}) collective-permute-start(bf16[128,1024]{1,0:T(8,128)(2,1)S(1)} %get-tuple-element.38), channel_id=1, source_target_pairs={{0,2},{1,3},{2,0},{3,1},{4,6},{5,7},{6,4},{7,5},{8,10},{9,11},{10,... | collective-permute-start | bytes 786440 | tf_op jit(solution)/shard_map/ppermute | solution.py:404
  89.6 5.3 %copy-start.1 = (bf16[2,1,2,64,1024]{4,3,2,1,0:T(8,128)(2,1)S(1)}, bf16[2,1,2,64,1024]{4,3,2,1,0:T(8,128)(2,1)}, u32[]{:S(2)}) copy-start(bf16[2,1,2,64,1024]{4,3,2,1,0:T(8,128)(2,1)} %param.6) | copy-start | bytes 1572868
  89.6 5.3 %copy-start.3 = (f32[1,1024]{1,0:T(1,128)S(1)}, f32[1,1024]{1,0:T(1,128)}, u32[]{:S(2)}) copy-start(f32[1,1024]{1,0:T(1,128)} %gain_ref.3) | copy-start | bytes 12292
  89.7 6.2 %copy-start.2 = (f32[128,1024]{1,0:T(8,128)}, f32[128,1024]{1,0:T(8,128)S(1)}, u32[]{:S(2)}) copy-start(f32[128,1024]{1,0:T(8,128)S(1)} %convert_add_fusion._) | copy-start | bytes 1572868
  93.3 1.6 %collective-permute-start.12 = (bf16[8,32,512]{2,1,0:T(8,128)(2,1)S(1)}, bf16[8,32,512]{2,1,0:T(8,128)(2,1)S(1)}, u32[]{:S(2)}, u32[]{:S(2)}) collective-permute-start(bf16[8,32,512]{2,1,0:T(8,128)(2,1)S(1)} %cut_mixed.1.own_ref), channel_id=1, source_target_pairs={{0,1},{1,0},{2,3},{3,2},{4,5},{5,4},{6,7},{7,6},{8,9},{9,8},{10,11... | collective-permute-start | bytes 786440 | tf_op jit(solution)/shard_map/ppermute | solution.py:404

commit v5 on v3

--- a/solution.py
+++ b/solution.py
@@ -602,7 +602,7 @@
     attended = attended.reshape(owners, owners, cells, features)
     attended = [chip_rows(attended, 2, chip ^ k).reshape(-1, features) for k in range(chips)]
     attended[1:] = [from_level(attended[k], 2 * k) for k in range(1, chips)]
-    flow_rows = arrange(flow_rows, received, sent).reshape(-1, half)
+    flow_rows = arrange(flow_rows, received, attended[-1]).reshape(-1, half)
     grads = mix_gradient(attended, (flow_rows, from_level(flow_rows, 1)), factor)
     mix_grad = grads[0]
     for k in range(1, chips):

time: 96.5 us -> 121 us (1.25)
  waiting for transfers between devices: 31.6 us -> 55.3 us
    all_to_all x4, waiting for transfers between devices: 6.59 us -> 32.3 us  [swap(): return lax.all_to_all(block, 'lat', split_axis=0, concat_axis=0, tiled=True)]
    ppermute x10, waiting for transfers between devices: 19.1 us -> 13 us  [from_level(): lax.ppermute(block, 'lev', [(i, i ^ offset) for i in range(lax.axis_size(...]
    ppermute x3, waiting for transfers between devices: 5.94 us -> 10 us  [from_owner(): lax.ppermute(block, 'lat', [(i, i ^ offset) for i in range(lax.axis_size(...]
    pallas_call x1, Pallas kernels: 0.74 us -> 1.96 us  [mix_gradient(): pl.pallas_call(functools.partial(mix_gradient_kernel, factor), out_shape=...]
  transfers between devices with their start and end apart: 17 -> 17, of which waited for: 10 -> 10; matrix products, arithmetic and copies ran while one was open for 0% -> 1% of each run, Pallas kernels for 25% -> 13%
where the time goes in v5:
time: 121 us
  waiting for transfers between devices  55.3 us (46%)
  starting transfers between devices  34.2 us (28%)
  Pallas kernels  29 us (24%)
  local copies, waits for them, and re-layouts  1.32 us (1%)
    all_to_all x4, waiting for transfers between devices, swap(): return lax.all_to_all(block, 'lat', split_axis=0, concat_axis=0, tiled=True)  32.3 us
    all_to_all x4, starting transfers between devices, swap(): return lax.all_to_all(block, 'lat', split_axis=0, concat_axis=0, tiled=True)  19.7 us
    ppermute x10, waiting for transfers between devices, from_level(): lax.ppermute(block, 'lev', [(i, i ^ offset) for i in range(lax.axis_size(...  13 us
    pallas_call x1, Pallas kernels, backward(): pl.pallas_call(backward_kernel, out_shape=jax.ShapeDtypeStruct((count, wi...  11.3 us
    ppermute x3, waiting for transfers between devices, from_owner(): lax.ppermute(block, 'lat', [(i, i ^ offset) for i in range(lax.axis_size(...  10 us
    pallas_call x1, Pallas kernels, forward(): pl.pallas_call(functools.partial(forward_kernel, samples, lat_count, chun...  9.77 us
    ppermute x10, starting transfers between devices, from_level(): lax.ppermute(block, 'lev', [(i, i ^ offset) for i in range(lax.axis_size(...  8.03 us
    ppermute x3, starting transfers between devices, from_owner(): lax.ppermute(block, 'lat', [(i, i ^ offset) for i in range(lax.axis_size(...  6.51 us
  transfers between devices with their start and end apart: 17, of which 10 were waited for; matrix products, arithmetic and copies ran while one was open for 1% of the time, Pallas kernels for 13%

profile of v5, /device:TPU:0, one launch (start us, length us, event | category | flops | bytes accessed | tf_op | source)
XLA Modules:
  0.0 120.7 jit_solution(6104363364913832480)
XLA Ops:
  0.6 2.1 %pack.1 = (bf16[8,32,1024]{2,1,0:T(8,128)(2,1)}, bf16[8,32,512]{2,1,0:T(8,128)(2,1)S(1)}, bf16[8,32,512]{2,1,0:T(8,128)(2,1)S(1)}) custom-call(bf16[2,2,4,16,1024]{4,3,2,1,0:T(8,128)(2,1)} %bitcast.25, bf16[2,2,4,16,1024]{4,3,2,1,0:T(8,128)(2,1)} %bitcast.23, f32[1,1024]{1,0:T(1,128)} %gain_ref.3), custom_call_target="tpu_custom_call" | custom-call | tf_op jit(solution)/shard_map/pack/pallas_call | solution.py:54
  2.7 7.4 %all-to-all-start = ((bf16[8,32,1024]{2,1,0:T(8,128)(2,1)}), bf16[8,32,1024]{2,1,0:T(8,128)(2,1)S(1)}, u32[]{:S(2)}, u32[]{:S(2)}) async-start(bf16[8,32,1024]{2,1,0:T(8,128)(2,1)} %get-tuple-element.21), calls=%async_computation | async-start | bytes 1048576 | tf_op jit(solution)/shard_map/all_to_all | solution.py:400
  10.1 0.0 collective-permute-start
  10.1 1.5 %collective-permute-done.received_ref = bf16[8,32,512]{2,1,0:T(8,128)(2,1)S(1)} collective-permute-done((bf16[8,32,512]{2,1,0:T(8,128)(2,1)S(1)}, bf16[8,32,512]{2,1,0:T(8,128)(2,1)S(1)}, u32[]{:S(2)}, u32[]{:S(2)}) %collective-permute-start) | collective-permute-done | bytes 262176 | tf_op jit(solution)/shard_map/ppermute | solution.py:404
  11.6 0.1 split_rows.1
  11.7 1.6 %collective-permute-start.1 = (bf16[8,16,512]{2,1,0:T(8,128)(2,1)S(1)}, bf16[8,16,512]{2,1,0:T(8,128)(2,1)S(1)}, u32[]{:S(2)}, u32[]{:S(2)}) collective-permute-start(bf16[8,16,512]{2,1,0:T(8,128)(2,1)S(1)} %get-tuple-element.25.second_ref), channel_id=1, source_target_pairs={{0,2},{1,3},{2,0},{3,1},{4,6},{5,7},{6,4},{7,5},{8,10},{9,11},{10,... | collective-permute-start | bytes 393224 | tf_op jit(solution)/shard_map/ppermute | solution.py:404
  13.3 4.0 %collective-permute-done.1.received_ref = bf16[8,16,512]{2,1,0:T(8,128)(2,1)S(1)} collective-permute-done((bf16[8,16,512]{2,1,0:T(8,128)(2,1)S(1)}, bf16[8,16,512]{2,1,0:T(8,128)(2,1)S(1)}, u32[]{:S(2)}, u32[]{:S(2)}) %collective-permute-start.1) | collective-permute-done | bytes 131104 | tf_op jit(solution)/shard_map/ppermute | solution.py:404
  17.3 2.1 %collective-permute-start.3 = (bf16[1,8,16,512]{3,2,1,0:T(8,128)(2,1)S(1)}, bf16[1,8,16,512]{3,2,1,0:T(8,128)(2,1)S(1)}, u32[]{:S(2)}, u32[]{:S(2)}) collective-permute-start(bf16[1,8,16,512]{3,2,1,0:T(8,128)(2,1)S(1)} %bitcast.28), channel_id=1, source_target_pairs={{0,8},{4,12},{8,0},{12,4},{16,24},{20,28},{24,16},{28,20},{1,9},{5... | collective-permute-start | bytes 393224 | tf_op jit(solution)/shard_map/ppermute | solution.py:488
  19.4 1.5 %collective-permute-start.2 = (bf16[8,16,512]{2,1,0:T(8,128)(2,1)S(1)}, bf16[8,16,512]{2,1,0:T(8,128)(2,1)S(1)}, u32[]{:S(2)}, u32[]{:S(2)}) collective-permute-start(bf16[8,16,512]{2,1,0:T(8,128)(2,1)S(1)} %get-tuple-element.24.own_ref), channel_id=1, source_target_pairs={{0,2},{1,3},{2,0},{3,1},{4,6},{5,7},{6,4},{7,5},{8,10},{9,11},{10,... | collective-permute-start | bytes 393224 | tf_op jit(solution)/shard_map/ppermute | solution.py:404
  20.9 3.9 %collective-permute-done.3.second_ref = bf16[1,8,16,512]{3,2,1,0:T(8,128)(2,1)S(1)} collective-permute-done((bf16[1,8,16,512]{3,2,1,0:T(8,128)(2,1)S(1)}, bf16[1,8,16,512]{3,2,1,0:T(8,128)(2,1)S(1)}, u32[]{:S(2)}, u32[]{:S(2)}) %collective-permute-start.3) | collective-permute-done | bytes 131104 | tf_op jit(solution)/shard_map/ppermute | solution.py:488
  24.8 0.0 collective-permute-done.2.received_ref
  24.8 0.0 all-to-all-done
  24.8 0.7 add_flow.1._
  25.5 9.8 %forward.1 = (bf16[256,1024]{1,0:T(8,128)(2,1)}, bf16[256,1024]{1,0:T(8,128)(2,1)}, bf16[256,1024]{1,0:T(8,128)(2,1)}, bf16[256,1024]{1,0:T(8,128)(2,1)}, bf16[2...) custom-call(bf16[256,1024]{1,0:T(8,128)(2,1)S(1)} %bitcast.19, ...), custom_call_target="tpu_custom_call" | custom-call | flops 3221225472 | bytes 13631488 | tf_op jit(solution)/shard_map/forward/pallas_call | solution.py:226
  35.3 4.8 %all-to-all-start.3 = ((bf16[8,256,128]{2,1,0:T(8,128)(2,1)}), bf16[8,256,128]{2,1,0:T(8,128)(2,1)S(1)}, u32[]{:S(2)}, u32[]{:S(2)}) async-start(bf16[8,256,128]{2,1,0:T(8,128)(2,1)} %get-tuple-element.36), calls=%async_computation.3 | async-start | bytes 1048576 | tf_op jit(solution)/shard_map/all_to_all | solution.py:400
  40.2 2.9 %collective-permute-start.7 = (bf16[2,8,16,512]{3,2,1,0:T(8,128)(2,1)S(1)}, bf16[2,8,16,512]{3,2,1,0:T(8,128)(2,1)S(1)}, u32[]{:S(2)}, u32[]{:S(2)}) collective-permute-start(bf16[2,8,16,512]{3,2,1,0:T(8,128)(2,1)S(1)} %join.2.__.first_ref), channel_id=1, source_target_pairs={{0,16},{4,20},{8,24},{12,28},{16,0},{20,4},{24,8},{28,12},{1,17},{... | collective-permute-start | bytes 786440 | tf_op jit(solution)/shard_map/ppermute | solution.py:488
  43.1 18.7 %all-to-all-done.3 = bf16[8,256,128]{2,1,0:T(8,128)(2,1)S(1)} async-done(((bf16[8,256,128]{2,1,0:T(8,128)(2,1)}), bf16[8,256,128]{2,1,0:T(8,128)(2,1)S(1)}, u32[]{:S(2)}, u32[]{:S(2)}) %all-to-all-start.3) | async-done | bytes 524320 | tf_op jit(solution)/shard_map/all_to_all | solution.py:400
  61.8 3.4 %all-to-all-start.1 = ((bf16[8,32,512]{2,1,0:T(8,128)(2,1)}), bf16[8,32,512]{2,1,0:T(8,128)(2,1)S(1)}, u32[]{:S(2)}, u32[]{:S(2)}) async-start(bf16[8,32,512]{2,1,0:T(8,128)(2,1)} %add_flow.1._), calls=%async_computation.1 | async-start | bytes 524288 | tf_op jit(solution)/shard_map/all_to_all | solution.py:400
  65.2 0.5 collective-permute-done.7.second_ref
  65.7 1.5 %collective-permute-start.8 = (bf16[4,8,16,512]{3,2,1,0:T(8,128)(2,1)S(1)}, bf16[4,8,16,512]{3,2,1,0:T(8,128)(2,1)S(1)}, u32[]{:S(2)}, u32[]{:S(2)}) collective-permute-start(bf16[4,8,16,512]{3,2,1,0:T(8,128)(2,1)S(1)} %join.3.rest_1_.first_ref), channel_id=1, source_target_pairs={{0,4},{4,0},{8,12},{12,8},{16,20},{20,16},{24,28},{28,24},{1,5},{5... | collective-permute-start | bytes 1572872 | tf_op jit(solution)/shard_map/ppermute | solution.py:488
  67.2 0.0 collective-permute-start.4
  67.2 1.3 %constant_dynamic-slice_fusion = (bf16[8,8,16,128]{3,2,1,0:T(8,128)(2,1)S(1)}, bf16[8,8,16,128]{3,2,1,0:T(8,128)(2,1)S(1)}) fusion(bf16[8,8,32,128]{3,2,1,0:T(8,128)(2,1)} %bitcast.35, u32[]{:T(128)S(6)} %convert_element_type.10, u32[]{:T(128)S(6)} %convert_element_type.9), kind=kLoop, calls=%fused_computation.1 | loop fusion | bytes 1048584 | tf_op jit(solution)/shard_map/dynamic_slice | solution.py:396
  68.5 1.6 %collective-permute-start.9 = (bf16[1024,128]{1,0:T(8,128)(2,1)S(1)}, bf16[1024,128]{1,0:T(8,128)(2,1)S(1)}, u32[]{:S(2)}, u32[]{:S(2)}) collective-permute-start(bf16[1024,128]{1,0:T(8,128)(2,1)S(1)} %bitcast.38), channel_id=1, source_target_pairs={{0,2},{1,3},{2,0},{3,1},{4,6},{5,7},{6,4},{7,5},{8,10},{9,11},{10,... | collective-permute-start | bytes 786440 | tf_op jit(solution)/shard_map/ppermute | solution.py:404
  70.1 3.3 %all-to-all-done.1 = bf16[8,32,512]{2,1,0:T(8,128)(2,1)S(1)} async-done(((bf16[8,32,512]{2,1,0:T(8,128)(2,1)}), bf16[8,32,512]{2,1,0:T(8,128)(2,1)S(1)}, u32[]{:S(2)}, u32[]{:S(2)}) %all-to-all-start.1) | async-done | bytes 262176 | tf_op jit(solution)/shard_map/all_to_all | solution.py:400
  73.5 0.0 collective-permute-start.6
  73.5 0.0 collective-permute-done.4.received_ref
  73.5 0.1 add.8.rest_0_.own_ref
  73.5 1.6 %collective-permute-start.5 = (bf16[256,512]{1,0:T(8,128)(2,1)S(1)}, bf16[256,512]{1,0:T(8,128)(2,1)S(1)}, u32[]{:S(2)}, u32[]{:S(2)}) collective-permute-start(bf16[256,512]{1,0:T(8,128)(2,1)S(1)} %add.8.rest_0_.own_ref), channel_id=1, source_target_pairs={{0,2},{1,3},{2,0},{3,1},{4,6},{5,7},{6,4},{7,5},{8,10},{9,11},{10,... | collective-permute-start | bytes 786440 | tf_op jit(solution)/shard_map/ppermute | solution.py:404
  75.1 5.7 %collective-permute-done.8.second_ref = bf16[4,8,16,512]{3,2,1,0:T(8,128)(2,1)S(1)} collective-permute-done((bf16[4,8,16,512]{3,2,1,0:T(8,128)(2,1)S(1)}, bf16[4,8,16,512]{3,2,1,0:T(8,128)(2,1)S(1)}, u32[]{:S(2)}, u32[]{:S(2)}) %collective-permute-start.8) | collective-permute-done | bytes 524320 | tf_op jit(solution)/shard_map/ppermute | solution.py:488
  80.8 0.0 collective-permute-done.9._.refs_1_
  80.8 0.1 arrange.1
  80.9 0.1 collective-permute-start.10
  81.0 0.0 collective-permute-done.6.other_ref
  81.0 11.3 %backward.1.back_ref = bf16[256,1024]{1,0:T(8,128)(2,1)S(1)} custom-call(bf16[256,1024]{1,0:T(8,128)(2,1)S(1)} %bitcast.20, bf16[256,512]{1,0:T(8,128)(2,1)S(1)} %bitcast.31, bf16[256,512]{1,0:T(8,128)(2,1)S(1)} %collective-permute-done.6.other_ref, bf16[1024,1024]{1,0:T(8,128)(2,1)} %bitcast.34, bf16[1024,3072]{1,0:T(8,128)(2,1)} %wv_ref.3, ...), custom_call_target="tpu_custom_call" | custom-call | flops 4294967296 | bytes 13631488 | tf_op jit(solution)/shard_map/backward/pallas_call | solution.py:338
  92.3 0.0 collective-permute-done.5.received_ref
  92.3 1.0 add_mixed.1
  93.3 4.0 %all-to-all-start.2 = ((bf16[8,32,1536]{2,1,0:T(8,128)(2,1)}), bf16[8,32,1536]{2,1,0:T(8,128)(2,1)S(1)}, u32[]{:S(2)}, u32[]{:S(2)}) async-start(bf16[8,32,1536]{2,1,0:T(8,128)(2,1)} %bitcast.6), calls=%async_computation.2 | async-start | bytes 1572864 | tf_op jit(solution)/shard_map/all_to_all | solution.py:400
  97.3 2.0 %mix_gradient.1 = (f32[128,1024]{1,0:T(8,128)S(1)}, bf16[128,1024]{1,0:T(8,128)(2,1)S(1)}) custom-call(bf16[1024,512]{1,0:T(8,128)(2,1)S(1)} %bitcast.22, bf16[1024,512]{1,0:T(8,128)(2,1)} %collective-permute-done.10.other_flow_ref, bf16[1024,128]{1,0:T(8,128)(2,1)S(1)} %bitcast.32, bf16[1024,128]{1,0:T(8,128)(2,1)S(1)} %collective-permute-done.9._.refs_1_), custom_call_target="tpu_custom_call" | custom-call | flops 536870912 | bytes 2621440 | tf_op jit(solution)/shard_map/mix_gradient/pallas_call | solution.py:381
  99.3 0.0 copy-start
  99.3 1.6 %collective-permute-start.11 = (bf16[128,1024]{1,0:T(8,128)(2,1)S(1)}, bf16[128,1024]{1,0:T(8,128)(2,1)S(1)}, u32[]{:S(2)}, u32[]{:S(2)}) collective-permute-start(bf16[128,1024]{1,0:T(8,128)(2,1)S(1)} %get-tuple-element.38), channel_id=1, source_target_pairs={{0,2},{1,3},{2,0},{3,1},{4,6},{5,7},{6,4},{7,5},{8,10},{9,11},{10,... | collective-permute-start | bytes 786440 | tf_op jit(solution)/shard_map/ppermute | solution.py:404
  100.9 6.9 %collective-permute-done.11 = bf16[128,1024]{1,0:T(8,128)(2,1)S(1)} collective-permute-done((bf16[128,1024]{1,0:T(8,128)(2,1)S(1)}, bf16[128,1024]{1,0:T(8,128)(2,1)S(1)}, u32[]{:S(2)}, u32[]{:S(2)}) %collective-permute-start.11) | collective-permute-done | bytes 262176 | tf_op jit(solution)/shard_map/ppermute | solution.py:404
  107.8 0.1 convert_add_fusion._
  107.9 0.0 copy-start.2
  107.9 10.3 %all-to-all-done.2.in_ref.back_ref = bf16[8,32,1536]{2,1,0:T(8,128)(2,1)S(1)} async-done(((bf16[8,32,1536]{2,1,0:T(8,128)(2,1)}), bf16[8,32,1536]{2,1,0:T(8,128)(2,1)S(1)}, u32[]{:S(2)}, u32[]{:S(2)}) %all-to-all-start.2) | async-done | bytes 786464 | tf_op jit(solution)/shard_map/all_to_all | solution.py:400
  118.1 0.1 collective-permute-start.12
  118.2 0.9 make_gradient.1
  119.1 0.6 collective-permute-done.12.other_ref
  119.7 1.0 make_output.1
  (15 shorter events, 0.1 us)
Async XLA Ops:
  2.7 22.9 %copy-start.4 = (s32[2,16]{1,0:T(2,128)S(1)}, s32[2,16]{1,0:T(2,128)}, u32[]{:S(2)}) copy-start(s32[2,16]{1,0:T(2,128)} %mask_ref.1) | copy-start | bytes 388
  2.7 22.1 %all-to-all-start = ((bf16[8,32,1024]{2,1,0:T(8,128)(2,1)}), bf16[8,32,1024]{2,1,0:T(8,128)(2,1)S(1)}, u32[]{:S(2)}, u32[]{:S(2)}) async-start(bf16[8,32,1024]{2,1,0:T(8,128)(2,1)} %get-tuple-element.21), calls=%async_computation | async-start | bytes 1048576 | tf_op jit(solution)/shard_map/all_to_all | solution.py:400
  10.1 1.5 %collective-permute-start = (bf16[8,32,512]{2,1,0:T(8,128)(2,1)S(1)}, bf16[8,32,512]{2,1,0:T(8,128)(2,1)S(1)}, u32[]{:S(2)}, u32[]{:S(2)}) collective-permute-start(bf16[8,32,512]{2,1,0:T(8,128)(2,1)S(1)} %get-tuple-element.23), channel_id=1, source_target_pairs={{0,1},{1,0},{2,3},{3,2},{4,5},{5,4},{6,7},{7,6},{8,9},{9,8},{10,11... | collective-permute-start | bytes 786440 | tf_op jit(solution)/shard_map/ppermute | solution.py:404
  11.7 5.6 %collective-permute-start.1 = (bf16[8,16,512]{2,1,0:T(8,128)(2,1)S(1)}, bf16[8,16,512]{2,1,0:T(8,128)(2,1)S(1)}, u32[]{:S(2)}, u32[]{:S(2)}) collective-permute-start(bf16[8,16,512]{2,1,0:T(8,128)(2,1)S(1)} %get-tuple-element.25.second_ref), channel_id=1, source_target_pairs={{0,2},{1,3},{2,0},{3,1},{4,6},{5,7},{6,4},{7,5},{8,10},{9,11},{10,... | collective-permute-start | bytes 393224 | tf_op jit(solution)/shard_map/ppermute | solution.py:404
  17.3 7.5 %collective-permute-start.3 = (bf16[1,8,16,512]{3,2,1,0:T(8,128)(2,1)S(1)}, bf16[1,8,16,512]{3,2,1,0:T(8,128)(2,1)S(1)}, u32[]{:S(2)}, u32[]{:S(2)}) collective-permute-start(bf16[1,8,16,512]{3,2,1,0:T(8,128)(2,1)S(1)} %bitcast.28), channel_id=1, source_target_pairs={{0,8},{4,12},{8,0},{12,4},{16,24},{20,28},{24,16},{28,20},{1,9},{5... | collective-permute-start | bytes 393224 | tf_op jit(solution)/shard_map/ppermute | solution.py:488
  19.4 5.4 %collective-permute-start.2 = (bf16[8,16,512]{2,1,0:T(8,128)(2,1)S(1)}, bf16[8,16,512]{2,1,0:T(8,128)(2,1)S(1)}, u32[]{:S(2)}, u32[]{:S(2)}) collective-permute-start(bf16[8,16,512]{2,1,0:T(8,128)(2,1)S(1)} %get-tuple-element.24.own_ref), channel_id=1, source_target_pairs={{0,2},{1,3},{2,0},{3,1},{4,6},{5,7},{6,4},{7,5},{8,10},{9,11},{10,... | collective-permute-start | bytes 393224 | tf_op jit(solution)/shard_map/ppermute | solution.py:404
  35.3 26.5 %all-to-all-start.3 = ((bf16[8,256,128]{2,1,0:T(8,128)(2,1)}), bf16[8,256,128]{2,1,0:T(8,128)(2,1)S(1)}, u32[]{:S(2)}, u32[]{:S(2)}) async-start(bf16[8,256,128]{2,1,0:T(8,128)(2,1)} %get-tuple-element.36), calls=%async_computation.3 | async-start | bytes 1048576 | tf_op jit(solution)/shard_map/all_to_all | solution.py:400
  40.2 25.5 %collective-permute-start.7 = (bf16[2,8,16,512]{3,2,1,0:T(8,128)(2,1)S(1)}, bf16[2,8,16,512]{3,2,1,0:T(8,128)(2,1)S(1)}, u32[]{:S(2)}, u32[]{:S(2)}) collective-permute-start(bf16[2,8,16,512]{3,2,1,0:T(8,128)(2,1)S(1)} %join.2.__.first_ref), channel_id=1, source_target_pairs={{0,16},{4,20},{8,24},{12,28},{16,0},{20,4},{24,8},{28,12},{1,17},{... | collective-permute-start | bytes 786440 | tf_op jit(solution)/shard_map/ppermute | solution.py:488
  61.8 5.5 %copy-start.5 = (bf16[8,256,128]{2,1,0:T(8,128)(2,1)}, bf16[8,256,128]{2,1,0:T(8,128)(2,1)S(1)}, u32[]{:S(2)}) copy-start(bf16[8,256,128]{2,1,0:T(8,128)(2,1)S(1)} %all-to-all-done.3) | copy-start | bytes 1572868
  61.8 11.7 %all-to-all-start.1 = ((bf16[8,32,512]{2,1,0:T(8,128)(2,1)}), bf16[8,32,512]{2,1,0:T(8,128)(2,1)S(1)}, u32[]{:S(2)}, u32[]{:S(2)}) async-start(bf16[8,32,512]{2,1,0:T(8,128)(2,1)} %add_flow.1._), calls=%async_computation.1 | async-start | bytes 524288 | tf_op jit(solution)/shard_map/all_to_all | solution.py:400
  65.7 15.1 %collective-permute-start.8 = (bf16[4,8,16,512]{3,2,1,0:T(8,128)(2,1)S(1)}, bf16[4,8,16,512]{3,2,1,0:T(8,128)(2,1)S(1)}, u32[]{:S(2)}, u32[]{:S(2)}) collective-permute-start(bf16[4,8,16,512]{3,2,1,0:T(8,128)(2,1)S(1)} %join.3.rest_1_.first_ref), channel_id=1, source_target_pairs={{0,4},{4,0},{8,12},{12,8},{16,20},{20,16},{24,28},{28,24},{1,5},{5... | collective-permute-start | bytes 1572872 | tf_op jit(solution)/shard_map/ppermute | solution.py:488
  67.2 6.2 %collective-permute-start.4 = (bf16[256,512]{1,0:T(8,128)(2,1)S(1)}, bf16[256,512]{1,0:T(8,128)(2,1)S(1)}, u32[]{:S(2)}, u32[]{:S(2)}) collective-permute-start(bf16[256,512]{1,0:T(8,128)(2,1)S(1)} %get-tuple-element.27), channel_id=1, source_target_pairs={{0,1},{1,0},{2,3},{3,2},{4,5},{5,4},{6,7},{7,6},{8,9},{9,8},{10,11... | collective-permute-start | bytes 786440 | tf_op jit(solution)/shard_map/ppermute | solution.py:404
  68.5 12.3 %collective-permute-start.9 = (bf16[1024,128]{1,0:T(8,128)(2,1)S(1)}, bf16[1024,128]{1,0:T(8,128)(2,1)S(1)}, u32[]{:S(2)}, u32[]{:S(2)}) collective-permute-start(bf16[1024,128]{1,0:T(8,128)(2,1)S(1)} %bitcast.38), channel_id=1, source_target_pairs={{0,2},{1,3},{2,0},{3,1},{4,6},{5,7},{6,4},{7,5},{8,10},{9,11},{10,... | collective-permute-start | bytes 786440 | tf_op jit(solution)/shard_map/ppermute | solution.py:404
  73.5 7.5 %collective-permute-start.6 = (bf16[256,512]{1,0:T(8,128)(2,1)S(1)}, bf16[256,512]{1,0:T(8,128)(2,1)S(1)}, u32[]{:S(2)}, u32[]{:S(2)}) collective-permute-start(bf16[256,512]{1,0:T(8,128)(2,1)S(1)} %bitcast.30), channel_id=1, source_target_pairs={{0,1},{1,0},{2,3},{3,2},{4,5},{5,4},{6,7},{7,6},{8,9},{9,8},{10,11... | collective-permute-start | bytes 786440 | tf_op jit(solution)/shard_map/ppermute | solution.py:404
  73.5 18.8 %collective-permute-start.5 = (bf16[256,512]{1,0:T(8,128)(2,1)S(1)}, bf16[256,512]{1,0:T(8,128)(2,1)S(1)}, u32[]{:S(2)}, u32[]{:S(2)}) collective-permute-start(bf16[256,512]{1,0:T(8,128)(2,1)S(1)} %add.8.rest_0_.own_ref), channel_id=1, source_target_pairs={{0,2},{1,3},{2,0},{3,1},{4,6},{5,7},{6,4},{7,5},{8,10},{9,11},{10,... | collective-permute-start | bytes 786440 | tf_op jit(solution)/shard_map/ppermute | solution.py:404
  80.9 16.4 %collective-permute-start.10 = (bf16[1024,512]{1,0:T(8,128)(2,1)S(1)}, bf16[1024,512]{1,0:T(8,128)(2,1)}, u32[]{:S(2)}, u32[]{:S(2)}) collective-permute-start(bf16[1024,512]{1,0:T(8,128)(2,1)S(1)} %bitcast.21), channel_id=1, source_target_pairs={{0,1},{1,0},{2,3},{3,2},{4,5},{5,4},{6,7},{7,6},{8,9},{9,8},{10,11... | collective-permute-start | bytes 3145736 | tf_op jit(solution)/shard_map/ppermute | solution.py:404
  93.3 24.8 %all-to-all-start.2 = ((bf16[8,32,1536]{2,1,0:T(8,128)(2,1)}), bf16[8,32,1536]{2,1,0:T(8,128)(2,1)S(1)}, u32[]{:S(2)}, u32[]{:S(2)}) async-start(bf16[8,32,1536]{2,1,0:T(8,128)(2,1)} %bitcast.6), calls=%async_computation.2 | async-start | bytes 1572864 | tf_op jit(solution)/shard_map/all_to_all | solution.py:400
  99.3 18.9 %copy-start = (bf16[2,1,2,64,1024]{4,3,2,1,0:T(8,128)(2,1)S(1)}, bf16[2,1,2,64,1024]{4,3,2,1,0:T(8,128)(2,1)}, u32[]{:S(2)}) copy-start(bf16[2,1,2,64,1024]{4,3,2,1,0:T(8,128)(2,1)} %param.11) | copy-start | bytes 1572868
  99.3 8.5 %collective-permute-start.11 = (bf16[128,1024]{1,0:T(8,128)(2,1)S(1)}, bf16[128,1024]{1,0:T(8,128)(2,1)S(1)}, u32[]{:S(2)}, u32[]{:S(2)}) collective-permute-start(bf16[128,1024]{1,0:T(8,128)(2,1)S(1)} %get-tuple-element.38), channel_id=1, source_target_pairs={{0,2},{1,3},{2,0},{3,1},{4,6},{5,7},{6,4},{7,5},{8,10},{9,11},{10,... | collective-permute-start | bytes 786440 | tf_op jit(solution)/shard_map/ppermute | solution.py:404
  107.8 12.0 %copy-start.1 = (bf16[2,1,2,64,1024]{4,3,2,1,0:T(8,128)(2,1)S(1)}, bf16[2,1,2,64,1024]{4,3,2,1,0:T(8,128)(2,1)}, u32[]{:S(2)}) copy-start(bf16[2,1,2,64,1024]{4,3,2,1,0:T(8,128)(2,1)} %param.6) | copy-start | bytes 1572868
  107.8 12.0 %copy-start.3 = (f32[1,1024]{1,0:T(1,128)S(1)}, f32[1,1024]{1,0:T(1,128)}, u32[]{:S(2)}) copy-start(f32[1,1024]{1,0:T(1,128)} %gain_ref.3) | copy-start | bytes 12292
  107.9 12.9 %copy-start.2 = (f32[128,1024]{1,0:T(8,128)}, f32[128,1024]{1,0:T(8,128)S(1)}, u32[]{:S(2)}) copy-start(f32[128,1024]{1,0:T(8,128)S(1)} %convert_add_fusion._) | copy-start | bytes 1572868
  118.1 1.6 %collective-permute-start.12 = (bf16[8,32,512]{2,1,0:T(8,128)(2,1)S(1)}, bf16[8,32,512]{2,1,0:T(8,128)(2,1)S(1)}, u32[]{:S(2)}, u32[]{:S(2)}) collective-permute-start(bf16[8,32,512]{2,1,0:T(8,128)(2,1)S(1)} %cut_mixed.1.own_ref), channel_id=1, source_target_pairs={{0,1},{1,0},{2,3},{3,2},{4,5},{5,4},{6,7},{7,6},{8,9},{9,8},{10,11... | collective-permute-start | bytes 786440 | tf_op jit(solution)/shard_map/ppermute | solution.py:404
